TPU v7x, 32 devices: a whole 2x2x4 slice. The times are simulated.
32 devices in a mesh: groups: 2 (over y), rows: 4 (over z), heads: 4 (over x, core).
Axes of the slice: x: 2, y: 2, z: 4, core: 2. Of those that a mesh axis runs over, the one named last changes fastest.
Arguments:
- resid: bfloat16 [256, 5120], P(('groups', 'heads'), 'rows'), parts along dimension 0, may hold values from -6 to 6
- queries: bfloat16 [256, 8192], P(('groups', 'rows'), 'heads'), parts along dimension 0, may hold values from -600 to 600
- kv_codes: bfloat16 [512, 2, 8, 128, 128], P(('groups', 'rows'), None, 'heads'), parts along dimension 0, may hold values from -127 to 127, as said below
- kv_scale: float32 [4, 8], P('groups', 'heads'), parts along dimension 0, may hold values from 0.004 to 0.016
- row_blocks: int32 [256, 32], P(('groups', 'rows')), parts along dimension 0, may hold values from 0 to 255, as said below
- row_len: int32 [256], P(('groups', 'rows')), parts along dimension 0, may hold values from 1 to 4096, as said below
- w_out: bfloat16 [8192, 5120], P('heads', 'rows'), may hold values from -0.0625 to 0.0625
- norm_gain: float32 [5120], replicated, may hold values from 0.1 to 1.9
- w_gate: bfloat16 [5120, 16384], P(None, ('rows', 'heads')), may hold values from -0.078125 to 0.078125
- w_up: bfloat16 [5120, 16384], P(None, ('rows', 'heads')), may hold values from -0.078125 to 0.078125
- w_down: bfloat16 [16384, 5120], P(('rows', 'heads')), may hold values from -0.0625 to 0.0625
Outputs:
- layer_out: bfloat16 [256, 5120], P(('groups', 'heads'), 'rows'), parts along dimension 0
There are 2 independent parts, one for each index of `groups`. A program takes and returns all parts, laid end to end along the dimension named above; an argument that names none is the same for every part. Nothing has to cross between parts.
Inputs may be any that keep to these rules, and one draw needn't show every extreme that they name: `row_blocks`: each row's list holds the 32 distinct block ids of one document in the document's order; all blocks of a document lie in one range from o * 64 to (o + 1) * 64 - 1 for some index o of rows, and every such range holds 2 documents. Among the rows of one index of rows (aligned blocks of 32 rows) at most 16 have lists in the same range, and exactly 16 do for some range. `row_len`: the largest value, 4096, is reached. `kv_codes`: every code is a whole number, so the codes fit int8.
All inputs are finite; a program needn't handle non-finite values.
Results may differ from a plain program's by a relative error of at most 0.015.
Values may be sent and summed in bfloat16 or wider, within the bound.
No kernel may reach another device: no remote copies, remote signals or barrier semaphores. Data moves between devices by JAX's collectives and lax.ppermute only.
A program may use at most 128 MiB of HBM per device.

v0:
```python
import math

import jax
import jax.numpy as jnp
from jax import lax
from jax.sharding import PartitionSpec as P

norm_eps = 1e-06


def shards(
    resid, queries, kv_codes, kv_scale, row_blocks, row_len, w_out, norm_gain, w_gate, w_up, w_down
):
    row_devs = lax.axis_size("rows")
    rows_dev = queries.shape[0]
    capacity = max(2, 2 * rows_dev // row_devs)
    slot_count = row_devs * capacity
    blocks_dev = kv_codes.shape[0]
    block_tok = kv_codes.shape[3]
    head_dim = kv_codes.shape[4]
    heads_dev = kv_scale.shape[1]
    width_q = queries.shape[1]
    group_size = width_q // (heads_dev * head_dim)
    owner_dev = row_blocks[:, 0] // blocks_dev
    same_owner = owner_dev[:, None] == owner_dev[None, :]
    earlier = lax.broadcasted_iota(jnp.int32, (rows_dev, rows_dev), 1) < lax.broadcasted_iota(
        jnp.int32, (rows_dev, rows_dev), 0
    )
    slot_rank = jnp.sum((same_owner & earlier).astype(jnp.int32), axis=1)
    target = owner_dev * capacity + slot_rank
    placing = jnp.arange(slot_count, dtype=jnp.int32)[:, None] == target[None, :]
    place_bf = placing.astype(jnp.bfloat16)
    place_fl = placing.astype(jnp.float32)
    send_queries = jnp.dot(place_bf, queries, preferred_element_type=jnp.float32).astype(
        jnp.bfloat16
    )
    send_queries = send_queries.reshape(row_devs, capacity, width_q)
    send_lists = jnp.dot(
        place_fl, row_blocks.astype(jnp.float32), precision=lax.Precision.HIGHEST
    ).astype(jnp.int32)
    send_lists = send_lists.reshape(row_devs, capacity, -1)
    send_lens = jnp.dot(
        place_fl, row_len.astype(jnp.float32), precision=lax.Precision.HIGHEST
    ).astype(jnp.int32)
    send_lens = send_lens.reshape(row_devs, capacity)
    got_queries = lax.all_to_all(send_queries, "rows", split_axis=0, concat_axis=0, tiled=True)
    got_lists, got_lens = (
        lax.all_to_all(send_lists, "rows", split_axis=0, concat_axis=0, tiled=True),
        lax.all_to_all(send_lens, "rows", split_axis=0, concat_axis=0, tiled=True),
    )
    my_index = lax.axis_index("rows")
    local_ids = got_lists.reshape(slot_count, -1) - my_index * blocks_dev
    list_len = local_ids.shape[1]
    matches = local_ids[:, :, None] == jnp.arange(blocks_dev, dtype=jnp.int32)[None, None, :]
    list_place = jnp.sum(
        jnp.where(matches, jnp.arange(list_len, dtype=jnp.int32)[None, :, None], 0), axis=1
    )
    present = jnp.any(matches, axis=1)
    position = (
        list_place[:, :, None] * block_tok + jnp.arange(block_tok, dtype=jnp.int32)[None, None, :]
    )
    is_valid = present[:, :, None] & (position < got_lens.reshape(slot_count)[:, None, None])
    queries_in = got_queries.reshape(slot_count, heads_dev, group_size, head_dim)
    key_codes = kv_codes[:, 0]
    value_codes = kv_codes[:, 1]
    scores = jnp.einsum(
        "skgd,bktd->skgbt", queries_in, key_codes, preferred_element_type=jnp.float32
    )
    scores = scores * (kv_scale[0] / math.sqrt(head_dim))[None, :, None, None, None]
    scores = jnp.where(is_valid[:, None, None], scores, -1e30)
    peak_score = jnp.max(scores, axis=(3, 4), keepdims=True)
    weights = jnp.exp(scores - peak_score)
    denom_sum = jnp.sum(weights, axis=(3, 4))
    mixture = jnp.einsum(
        "skgbt,bktd->skgd",
        weights.astype(jnp.bfloat16),
        value_codes,
        preferred_element_type=jnp.float32,
    )
    mixture = mixture * kv_scale[1][None, :, None, None] / denom_sum[..., None]
    slot_out = mixture.astype(jnp.bfloat16).reshape(row_devs, capacity, width_q)
    returned = lax.all_to_all(slot_out, "rows", split_axis=0, concat_axis=0, tiled=True)
    attended = jnp.einsum(
        "sr,sq->rq",
        place_bf,
        returned.reshape(slot_count, width_q),
        preferred_element_type=jnp.float32,
    ).astype(jnp.bfloat16)
    head_terms = jnp.dot(
        lax.all_gather(attended, "rows", axis=0, tiled=True),
        w_out,
        preferred_element_type=jnp.float32,
    )
    attn_out = lax.psum_scatter(
        head_terms.astype(jnp.bfloat16), "heads", scatter_dimension=0, tiled=True
    ).astype(jnp.float32)
    hidden_state = (resid.astype(jnp.float32) + attn_out).astype(jnp.bfloat16)
    as_float = hidden_state.astype(jnp.float32)
    cols_dev = hidden_state.shape[1]
    model_width = cols_dev * row_devs
    squares = jnp.sum(as_float * as_float, axis=1)
    totals = lax.psum(squares, "rows")
    gain_slice = lax.dynamic_slice_in_dim(norm_gain, my_index * cols_dev, cols_dev)
    normed = (as_float * lax.rsqrt(totals / model_width + norm_eps)[:, None] * gain_slice).astype(
        jnp.bfloat16
    )
    full_rows = lax.all_gather(normed, "rows", axis=1, tiled=True)
    piece_rows = lax.all_gather(full_rows, "heads", axis=0, tiled=True)
    gate_proj = jnp.dot(piece_rows, w_gate, preferred_element_type=jnp.float32)
    up_proj = jnp.dot(piece_rows, w_up, preferred_element_type=jnp.float32)
    inner_act = (jax.nn.silu(gate_proj) * up_proj).astype(jnp.bfloat16)
    partial_sum = jnp.dot(inner_act, w_down, preferred_element_type=jnp.float32)
    section_sum = lax.psum_scatter(
        partial_sum.astype(jnp.bfloat16), "heads", scatter_dimension=0, tiled=True
    )
    ffn_out = lax.psum_scatter(section_sum, "rows", scatter_dimension=1, tiled=True).astype(
        jnp.float32
    )
    return (as_float + ffn_out).astype(jnp.bfloat16)


def solution(mesh):
    placed = (
        P(("groups", "heads"), "rows"),
        P(("groups", "rows"), "heads"),
        P(("groups", "rows"), None, "heads", None, None),
        P("groups", "heads"),
        P(("groups", "rows"), None),
        P(("groups", "rows")),
        P("heads", "rows"),
        P(),
        P(None, ("rows", "heads")),
        P(None, ("rows", "heads")),
        P(("rows", "heads"), None),
    )
    return jax.shard_map(
        shards,
        mesh=mesh,
        in_specs=placed,
        out_specs=P(("groups", "heads"), "rows"),
        check_vma=False,
    )
```

profile of v0, /device:TPU:0, one launch (start us, length us, event | category | flops | bytes accessed | tf_op | source)
XLA Modules:
  0.0 261.5 jit_solution(14837088297054705216)
XLA Ops:
  9.1 6.3 %all-to-all-start.1 = ((s32[4,1,16]{2,1,0:T(1,128)}), s32[4,1,16]{2,1,0:T(1,128)S(1)}, u32[]{:S(2)}, u32[]{:S(2)}) async-start(s32[4,1,16]{2,1,0:T(1,128)} %bitcast.4), calls=%async_computation.1 | async-start | bytes 4096 | tf_op jit(solution)/shard_map/all_to_all | solution.py:49
  16.4 6.0 %fusion.48 = (bf16[64,1,2,128,128]{4,3,2,1,0:T(8,128)(2,1)}, bf16[64,1,2,128,128]{4,3,2,1,0:T(8,128)(2,1)}) fusion(bf16[64,2,2,128,128]{4,3,2,1,0:T(8,128)(2,1)} %param.13), kind=kLoop, calls=%fused_computation.76 | loop fusion | bytes 16777216 | tf_op jit(solution)/shard_map/slice | solution.py:64
  23.4 5.1 %all-to-all-start = ((s32[4,1,512]{2,1,0:T(1,128)}), s32[4,1,512]{2,1,0:T(1,128)S(1)}, u32[]{:S(2)}, u32[]{:S(2)}) async-start(s32[4,1,512]{2,1,0:T(1,128)} %reshape.114), calls=%async_computation | async-start | bytes 16384 | tf_op jit(solution)/shard_map/all_to_all | solution.py:48
  29.8 4.3 %all-to-all-done = s32[4,1,512]{2,1,0:T(1,128)S(1)} async-done(((s32[4,1,512]{2,1,0:T(1,128)}), s32[4,1,512]{2,1,0:T(1,128)S(1)}, u32[]{:S(2)}, u32[]{:S(2)}) %all-to-all-start) | async-done | bytes 8224 | tf_op jit(solution)/shard_map/all_to_all | solution.py:48
  34.0 3.4 %all-to-all-start.2 = ((bf16[4,16,2048]{2,1,0:T(8,128)(2,1)}), bf16[4,16,2048]{2,1,0:T(8,128)(2,1)S(1)}, u32[]{:S(2)}, u32[]{:S(2)}) async-start(bf16[4,16,2048]{2,1,0:T(8,128)(2,1)} %bitcast.5), calls=%async_computation.2 | async-start | bytes 524288 | tf_op jit(solution)/shard_map/all_to_all | solution.py:46
  39.6 1.5 fusion.7
  41.1 3.1 %all-to-all-done.2 = bf16[4,16,2048]{2,1,0:T(8,128)(2,1)S(1)} async-done(((bf16[4,16,2048]{2,1,0:T(8,128)(2,1)}), bf16[4,16,2048]{2,1,0:T(8,128)(2,1)S(1)}, u32[]{:S(2)}, u32[]{:S(2)}) %all-to-all-start.2) | async-done | bytes 262176 | tf_op jit(solution)/shard_map/all_to_all | solution.py:46
  44.2 16.3 %bitcast_reduce_fusion = (f32[64,2,8]{2,0,1:T(8,128)S(1)}, f32[2,64,8,64,128]{4,2,3,1,0:T(8,128)}) fusion(f32[2]{0:T(128)S(1)} %get-tuple-element.10, pred[64,64,128]{2,1,0:T(8,128)(4,1)S(1)} %fusion.7, bf16[64,1,2,128,128]{4,3,2,1,0:T(8,128)(2,1)} %get-tuple-element.7, bf16[64,2,8,128,1]{3,2,1,0,4:T(8,128)(2,1)S(1)} %bitcast.94), kind=kOutput, calls=%fused_computation.1 | convolution fusion | flops 2172648448 | bytes 38539272 | tf_op jit(solution)/shard_map/skgd,bktd->skgbt/dot_general | solution.py:66
  60.6 15.7 %fusion.1 = f32[64,2,8]{2,0,1:T(8,128)S(1)} fusion(f32[2,64,8,64,128]{4,2,3,1,0:T(8,128)} %get-tuple-element.12, f32[64,2,8]{2,0,1:T(8,128)S(1)} %get-tuple-element.11, f32[2]{0:T(128)S(1)} %get-tuple-element.10, pred[64,64,128]{2,1,0:T(8,128)(4,1)S(1)} %fusion.7), kind=kLoop, calls=%fused_computation.4 | loop fusion | flops 33553408 | bytes 34086920 | tf_op jit(solution)/shard_map/reduce_sum | solution.py:73
  76.3 15.4 %fusion.22 = bf16[64,2,8,128]{3,2,0,1:T(8,128)(2,1)S(1)} fusion(bf16[64,1,2,128,128]{4,3,2,1,0:T(8,128)(2,1)} %get-tuple-element.8, f32[2,64,8,64,128]{4,2,3,1,0:T(8,128)} %get-tuple-element.12, f32[64,2,8]{2,0,1:T(8,128)S(1)} %get-tuple-element.11, f32[2]{0:T(128)S(1)} %get-tuple-element.10, pred[64,64,128]{2,1,0:T(8,128)(4,1)S(1)} %fusion.7, ...), kind=kOutput, calls=%fused_computation.26 | convolution fusion | flops 2181431296 | bytes 38543376 | tf_op jit(solution)/shard_map/skgbt,bktd->skgd/dot_general | solution.py:74
  91.8 10.5 %all_to_all.24 = bf16[4,16,2048]{2,1,0:T(8,128)(2,1)S(1)} all-to-all(bf16[4,16,2048]{2,1,0:T(8,128)(2,1)S(1)} %reshape.95), channel_id=1, replica_groups=mesh['groups'=2,'rows'=4,'heads'=4] {'rows'}, dimensions={0} | all-to-all | bytes 524288 | tf_op jit(solution)/shard_map/all_to_all | solution.py:82
  102.5 16.2 %all_gather.9 = bf16[128,2048]{1,0:T(8,128)(2,1)S(1)} all-gather(bf16[32,2048]{1,0:T(8,128)(2,1)S(1)} %convolution_convert_fusion.3), channel_id=1, replica_groups=mesh['groups'=2,'rows'=4,'heads'=4] {'rows'}, dimensions={0}, use_global_device_ids=true | all-gather | bytes 655360 | tf_op jit(solution)/shard_map/all_gather | solution.py:90
  118.7 4.1 %convolution_convert_fusion.1 = bf16[128,1280]{1,0:T(8,128)(2,1)} fusion(bf16[128,2048]{1,0:T(8,128)(2,1)S(1)} %all_gather.9, bf16[2048,1280]{1,0:T(8,128)(2,1)} %param.17), kind=kOutput, calls=%fused_computation.12 | convolution fusion | flops 671252480 | bytes 6094848 | tf_op jit(solution)/shard_map/dot_general | solution.py:89
  123.6 19.6 %reduce-scatter.4.cloned.1.call-done = bf16[32,1280]{1,0:T(8,128)(2,1)} async-done(((bf16[128,1280]{1,0:T(8,128)(2,1)}), bf16[32,1280]{1,0:T(8,128)(2,1)}) %reduce-scatter.4.cloned.1.call-update) | async-done | bytes 81936 | tf_op jit(solution)/shard_map/reduce_scatter | solution.py:94
  143.2 1.0 fusion.33
  144.2 11.7 %psum.7 = f32[32]{0:T(128)S(1)} all-reduce(f32[32]{0:T(128)S(1)} %fusion.33), channel_id=1, replica_groups=mesh['groups'=2,'rows'=4,'heads'=4] {'rows'}, use_global_device_ids=true, to_apply=%region_7.8 | all-reduce | flops 32 | bytes 256 | tf_op jit(solution)/shard_map/psum | solution.py:102
  155.9 1.0 fusion.35
  156.9 14.8 %all_gather.10 = bf16[32,5120]{1,0:T(8,128)(2,1)} all-gather(bf16[32,1280]{1,0:T(8,128)(2,1)S(1)} %fusion.35), channel_id=1, replica_groups=mesh['groups'=2,'rows'=4,'heads'=4] {'rows'}, dimensions={1}, use_global_device_ids=true | all-gather | bytes 409600 | tf_op jit(solution)/shard_map/all_gather | solution.py:107
  171.8 15.6 %all-gather.2.cloned.1.call-done = bf16[128,5120]{1,0:T(8,128)(2,1)} async-done(((bf16[32,5120]{1,0:T(8,128)(2,1)}), bf16[128,5120]{1,0:T(8,128)(2,1)}) %all-gather.2.cloned.1.call-update) | async-done | bytes 1310736 | tf_op jit(solution)/shard_map/all_gather | solution.py:108
  187.4 6.0 %fusion.49 = f32[128,1024]{1,0:T(8,128)S(1)} fusion(bf16[128,5120]{1,0:T(8,128)(2,1)} %all-gather.2.cloned.1.call-done, bf16[5120,1024]{1,0:T(8,128)(2,1)} %param.19), kind=kOutput, calls=%fused_computation.77 | convolution fusion | flops 1342177280 | bytes 12320768 | tf_op jit(solution)/shard_map/dot_general | solution.py:109
  193.5 11.1 %convolution_convert_fusion = bf16[128,5120]{1,0:T(8,128)(2,1)} fusion(bf16[1024,5120]{1,0:T(8,128)(2,1)} %param.21, bf16[128,5120]{1,0:T(8,128)(2,1)S(1)} %copy-done.2, bf16[5120,1024]{1,0:T(8,128)(2,1)} %param.20, f32[128,1024]{1,0:T(8,128)S(1)} %fusion.49), kind=kOutput, calls=%fused_computation.8 | convolution fusion | flops 2685796352 | bytes 24117248 | tf_op jit(solution)/shard_map/dot_general | solution.py:112
  204.6 26.6 %reduce-scatter.6.cloned.1.call-done = bf16[32,5120]{1,0:T(8,128)(2,1)} async-done(((bf16[128,5120]{1,0:T(8,128)(2,1)}), bf16[32,5120]{1,0:T(8,128)(2,1)}) %reduce-scatter.6.cloned.1.call-update) | async-done | bytes 327696 | tf_op jit(solution)/shard_map/reduce_scatter | solution.py:113
  231.2 22.2 %reduce-scatter.8.cloned.1.call-done = bf16[32,1280]{1,0:T(8,128)(2,1)} async-done(((bf16[32,5120]{1,0:T(8,128)(2,1)}), bf16[32,1280]{1,0:T(8,128)(2,1)}) %reduce-scatter.8.cloned.1.call-update) | async-done | bytes 81936 | tf_op jit(solution)/shard_map/reduce_scatter | solution.py:116
  253.4 1.6 fusion.36
  (50 shorter events, 9.4 us)
Async XLA Ops:
  6.5 8.9 %copy-start = (bf16[32,2048]{1,0:T(8,128)(2,1)S(1)}, bf16[32,2048]{1,0:T(8,128)(2,1)}, u32[]{:S(2)}) copy-start(bf16[32,2048]{1,0:T(8,128)(2,1)} %param.12) | copy-start | bytes 393220
  6.5 15.8 %copy-start.5 = (s32[32,32]{1,0:T(8,128)S(1)}, s32[32,32]{1,0:T(8,128)}, u32[]{:S(2)}) copy-start(s32[32,32]{1,0:T(8,128)} %param.15) | copy-start | bytes 12292
  6.5 21.9 %copy-start.6 = (f32[2,2]{1,0:T(2,128)S(1)}, f32[2,2]{1,0:T(2,128)}, u32[]{:S(2)}) copy-start(f32[2,2]{1,0:T(2,128)} %param.14) | copy-start | bytes 52
  9.1 14.2 %all-to-all-start.1 = ((s32[4,1,16]{2,1,0:T(1,128)}), s32[4,1,16]{2,1,0:T(1,128)S(1)}, u32[]{:S(2)}, u32[]{:S(2)}) async-start(s32[4,1,16]{2,1,0:T(1,128)} %bitcast.4), calls=%async_computation.1 | async-start | bytes 4096 | tf_op jit(solution)/shard_map/all_to_all | solution.py:49
  23.4 10.7 %all-to-all-start = ((s32[4,1,512]{2,1,0:T(1,128)}), s32[4,1,512]{2,1,0:T(1,128)S(1)}, u32[]{:S(2)}, u32[]{:S(2)}) async-start(s32[4,1,512]{2,1,0:T(1,128)} %reshape.114), calls=%async_computation | async-start | bytes 16384 | tf_op jit(solution)/shard_map/all_to_all | solution.py:48
  34.0 10.2 %all-to-all-start.2 = ((bf16[4,16,2048]{2,1,0:T(8,128)(2,1)}), bf16[4,16,2048]{2,1,0:T(8,128)(2,1)S(1)}, u32[]{:S(2)}, u32[]{:S(2)}) async-start(bf16[4,16,2048]{2,1,0:T(8,128)(2,1)} %bitcast.5), calls=%async_computation.2 | async-start | bytes 524288 | tf_op jit(solution)/shard_map/all_to_all | solution.py:46
  37.5 105.7 %reduce-scatter.4.cloned.1.call-start = ((), (), s32[]{:S(2)}) async-start(), calls=%async_computation.7 | async-start | bytes 409600 | tf_op jit(solution)/shard_map/reduce_scatter | solution.py:94
  76.3 66.9 %copy-start.3 = (bf16[32,1280]{1,0:T(8,128)(2,1)S(1)}, bf16[32,1280]{1,0:T(8,128)(2,1)}, u32[]{:S(2)}) copy-start(bf16[32,1280]{1,0:T(8,128)(2,1)} %param.11) | copy-start | bytes 245764
  122.8 64.6 %all-gather.2.cloned.1.call-start = ((), (), s32[]{:S(2)}) async-start(), calls=%async_computation.8 | async-start | bytes 1638400 | tf_op jit(solution)/shard_map/all_gather | solution.py:108
  171.7 59.5 %reduce-scatter.6.cloned.1.call-start = ((), (), s32[]{:S(2)}) async-start(), calls=%async_computation.9 | async-start | bytes 1638400 | tf_op jit(solution)/shard_map/reduce_scatter | solution.py:113
  187.4 6.0 %copy-start.2 = (bf16[128,5120]{1,0:T(8,128)(2,1)S(1)}, bf16[128,5120]{1,0:T(8,128)(2,1)}, u32[]{:S(2)}) copy-start(bf16[128,5120]{1,0:T(8,128)(2,1)} %all-gather.2.cloned.1.call-done) | copy-start | bytes 3932164
  187.4 67.5 %copy-start.1 = (bf16[32,2048]{1,0:T(8,128)(2,1)S(1)}, bf16[32,2048]{1,0:T(8,128)(2,1)}, u32[]{:S(2)}) copy-start(bf16[32,2048]{1,0:T(8,128)(2,1)} %param.12) | copy-start | bytes 393220
  193.4 59.9 %copy-start.4 = (bf16[32,1280]{1,0:T(8,128)(2,1)S(1)}, bf16[32,1280]{1,0:T(8,128)(2,1)}, u32[]{:S(2)}) copy-start(bf16[32,1280]{1,0:T(8,128)(2,1)} %reduce-scatter.4.cloned.1.call-done) | copy-start | bytes 245764
  204.5 48.9 %reduce-scatter.8.cloned.1.call-start = ((), (), s32[]{:S(2)}) async-start(), calls=%async_computation.10 | async-start | bytes 409600 | tf_op jit(solution)/shard_map/reduce_scatter | solution.py:116
Sparse Core Ops, SparseCore 0:
  122.9 20.2 reduce-scatter.3
  171.9 15.5 all-gather.1
  204.7 26.5 reduce-scatter.5
  233.3 20.0 reduce-scatter.7
where the time goes:
time: 262 us; the launch traced here: 261 us
  waiting for transfers between devices  91.4 us (35%)
  matrix products  54.9 us (21%)
  blocking collectives  53.1 us (20%)
  other arithmetic  24 us (9%)
  starting transfers between devices  15 us (6%)
  between operations  13.3 us (5%)
  local copies, waits for them, and re-layouts  9.74 us (4%)
    reduce_scatter x1, waiting for transfers between devices, shards(): lax.psum_scatter(partial_sum.astype(jnp.bfloat16), 'heads', scatter_dimen...  26.6 us
    reduce_scatter x1, waiting for transfers between devices, shards(): lax.psum_scatter(section_sum, 'rows', scatter_dimension=1, tiled=True)  22.2 us
    reduce_scatter x1, waiting for transfers between devices, shards(): lax.psum_scatter(head_terms.astype(jnp.bfloat16), 'heads', scatter_dimens...  19.6 us
    dot_general x1, matrix products, shards(): jnp.einsum('skgd,bktd->skgbt', queries_in, key_codes, preferred_element_t...  16.3 us
    all_gather x1, blocking collectives, shards(): lax.all_gather(attended, 'rows', axis=0, tiled=True)  16.2 us
    reduce_sum x1, other arithmetic, shards(): denom_sum = jnp.sum(weights, axis=(3, 4))  15.7 us
    all_gather x1, waiting for transfers between devices, shards(): piece_rows = lax.all_gather(full_rows, 'heads', axis=0, tiled=True)  15.6 us
    dot_general x1, matrix products, shards(): jnp.einsum('skgbt,bktd->skgd', weights.astype(jnp.bfloat16), value_codes,...  15.4 us
  transfers between devices with their start and end apart: 7, of which 6 were waited for; matrix products, arithmetic and copies ran while one was open for 5% of the time, Pallas kernels for 0%

commit v1 on v0

v1 whole, which is shorter than its diff:
```python
import functools
import math

import jax
import jax.numpy as jnp
from jax import lax
from jax.experimental import pallas as pl
from jax.experimental.pallas import tpu as pltpu
from jax.sharding import PartitionSpec as P

norm_eps = 1e-06
log2_e = 1.4426950408889634
mib = 1 << 20
lanes = 128
f32 = jnp.float32
bf16 = jnp.bfloat16

vmem = functools.partial(pl.BlockSpec, memory_space=pltpu.VMEM)
smem = functools.partial(pl.BlockSpec, memory_space=pltpu.SMEM)
hbm = functools.partial(pl.BlockSpec, memory_space=pl.ANY)


def iota(shape, dim):
    return lax.broadcasted_iota(jnp.int32, shape, dim)


def mxu(a, b, contract):
    return lax.dot_general(a, b, ((contract[:1], contract[1:]), ((), ())), preferred_element_type=f32)


def dispatch_kernel(blocks_dev, me_ref, ids_ref, len_ref, q_ref, place_ref, *send_refs):
    count = len(send_refs)
    slots = send_refs[0].shape[0]
    width = q_ref.shape[1]
    rows, listed = ids_ref.shape
    me = me_ref[0]
    ids = ids_ref[...].astype(f32)
    owner = jnp.floor((ids[:, 0:1] + 0.5) * (1.0 / blocks_dev))
    ahead = owner - me.astype(f32)
    ahead = jnp.where(ahead < 0, ahead + count, ahead)
    lane = iota((rows, lanes), 1)
    hot = jnp.where(lane.astype(f32) == ahead, 1.0, 0.0)
    lower = jnp.where(iota((rows, rows), 1) < iota((rows, rows), 0), 1.0, 0.0)
    before = mxu(lower.astype(bf16), hot.astype(bf16), (1, 0))
    rank = jnp.sum(before * hot, axis=1, keepdims=True)
    target = ahead * slots + rank
    place = jnp.where(iota((rows, count * slots), 1).astype(f32) == target, 1.0, 0.0).astype(bf16)
    place_ref[...] = place
    local = (ids - owner * blocks_dev).astype(bf16)
    eye = jnp.where(iota((listed, lanes), 0) == iota((listed, lanes), 1), 1.0, 0.0).astype(bf16)
    meta = mxu(local, eye, (1, 0))
    spread = jnp.broadcast_to(len_ref[...].astype(f32), (rows, rows))
    length = jnp.sum(
        jnp.where(iota((rows, rows), 0) == iota((rows, rows), 1), spread, 0.0), axis=1, keepdims=True
    )
    high = jnp.floor(length * (1.0 / 64))
    meta = jnp.where(lane == listed, high, meta)
    meta = jnp.where(lane == listed + 1, length - high * 64, meta)
    send = mxu(place, q_ref[...], (0, 0)).astype(bf16)
    send_meta = mxu(place, meta.astype(bf16), (0, 0)).astype(bf16)
    for s in range(count):
        send_refs[s][:, 0:width] = send[s * slots : (s + 1) * slots]
        send_refs[s][:, width : width + lanes] = send_meta[s * slots : (s + 1) * slots]


def dispatch(me, queries, row_blocks, row_len, count, slots, blocks_dev):
    rows, width = queries.shape
    outs = [jax.ShapeDtypeStruct((rows, count * slots), bf16)]
    outs += [jax.ShapeDtypeStruct((slots, width + lanes), bf16)] * count
    got = pl.pallas_call(
        functools.partial(dispatch_kernel, blocks_dev),
        out_shape=outs,
        in_specs=[smem(), vmem(), vmem(), vmem()],
        out_specs=[vmem()] * (count + 1),
        name="dispatch",
    )(me, row_blocks, row_len.reshape(1, rows), queries)
    return got[0], got[1:]


tile_rows = 16


def attend_kernel(count, listed, group, step_blocks, scale_ref, kv_ref, *refs):
    in_refs, out_refs = refs[:count], refs[count : 2 * count]
    kv, qs, os, lens, ints, scalars, kv_sem, int_sem = refs[2 * count :]
    slots = out_refs[0].shape[0]
    width = out_refs[0].shape[1]
    total = count * slots
    places = qs.shape[0]
    heads, tok, dim = kv.shape[2:]
    kv_copy = pltpu.make_async_copy(kv_ref, kv, kv_sem)
    kv_copy.start()

    meta = jnp.concatenate([r[:, width : width + lanes] for r in in_refs], axis=0).astype(f32)
    lane = iota((total, lanes), 1)
    length = jnp.sum(
        jnp.where(lane == listed, meta * 64.0, jnp.where(lane == listed + 1, meta, 0.0)), axis=1, keepdims=True
    )
    ids = jnp.where(lane < listed, meta, 0.0)
    slot = iota((total, 1), 0).astype(f32)
    valid = length > 0.0
    big = float(total)

    def first_list(mask):
        first = jnp.min(jnp.where(mask, slot, big), axis=0, keepdims=True)
        return jnp.sum(jnp.where(slot == first, ids, 0.0), axis=0, keepdims=True)

    list_a = first_list(valid)
    same_a = jnp.sum(jnp.abs(ids - list_a), axis=1, keepdims=True) == 0.0
    in_a = valid & same_a
    in_b = valid & jnp.logical_not(same_a)
    list_b = first_list(in_b)
    span = float(2 * listed * tok)
    key = jnp.where(in_a, 2 * span + length, jnp.where(in_b, span + length, 0.0))
    key = key * total + (total - 1 - slot)
    eye = iota((total, total), 0) == iota((total, total), 1)
    key_row = jnp.sum(jnp.where(eye, key, 0.0), axis=0, keepdims=True)
    len_row = jnp.sum(jnp.where(eye, length, 0.0), axis=0, keepdims=True)
    rank = jnp.sum(jnp.where(key > key_row, 1.0, 0.0), axis=0, keepdims=True)
    a_row = key_row >= 2 * span * total
    b_row = jnp.logical_and(key_row >= span * total, jnp.logical_not(a_row))
    a_count = jnp.sum(jnp.where(a_row, 1.0, 0.0), axis=1, keepdims=True)
    a_tiles = jnp.floor((a_count + (tile_rows - 1)) * (1.0 / tile_rows))
    spot = jnp.where(a_row, rank, jnp.where(b_row, rank - a_count + a_tiles * tile_rows, float(places)))
    placed = iota((places, total), 0).astype(f32) == spot
    perm = jnp.where(placed, 1.0, 0.0).astype(bf16)
    len_sorted = jnp.sum(jnp.where(placed, len_row, 0.0), axis=1, keepdims=True)
    lens[...] = jnp.broadcast_to(len_sorted, (places, lanes)).astype(jnp.int32)
    tops = jnp.sum(
        jnp.where(iota((places, lanes), 0) == iota((places, lanes), 1) * tile_rows, len_sorted, 0.0),
        axis=0,
        keepdims=True,
    )
    row = iota((8, lanes), 0)
    ints[...] = jnp.where(
        row == 0, list_a, jnp.where(row == 1, list_b, jnp.where(row == 2, tops, a_tiles))
    ).astype(jnp.int32)
    int_copy = pltpu.make_async_copy(ints, scalars, int_sem)
    int_copy.start()
    queries = jnp.concatenate([r[:, 0:width] for r in in_refs], axis=0)
    qs[...] = mxu(perm, queries, (1, 0)).astype(bf16)
    os[...] = jnp.zeros_like(os)
    int_copy.wait()
    kv_copy.wait()

    tokens = step_blocks * tok
    tall = group * tile_rows
    factors = [scale_ref[0, k] * (log2_e / math.sqrt(dim)) for k in range(heads)]
    spread = iota((tall, tokens), 1)

    def tile_body(t, _):
        top = scalars[2, t]
        doc = jnp.where(t >= scalars[3, 0], 1, 0)
        at = pl.multiple_of(t * tile_rows, tile_rows)
        spans = jnp.concatenate([lens[pl.ds(at, tile_rows), :]] * group, axis=0)[:, 0:1]
        qt = [
            jnp.concatenate(
                [qs[pl.ds(at, tile_rows), (k * group + g) * dim : (k * group + g + 1) * dim] for g in range(group)],
                axis=0,
            )
            for k in range(heads)
        ]

        def step(c, carry):
            keep = spread < spans - c * tokens
            blocks = [scalars[doc, c * step_blocks + j] for j in range(step_blocks)]
            after = []
            for k in range(heads):
                peak, denom, acc = carry[k]
                keys = jnp.concatenate([kv[b, 0, k] for b in blocks], axis=0)
                scores = mxu(qt[k], keys, (1, 1)) * factors[k]
                scores = jnp.where(keep, scores, -1e30)
                higher = jnp.maximum(peak, jnp.max(scores, axis=1, keepdims=True))
                shrink = jnp.exp2(peak - higher)
                weights = jnp.exp2(scores - higher)
                denom = denom * shrink + jnp.sum(weights, axis=1, keepdims=True)
                values = jnp.concatenate([kv[b, 1, k] for b in blocks], axis=0)
                acc = acc * shrink + mxu(weights.astype(bf16), values, (1, 0))
                after.append((higher, denom, acc))
            return tuple(after)

        start = tuple(
            (jnp.full((tall, 1), -1e30, f32), jnp.zeros((tall, 1), f32), jnp.zeros((tall, dim), f32))
            for _ in range(heads)
        )
        steps = (top + (tokens - 1)) // tokens

        @pl.when(steps > 0)
        def _():
            done = lax.fori_loop(0, steps, step, start)
            for k in range(heads):
                _, denom, acc = done[k]
                out = (acc * (scale_ref[1, k] / denom)).astype(bf16)
                for g in range(group):
                    col = (k * group + g) * dim
                    os[pl.ds(at, tile_rows), col : col + dim] = out[g * tile_rows : (g + 1) * tile_rows]

        return 0

    lax.fori_loop(0, places // tile_rows, tile_body, 0)
    out = mxu(perm, os[...], (0, 0)).astype(bf16)
    for s in range(count):
        out_refs[s][...] = out[s * slots : (s + 1) * slots]


def attend(received, kv_codes, kv_scale, listed, group):
    count = len(received)
    slots, wide = received[0].shape
    width = wide - lanes
    total = count * slots
    places = total + tile_rows
    return pl.pallas_call(
        functools.partial(attend_kernel, count, listed, group, min(8, listed)),
        out_shape=[jax.ShapeDtypeStruct((slots, width), bf16)] * count,
        in_specs=[smem(), hbm()] + [vmem()] * count,
        out_specs=[vmem()] * count,
        scratch_shapes=[
            pltpu.VMEM(kv_codes.shape, bf16),
            pltpu.VMEM((places, width), bf16),
            pltpu.VMEM((places, width), bf16),
            pltpu.VMEM((places, lanes), jnp.int32),
            pltpu.VMEM((8, lanes), jnp.int32),
            pltpu.SMEM((8, lanes), jnp.int32),
            pltpu.SemaphoreType.DMA,
            pltpu.SemaphoreType.DMA,
        ],
        compiler_params=pltpu.CompilerParams(vmem_limit_bytes=32 * mib),
        name="attend",
    )(kv_scale, kv_codes, *received)


def project_kernel(count, parts, at_ref, *refs):
    in_refs, w_ref = refs[:count], refs[count]
    own_ref, out_refs = refs[count + 1], refs[count + 2 : count + 1 + parts]
    x, y = refs[count + 1 + parts :]
    rows = in_refs[0].shape[0]
    piece = own_ref.shape[0]

    @pl.when(pl.program_id(0) == 0)
    def _():
        for s in range(count):
            source = at_ref[0] - s
            source = jnp.where(source < 0, source + count, source)
            x[pl.ds(pl.multiple_of(source * rows, rows), rows), :] = in_refs[s][...]

    y[...] = mxu(x[...], w_ref[...], (1, 0))
    for s in range(parts):
        target = at_ref[1] + s
        target = jnp.where(target >= parts, target - parts, target)
        value = y[pl.ds(pl.multiple_of(target * piece, piece), piece), :]
        if s == 0:
            own_ref[...] = value
        else:
            out_refs[s - 1][...] = value.astype(bf16)


def project(at, pieces, w_out, parts):
    count = len(pieces)
    rows, depth = pieces[0].shape
    cols = w_out.shape[1]
    tall = rows * count
    piece = tall // parts
    wide = 256 if cols % 256 == 0 else cols
    whole = pl.BlockSpec((rows, depth), lambda j: (0, 0))
    part = pl.BlockSpec((piece, wide), lambda j: (0, j))
    got = pl.pallas_call(
        functools.partial(project_kernel, count, parts),
        grid=(cols // wide,),
        out_shape=[jax.ShapeDtypeStruct((piece, cols), f32)]
        + [jax.ShapeDtypeStruct((piece, cols), bf16)] * (parts - 1),
        in_specs=[smem()] + [whole] * count + [pl.BlockSpec((depth, wide), lambda j: (0, j))],
        out_specs=[part] * parts,
        scratch_shapes=[pltpu.VMEM((tall, depth), bf16), pltpu.VMEM((tall, wide), f32)],
        compiler_params=pltpu.CompilerParams(vmem_limit_bytes=32 * mib),
        name="project",
    )(at, *pieces, w_out)
    return got[0], got[1:]


def shift(x, axis, step):
    n = lax.axis_size(axis)
    return lax.ppermute(x, axis, [(i, (i + step) % n) for i in range(n)])


def shards(
    resid, queries, kv_codes, kv_scale, row_blocks, row_len, w_out, norm_gain, w_gate, w_up, w_down
):
    row_devs = lax.axis_size("rows")
    head_devs = lax.axis_size("heads")
    rows_dev, width_q = queries.shape
    listed = row_blocks.shape[1]
    blocks_dev = kv_codes.shape[0]
    heads_dev, head_dim = kv_codes.shape[2], kv_codes.shape[4]
    group = width_q // (heads_dev * head_dim)
    capacity = max(2, 2 * rows_dev // row_devs)
    slots = -(-capacity // 16) * 16
    my_row = lax.axis_index("rows").astype(jnp.int32)
    my_head = lax.axis_index("heads").astype(jnp.int32)
    at = jnp.stack([my_row, my_head])

    place, sends = dispatch(at, queries, row_blocks, row_len, row_devs, slots, blocks_dev)
    received = [sends[0]] + [shift(sends[s], "rows", s) for s in range(1, row_devs)]
    results = attend(received, kv_codes, kv_scale, listed, group)
    back = [results[0]] + [shift(results[s], "rows", -s) for s in range(1, row_devs)]
    attended = jnp.dot(place, jnp.concatenate(back, axis=0), preferred_element_type=f32).astype(bf16)
    pieces = [attended] + [shift(attended, "rows", s) for s in range(1, row_devs)]
    own, others = project(at, pieces, w_out, head_devs)
    attn_out = own
    for s in range(1, head_devs):
        attn_out = attn_out + shift(others[s - 1], "heads", s).astype(f32)
    hidden_state = (resid.astype(f32) + attn_out).astype(bf16)

    as_float = hidden_state.astype(f32)
    cols_dev = hidden_state.shape[1]
    model_width = cols_dev * row_devs
    full_rows = lax.all_gather(hidden_state, "rows", axis=1, tiled=True)
    piece_rows = lax.all_gather(full_rows, "heads", axis=0, tiled=True).astype(f32)
    totals = jnp.sum(piece_rows * piece_rows, axis=1)
    piece_rows = (
        piece_rows * lax.rsqrt(totals / model_width + norm_eps)[:, None] * norm_gain
    ).astype(bf16)
    gate_proj = jnp.dot(piece_rows, w_gate, preferred_element_type=f32)
    up_proj = jnp.dot(piece_rows, w_up, preferred_element_type=f32)
    inner_act = (jax.nn.silu(gate_proj) * up_proj).astype(bf16)
    partial_sum = jnp.dot(inner_act, w_down, preferred_element_type=f32)
    section_sum = lax.psum_scatter(partial_sum.astype(bf16), "heads", scatter_dimension=0, tiled=True)
    ffn_out = lax.psum_scatter(section_sum, "rows", scatter_dimension=1, tiled=True).astype(f32)
    return (as_float + ffn_out).astype(bf16)


def solution(mesh):
    placed = (
        P(("groups", "heads"), "rows"),
        P(("groups", "rows"), "heads"),
        P(("groups", "rows"), None, "heads", None, None),
        P("groups", "heads"),
        P(("groups", "rows"), None),
        P(("groups", "rows")),
        P("heads", "rows"),
        P(),
        P(None, ("rows", "heads")),
        P(None, ("rows", "heads")),
        P(("rows", "heads"), None),
    )
    return jax.shard_map(
        shards,
        mesh=mesh,
        in_specs=placed,
        out_specs=P(("groups", "heads"), "rows"),
        check_vma=False,
    )
```

time: 262 us -> 175 us (0.67)
  matrix products: 54.9 us -> 17.3 us
  blocking collectives: 53.1 us -> 15.7 us
  other arithmetic: 24 us -> 3.89 us
  Pallas kernels: 0 us -> 14.8 us
  local copies, waits for them, and re-layouts: 9.74 us -> 4.97 us
  waiting for transfers between devices: 91.4 us -> 87.1 us
    dot_general x9 -> x3, matrix products: 54.9 us -> 17.3 us  [the longest x1 11.1 us: shards(): partial_sum = jnp.dot(inner_act, w_down, preferred_element_type=f32)]
    ppermute x0 -> x12, waiting for transfers between devices: none -> 22.3 us  [shift(): return lax.ppermute(x, axis, [(i, (i + step) % n) for i in range(n)])]
    reduce_scatter x2 -> x1, waiting for transfers between devices: 46.2 us -> 26.6 us  [shards(): lax.psum_scatter(partial_sum.astype(bf16), 'heads', scatter_dimension=0,...]
    ppermute x0 -> x12, starting transfers between devices: none -> 17.3 us  [shift(): return lax.ppermute(x, axis, [(i, (i + step) % n) for i in range(n)])]
    reduce_sum x4 -> x1, other arithmetic: 17.3 us -> 1.65 us  [shards(): totals = jnp.sum(piece_rows * piece_rows, axis=1)]
    all_gather x2 -> x1, blocking collectives: 31 us -> 15.7 us  [shards(): full_rows = lax.all_gather(hidden_state, 'rows', axis=1, tiled=True)]
    all_to_all x3 -> x0, starting transfers between devices: 14.8 us -> none  [the longest x1 6.32 us: shards(): lax.all_to_all(send_lens, 'rows', split_axis=0, concat_axis=0, tiled=True)]
    pallas_call x0 -> x3, Pallas kernels: none -> 14.8 us  [the longest x1 9.82 us: attend(): pl.pallas_call(functools.partial(attend_kernel, count, listed, group, min...]
  transfers between devices with their start and end apart: 7 -> 15, of which waited for: 6 -> 12; matrix products, arithmetic and copies ran while one was open for 5% -> 0% of each run, Pallas kernels for 0% -> 0%
where the time goes in v1:
time: 175 us; the launch traced here: 174 us
  waiting for transfers between devices  87.1 us (50%)
  starting transfers between devices  17.4 us (10%)
  matrix products  17.3 us (10%)
  blocking collectives  15.7 us (9%)
  Pallas kernels  14.8 us (8%)
  between operations  13.2 us (8%)
  local copies, waits for them, and re-layouts  4.97 us (3%)
  other arithmetic  3.89 us (2%)
    reduce_scatter x1, waiting for transfers between devices, shards(): lax.psum_scatter(partial_sum.astype(bf16), 'heads', scatter_dimension=0,...  26.6 us
    reduce_scatter x1, waiting for transfers between devices, shards(): lax.psum_scatter(section_sum, 'rows', scatter_dimension=1, tiled=True)  22.4 us
    ppermute x12, waiting for transfers between devices, shift(): return lax.ppermute(x, axis, [(i, (i + step) % n) for i in range(n)])  22.3 us
    ppermute x12, starting transfers between devices, shift(): return lax.ppermute(x, axis, [(i, (i + step) % n) for i in range(n)])  17.3 us
    all_gather x1, blocking collectives, shards(): full_rows = lax.all_gather(hidden_state, 'rows', axis=1, tiled=True)  15.7 us
    all_gather x1, waiting for transfers between devices, shards(): lax.all_gather(full_rows, 'heads', axis=0, tiled=True).astype(f32)  15.7 us
    dot_general x1, matrix products, shards(): partial_sum = jnp.dot(inner_act, w_down, preferred_element_type=f32)  11.1 us
    pallas_call x1, Pallas kernels, attend(): pl.pallas_call(functools.partial(attend_kernel, count, listed, group, min...  9.82 us
  transfers between devices with their start and end apart: 15, of which 12 were waited for; matrix products, arithmetic and copies ran while one was open for 0% of the time, Pallas kernels for 0%

profile of v1, /device:TPU:0, one launch (start us, length us, event | category | flops | bytes accessed | tf_op | source)
XLA Modules:
  0.0 174.3 jit_solution(8316016669794581957)
XLA Ops:
  7.2 2.2 %dispatch.1 = (bf16[32,64]{1,0:T(8,128)(2,1)}, bf16[16,2176]{1,0:T(8,128)(2,1)}, bf16[16,2176]{1,0:T(8,128)(2,1)}, bf16[16,2176]{1,0:T(8,128)(2,1)}, bf16[16,2176]{1,0:T(8,128)(2,1)}) custom-call(s32[2]{0:T(128)} %pad_add_fusion.me_ref.at_ref, s32[32,32]{1,0:T(8,128)} %ids_ref.1, s32[1,32]{1,0:T(1,128)} %bitcast.7, bf16[32,2048]{1,0:T(8,128)(2,1)} %q_ref.1), custom_call_target="tpu_custom_call" | custom-call | tf_op jit(solution)/shard_map/dispatch/pallas_call | solution.py:70
  9.4 3.0 %collective-permute-start = (bf16[16,2176]{1,0:T(8,128)(2,1)}, bf16[16,2176]{1,0:T(8,128)(2,1)S(1)}, u32[]{:S(2)}, u32[]{:S(2)}) collective-permute-start(bf16[16,2176]{1,0:T(8,128)(2,1)} %get-tuple-element.20), channel_id=1, source_target_pairs={{0,4},{4,8},{8,12},{12,0},{1,5},{5,9},{9,13},{13,1},{2,6},{6,10},{... | collective-permute-start | bytes 208904 | tf_op jit(solution)/shard_map/ppermute | solution.py:282
  12.4 2.6 %collective-permute-start.1 = (bf16[16,2176]{1,0:T(8,128)(2,1)}, bf16[16,2176]{1,0:T(8,128)(2,1)S(1)}, u32[]{:S(2)}, u32[]{:S(2)}) collective-permute-start(bf16[16,2176]{1,0:T(8,128)(2,1)} %get-tuple-element.21), channel_id=1, source_target_pairs={{0,8},{4,12},{8,0},{12,4},{1,9},{5,13},{9,1},{13,5},{2,10},{6,14},... | collective-permute-start | bytes 208904 | tf_op jit(solution)/shard_map/ppermute | solution.py:282
  15.0 1.3 collective-permute-start.2
  17.3 2.6 %collective-permute-done.1.refs_2_ = bf16[16,2176]{1,0:T(8,128)(2,1)S(1)} collective-permute-done((bf16[16,2176]{1,0:T(8,128)(2,1)}, bf16[16,2176]{1,0:T(8,128)(2,1)S(1)}, u32[]{:S(2)}, u32[]{:S(2)}) %collective-permute-start.1) | collective-permute-done | bytes 69664 | tf_op jit(solution)/shard_map/ppermute | solution.py:282
  20.1 3.4 %copy-done = bf16[64,2,2,128,128]{4,3,2,1,0:T(8,128)(2,1)S(1)} copy-done((bf16[64,2,2,128,128]{4,3,2,1,0:T(8,128)(2,1)S(1)}, bf16[64,2,2,128,128]{4,3,2,1,0:T(8,128)(2,1)}, u32[]{:S(2)}) %copy-start) | copy-done | bytes 8388632
  25.1 9.8 %attend.1 = (bf16[16,2048]{1,0:T(8,128)(2,1)S(1)}, bf16[16,2048]{1,0:T(8,128)(2,1)S(1)}, bf16[16,2048]{1,0:T(8,128)(2,1)S(1)}, bf16[16,2048]{1,0:T(8,128)(2,1)S(1)}) custom-call(f32[2,2]{1,0:T(2,128)S(1)} %copy-done.4, bf16[64,2,2,128,128]{4,3,2,1,0:T(8,128)(2,1)S(1)} %copy-done, bf16[16,2176]{1,0:T(8,128)(2,1)S(1)} %copy-done.2, ...), custom_call_target="tpu_custom_call" | custom-call | tf_op jit(solution)/shard_map/attend/pallas_call | solution.py:212
  34.9 4.1 %collective-permute-start.3 = (bf16[16,2048]{1,0:T(8,128)(2,1)S(1)}, bf16[16,2048]{1,0:T(8,128)(2,1)S(1)}, u32[]{:S(2)}, u32[]{:S(2)}) collective-permute-start(bf16[16,2048]{1,0:T(8,128)(2,1)S(1)} %get-tuple-element.24), channel_id=1, source_target_pairs={{0,12},{4,0},{8,4},{12,8},{1,13},{5,1},{9,5},{13,9},{2,14},{6,2},{... | collective-permute-start | bytes 196616 | tf_op jit(solution)/shard_map/ppermute | solution.py:282
  40.0 1.5 collective-permute-done.3
  41.5 4.7 %collective-permute-done.4 = bf16[16,2048]{1,0:T(8,128)(2,1)S(1)} collective-permute-done((bf16[16,2048]{1,0:T(8,128)(2,1)S(1)}, bf16[16,2048]{1,0:T(8,128)(2,1)S(1)}, u32[]{:S(2)}, u32[]{:S(2)}) %collective-permute-start.4) | collective-permute-done | bytes 65568 | tf_op jit(solution)/shard_map/ppermute | solution.py:282
  47.6 1.3 collective-permute-start.6
  48.9 3.0 %collective-permute-done.8.refs_3_ = bf16[32,2048]{1,0:T(8,128)(2,1)S(1)} collective-permute-done((bf16[32,2048]{1,0:T(8,128)(2,1)S(1)}, bf16[32,2048]{1,0:T(8,128)(2,1)S(1)}, u32[]{:S(2)}, u32[]{:S(2)}) %collective-permute-start.8) | collective-permute-done | bytes 131104 | tf_op jit(solution)/shard_map/ppermute | solution.py:282
  51.9 6.7 %collective-permute-done.7.refs_2_ = bf16[32,2048]{1,0:T(8,128)(2,1)S(1)} collective-permute-done((bf16[32,2048]{1,0:T(8,128)(2,1)S(1)}, bf16[32,2048]{1,0:T(8,128)(2,1)S(1)}, u32[]{:S(2)}, u32[]{:S(2)}) %collective-permute-start.7) | collective-permute-done | bytes 131104 | tf_op jit(solution)/shard_map/ppermute | solution.py:282
  58.6 2.7 %project.1 = (f32[32,1280]{1,0:T(8,128)S(1)}, bf16[32,1280]{1,0:T(8,128)(2,1)S(1)}, bf16[32,1280]{1,0:T(8,128)(2,1)S(1)}, bf16[32,1280]{1,0:T(8,128)(2,1)S(1)}) custom-call(s32[2]{0:T(128)S(1)} %copy-done.3, bf16[32,2048]{1,0:T(8,128)(2,1)S(1)} %convolution_convert_fusion.1.refs_0_, bf16[32,2048]{1,0:T(8,128)(2,1)S(1)} %collective-permute-done.6.refs_1_, ...), custom_call_target="tpu_custom_call" | custom-call | tf_op jit(solution)/shard_map/project/pallas_call | solution.py:266
  62.6 1.4 collective-permute-start.11
  64.0 1.5 collective-permute-done.9
  66.8 15.7 %all_gather.6 = bf16[32,5120]{1,0:T(8,128)(2,1)} all-gather(bf16[32,1280]{1,0:T(8,128)(2,1)S(1)} %add_convert_fusion.1), channel_id=1, replica_groups=mesh['groups'=2,'rows'=4,'heads'=4] {'rows'}, dimensions={1}, use_global_device_ids=true | all-gather | bytes 409600 | tf_op jit(solution)/shard_map/all_gather | solution.py:316
  82.5 15.7 %all-gather.2.cloned.1.call-done = bf16[128,5120]{1,0:T(8,128)(2,1)} async-done(((bf16[32,5120]{1,0:T(8,128)(2,1)}), bf16[128,5120]{1,0:T(8,128)(2,1)}) %all-gather.2.cloned.1.call-update) | async-done | bytes 1310736 | tf_op jit(solution)/shard_map/all_gather | solution.py:317
  98.2 1.6 fusion
  99.9 6.0 %fusion.11 = f32[128,1024]{1,0:T(8,128)S(1)} fusion(bf16[5120,1024]{1,0:T(8,128)(2,1)} %param.19, bf16[128,5120]{1,0:T(8,128)(2,1)} %all-gather.2.cloned.1.call-done, f32[5120]{0:T(1024)S(1)} %copy-done.6, f32[128]{0:T(128)S(1)} %add_rsqrt_fusion), kind=kOutput, calls=%fused_computation.14 | convolution fusion | flops 1344798720 | bytes 12341760 | tf_op jit(solution)/shard_map/dot_general | solution.py:322
  106.0 11.1 %convolution_convert_fusion = bf16[128,5120]{1,0:T(8,128)(2,1)} fusion(bf16[1024,5120]{1,0:T(8,128)(2,1)} %param.21, bf16[5120,1024]{1,0:T(8,128)(2,1)} %param.20, f32[128,1024]{1,0:T(8,128)S(1)} %fusion.11, bf16[128,5120]{1,0:T(8,128)(2,1)S(1)} %copy-done.5, f32[5120]{0:T(1024)S(1)} %copy-done.6, f32[128]{0:T(128)S(1)} %add_rsqrt_fusion), kind=kOutput, calls=%fused_computation | convolution fusion | flops 2688417792 | bytes 24138240 | tf_op jit(solution)/shard_map/dot_general | solution.py:325
  117.1 26.6 %reduce-scatter.3.cloned.1.call-done = bf16[32,5120]{1,0:T(8,128)(2,1)} async-done(((bf16[128,5120]{1,0:T(8,128)(2,1)}), bf16[32,5120]{1,0:T(8,128)(2,1)}) %reduce-scatter.3.cloned.1.call-update) | async-done | bytes 327696 | tf_op jit(solution)/shard_map/reduce_scatter | solution.py:326
  143.8 22.4 %reduce-scatter.5.cloned.1.call-done = bf16[32,1280]{1,0:T(8,128)(2,1)} async-done(((bf16[32,5120]{1,0:T(8,128)(2,1)}), bf16[32,1280]{1,0:T(8,128)(2,1)}) %reduce-scatter.5.cloned.1.call-update) | async-done | bytes 81936 | tf_op jit(solution)/shard_map/reduce_scatter | solution.py:327
  166.2 1.5 add_convert_fusion
  (39 shorter events, 8.4 us)
Async XLA Ops:
  6.5 91.7 %all-gather.2.cloned.1.call-start = ((), (), s32[]{:S(2)}) async-start(), calls=%async_computation.2 | async-start | bytes 1638400 | tf_op jit(solution)/shard_map/all_gather | solution.py:317
  9.4 7.9 %collective-permute-start = (bf16[16,2176]{1,0:T(8,128)(2,1)}, bf16[16,2176]{1,0:T(8,128)(2,1)S(1)}, u32[]{:S(2)}, u32[]{:S(2)}) collective-permute-start(bf16[16,2176]{1,0:T(8,128)(2,1)} %get-tuple-element.20), channel_id=1, source_target_pairs={{0,4},{4,8},{8,12},{12,0},{1,5},{5,9},{9,13},{13,1},{2,6},{6,10},{... | collective-permute-start | bytes 208904 | tf_op jit(solution)/shard_map/ppermute | solution.py:282
  12.4 7.5 %collective-permute-start.1 = (bf16[16,2176]{1,0:T(8,128)(2,1)}, bf16[16,2176]{1,0:T(8,128)(2,1)S(1)}, u32[]{:S(2)}, u32[]{:S(2)}) collective-permute-start(bf16[16,2176]{1,0:T(8,128)(2,1)} %get-tuple-element.21), channel_id=1, source_target_pairs={{0,8},{4,12},{8,0},{12,4},{1,9},{5,13},{9,1},{13,5},{2,10},{6,14},... | collective-permute-start | bytes 208904 | tf_op jit(solution)/shard_map/ppermute | solution.py:282
  15.0 5.1 %collective-permute-start.2 = (bf16[16,2176]{1,0:T(8,128)(2,1)}, bf16[16,2176]{1,0:T(8,128)(2,1)S(1)}, u32[]{:S(2)}, u32[]{:S(2)}) collective-permute-start(bf16[16,2176]{1,0:T(8,128)(2,1)} %get-tuple-element.22), channel_id=1, source_target_pairs={{0,12},{4,0},{8,4},{12,8},{1,13},{5,1},{9,5},{13,9},{2,14},{6,2},{... | collective-permute-start | bytes 208904 | tf_op jit(solution)/shard_map/ppermute | solution.py:282
  20.1 3.4 %copy-start = (bf16[64,2,2,128,128]{4,3,2,1,0:T(8,128)(2,1)S(1)}, bf16[64,2,2,128,128]{4,3,2,1,0:T(8,128)(2,1)}, u32[]{:S(2)}) copy-start(bf16[64,2,2,128,128]{4,3,2,1,0:T(8,128)(2,1)} %kv_ref.1) | copy-start | bytes 25165828
  23.5 0.9 copy-start.2
  24.4 0.7 copy-start.4
  25.1 21.2 %copy-start.8 = (bf16[32,64]{1,0:T(8,128)(2,1)S(1)}, bf16[32,64]{1,0:T(8,128)(2,1)}, u32[]{:S(2)}) copy-start(bf16[32,64]{1,0:T(8,128)(2,1)} %get-tuple-element.18) | copy-start | bytes 12292
  25.1 33.5 %copy-start.1 = (bf16[2048,1280]{1,0:T(8,128)(2,1)S(1)}, bf16[2048,1280]{1,0:T(8,128)(2,1)}, u32[]{:S(2)}) copy-start(bf16[2048,1280]{1,0:T(8,128)(2,1)} %refs_4_.1) | copy-start | bytes 15728644
  25.1 33.5 %copy-start.3 = (s32[2]{0:T(128)S(1)}, s32[2]{0:T(128)}, u32[]{:S(2)}) copy-start(s32[2]{0:T(128)} %pad_add_fusion.me_ref.at_ref) | copy-start | bytes 28
  34.9 6.6 %collective-permute-start.3 = (bf16[16,2048]{1,0:T(8,128)(2,1)S(1)}, bf16[16,2048]{1,0:T(8,128)(2,1)S(1)}, u32[]{:S(2)}, u32[]{:S(2)}) collective-permute-start(bf16[16,2048]{1,0:T(8,128)(2,1)S(1)} %get-tuple-element.24), channel_id=1, source_target_pairs={{0,12},{4,0},{8,4},{12,8},{1,13},{5,1},{9,5},{13,9},{2,14},{6,2},{... | collective-permute-start | bytes 196616 | tf_op jit(solution)/shard_map/ppermute | solution.py:282
  39.0 7.2 %collective-permute-start.4 = (bf16[16,2048]{1,0:T(8,128)(2,1)S(1)}, bf16[16,2048]{1,0:T(8,128)(2,1)S(1)}, u32[]{:S(2)}, u32[]{:S(2)}) collective-permute-start(bf16[16,2048]{1,0:T(8,128)(2,1)S(1)} %get-tuple-element.25), channel_id=1, source_target_pairs={{0,8},{4,12},{8,0},{12,4},{1,9},{5,13},{9,1},{13,5},{2,10},{6,14},... | collective-permute-start | bytes 196616 | tf_op jit(solution)/shard_map/ppermute | solution.py:282
  40.0 6.2 %collective-permute-start.5 = (bf16[16,2048]{1,0:T(8,128)(2,1)S(1)}, bf16[16,2048]{1,0:T(8,128)(2,1)S(1)}, u32[]{:S(2)}, u32[]{:S(2)}) collective-permute-start(bf16[16,2048]{1,0:T(8,128)(2,1)S(1)} %get-tuple-element.26), channel_id=1, source_target_pairs={{0,4},{4,8},{8,12},{12,0},{1,5},{5,9},{9,13},{13,1},{2,6},{6,10},{... | collective-permute-start | bytes 196616 | tf_op jit(solution)/shard_map/ppermute | solution.py:282
  46.4 20.3 %copy-start.7 = (bf16[32,1280]{1,0:T(8,128)(2,1)S(1)}, bf16[32,1280]{1,0:T(8,128)(2,1)}, u32[]{:S(2)}) copy-start(bf16[32,1280]{1,0:T(8,128)(2,1)} %param.11) | copy-start | bytes 245764
  46.4 5.5 %collective-permute-start.8 = (bf16[32,2048]{1,0:T(8,128)(2,1)S(1)}, bf16[32,2048]{1,0:T(8,128)(2,1)S(1)}, u32[]{:S(2)}, u32[]{:S(2)}) collective-permute-start(bf16[32,2048]{1,0:T(8,128)(2,1)S(1)} %convolution_convert_fusion.1.refs_0_), channel_id=1, source_target_pairs={{0,12},{4,0},{8,4},{12,8},{1,13},{5,1},{9,5},{13,9},{2,14},{6,2},{... | collective-permute-start | bytes 393224 | tf_op jit(solution)/shard_map/ppermute | solution.py:282
  46.7 11.9 %collective-permute-start.7 = (bf16[32,2048]{1,0:T(8,128)(2,1)S(1)}, bf16[32,2048]{1,0:T(8,128)(2,1)S(1)}, u32[]{:S(2)}, u32[]{:S(2)}) collective-permute-start(bf16[32,2048]{1,0:T(8,128)(2,1)S(1)} %convolution_convert_fusion.1.refs_0_), channel_id=1, source_target_pairs={{0,8},{4,12},{8,0},{12,4},{1,9},{5,13},{9,1},{13,5},{2,10},{6,14},... | collective-permute-start | bytes 393224 | tf_op jit(solution)/shard_map/ppermute | solution.py:282
  47.6 11.0 %collective-permute-start.6 = (bf16[32,2048]{1,0:T(8,128)(2,1)S(1)}, bf16[32,2048]{1,0:T(8,128)(2,1)S(1)}, u32[]{:S(2)}, u32[]{:S(2)}) collective-permute-start(bf16[32,2048]{1,0:T(8,128)(2,1)S(1)} %convolution_convert_fusion.1.refs_0_), channel_id=1, source_target_pairs={{0,4},{4,8},{8,12},{12,0},{1,5},{5,9},{9,13},{13,1},{2,6},{6,10},{... | collective-permute-start | bytes 393224 | tf_op jit(solution)/shard_map/ppermute | solution.py:282
  61.3 38.6 %copy-start.6 = (f32[5120]{0:T(1024)S(1)}, f32[5120]{0:T(1024)}, u32[]{:S(2)}) copy-start(f32[5120]{0:T(1024)} %param.18) | copy-start | bytes 61444
  61.3 4.2 %collective-permute-start.9 = (bf16[32,1280]{1,0:T(8,128)(2,1)S(1)}, bf16[32,1280]{1,0:T(8,128)(2,1)S(1)}, u32[]{:S(2)}, u32[]{:S(2)}) collective-permute-start(bf16[32,1280]{1,0:T(8,128)(2,1)S(1)} %get-tuple-element.28), channel_id=1, source_target_pairs={{0,1},{1,2},{2,3},{3,0},{4,5},{5,6},{6,7},{7,4},{8,9},{9,10},{10,1... | collective-permute-start | bytes 245768 | tf_op jit(solution)/shard_map/ppermute | solution.py:282
  61.4 5.3 %collective-permute-start.10 = (bf16[32,1280]{1,0:T(8,128)(2,1)S(1)}, bf16[32,1280]{1,0:T(8,128)(2,1)S(1)}, u32[]{:S(2)}, u32[]{:S(2)}) collective-permute-start(bf16[32,1280]{1,0:T(8,128)(2,1)S(1)} %get-tuple-element.29), channel_id=1, source_target_pairs={{0,2},{1,3},{2,0},{3,1},{4,6},{5,7},{6,4},{7,5},{8,10},{9,11},{10,... | collective-permute-start | bytes 245768 | tf_op jit(solution)/shard_map/ppermute | solution.py:282
  62.6 4.1 %collective-permute-start.11 = (bf16[32,1280]{1,0:T(8,128)(2,1)S(1)}, bf16[32,1280]{1,0:T(8,128)(2,1)S(1)}, u32[]{:S(2)}, u32[]{:S(2)}) collective-permute-start(bf16[32,1280]{1,0:T(8,128)(2,1)S(1)} %get-tuple-element.30), channel_id=1, source_target_pairs={{0,3},{1,0},{2,1},{3,2},{4,7},{5,4},{6,5},{7,6},{8,11},{9,8},{10,9... | collective-permute-start | bytes 245768 | tf_op jit(solution)/shard_map/ppermute | solution.py:282
  82.5 61.3 %reduce-scatter.3.cloned.1.call-start = ((), (), s32[]{:S(2)}) async-start(), calls=%async_computation.3 | async-start | bytes 1638400 | tf_op jit(solution)/shard_map/reduce_scatter | solution.py:326
  99.9 6.1 %copy-start.5 = (bf16[128,5120]{1,0:T(8,128)(2,1)S(1)}, bf16[128,5120]{1,0:T(8,128)(2,1)}, u32[]{:S(2)}) copy-start(bf16[128,5120]{1,0:T(8,128)(2,1)} %all-gather.2.cloned.1.call-done) | copy-start | bytes 3932164
  117.1 49.1 %reduce-scatter.5.cloned.1.call-start = ((), (), s32[]{:S(2)}) async-start(), calls=%async_computation.4 | async-start | bytes 409600 | tf_op jit(solution)/shard_map/reduce_scatter | solution.py:327
Sparse Core Ops, SparseCore 0:
  82.6 15.5 all-gather.1
  117.2 26.5 reduce-scatter.2
  146.1 20.0 reduce-scatter.4

commit v2 on v1

--- a/solution.py
+++ b/solution.py
@@ -277,9 +277,161 @@
     return got[0], got[1:]
 
 
+hidden_tile = 256
+
+
+def swiglu_kernel(row_devs, head_devs, at_ref, gain_ref, *refs):
+    pieces = refs[: row_devs * head_devs]
+    gate_ref, up_ref, down_ref = refs[row_devs * head_devs : row_devs * head_devs + 3]
+    outs = refs[row_devs * head_devs + 3 :]
+    keep_refs, send_refs = outs[:row_devs], outs[row_devs : 2 * row_devs]
+    x, gate_w, up_w, down_w, inner, y, gate_sem, up_sem, down_sem = outs[2 * row_devs :]
+    rows, cols = pieces[0].shape
+    tall = x.shape[1]
+    hidden = gate_w.shape[1]
+    steps = hidden // hidden_tile
+
+    def gate_copy(j):
+        cut = pl.ds(j * hidden_tile, hidden_tile)
+        return (
+            pltpu.make_async_copy(gate_ref.at[:, cut], gate_w.at[:, cut], gate_sem.at[j]),
+            pltpu.make_async_copy(up_ref.at[:, cut], up_w.at[:, cut], up_sem.at[j]),
+        )
+
+    def down_copy(i):
+        cut = pl.ds(i * cols, cols)
+        return pltpu.make_async_copy(down_ref.at[:, cut], down_w.at[i], down_sem.at[i])
+
+    for j in range(steps):
+        for copy in gate_copy(j):
+            copy.start()
+    for i in range(row_devs):
+        down_copy(i).start()
+
+    me_row, me_head = at_ref[0], at_ref[1]
+
+    def flip(j):
+        return me_head + (j & 1) * (1 - 2 * lax.rem(me_head, 2)) + (j & 2) * (1 - lax.rem(lax.div(me_head, 2), 2) * 2)
+
+    def start_of(j):
+        return pl.multiple_of(flip(j) * rows, rows)
+
+    def behind(s):
+        source = me_row - s
+        return jnp.where(source < 0, source + row_devs, source)
+
+    for s in range(row_devs):
+        for j in range(head_devs):
+            x[behind(s), pl.ds(start_of(j), rows), :] = pieces[s * head_devs + j][...]
+    squares = jnp.zeros((tall, 1), f32)
+    for z in range(row_devs):
+        value = x[z].astype(f32)
+        squares = squares + jnp.sum(value * value, axis=1, keepdims=True)
+    inverse = lax.rsqrt(squares / (row_devs * cols) + norm_eps)
+    for z in range(row_devs):
+        x[z] = (x[z].astype(f32) * inverse * gain_ref[:, z * cols : (z + 1) * cols]).astype(bf16)
+
+    for j in range(steps):
+        for copy in gate_copy(j):
+            copy.wait()
+        cut = slice(j * hidden_tile, (j + 1) * hidden_tile)
+        gate = jnp.zeros((tall, hidden_tile), f32)
+        up = jnp.zeros((tall, hidden_tile), f32)
+        for z in range(row_devs):
+            gate = gate + mxu(x[z], gate_w[z * cols : (z + 1) * cols, cut], (1, 0))
+            up = up + mxu(x[z], up_w[z * cols : (z + 1) * cols, cut], (1, 0))
+        inner[:, cut] = (gate / (1.0 + jnp.exp(-gate)) * up).astype(bf16)
+
+    for i in range(row_devs):
+        down_copy(i).wait()
+
+        @pl.loop(0, cols // hidden_tile)
+        def _(t):
+            cut = pl.ds(pl.multiple_of(t * hidden_tile, hidden_tile), hidden_tile)
+            y[i, :, cut] = mxu(inner[...], down_w[i, :, cut], (1, 0))
+
+    for i in range(row_devs):
+        target = me_row + i
+        target = jnp.where(target >= row_devs, target - row_devs, target)
+        for j in range(head_devs):
+            value = y[target, pl.ds(start_of(j), rows), :]
+            half = slice((j // 2) * rows, (j // 2 + 1) * rows)
+            if j % 2 == 0:
+                keep_refs[i][half, :] = value
+            else:
+                send_refs[i][half, :] = value.astype(bf16)
+
+
+def swiglu(at, pieces, gain, w_gate, w_up, w_down, row_devs, head_devs):
+    rows, cols = pieces[0].shape
+    tall = rows * head_devs
+    width, hidden = w_gate.shape
+    half = rows * head_devs // 2
+    steps = hidden // hidden_tile
+    got = pl.pallas_call(
+        functools.partial(swiglu_kernel, row_devs, head_devs),
+        out_shape=[jax.ShapeDtypeStruct((half, cols), f32)] * row_devs
+        + [jax.ShapeDtypeStruct((half, cols), bf16)] * row_devs,
+        in_specs=[smem(), vmem()] + [vmem()] * len(pieces) + [hbm()] * 3,
+        out_specs=[vmem()] * (2 * row_devs),
+        scratch_shapes=[
+            pltpu.VMEM((row_devs, tall, cols), bf16),
+            pltpu.VMEM((width, hidden), bf16),
+            pltpu.VMEM((width, hidden), bf16),
+            pltpu.VMEM((row_devs, hidden, cols), bf16),
+            pltpu.VMEM((tall, hidden), bf16),
+            pltpu.VMEM((row_devs, tall, cols), f32),
+            pltpu.SemaphoreType.DMA((steps,)),
+            pltpu.SemaphoreType.DMA((steps,)),
+            pltpu.SemaphoreType.DMA((row_devs,)),
+        ],
+        compiler_params=pltpu.CompilerParams(vmem_limit_bytes=52 * mib),
+        name="swiglu",
+    )(at, gain.reshape(1, width), *pieces, w_gate, w_up, w_down)
+    return got[:row_devs], got[row_devs:]
+
+
 def shift(x, axis, step):
     n = lax.axis_size(axis)
     return lax.ppermute(x, axis, [(i, (i + step) % n) for i in range(n)])
+
+
+def swap(x, axis, flip):
+    return lax.ppermute(x, axis, [(i, i ^ flip) for i in range(lax.axis_size(axis))])
+
+
+def feed_forward(at, hidden_state, norm_gain, w_gate, w_up, w_down):
+    row_devs = lax.axis_size("rows")
+    head_devs = lax.axis_size("heads")
+    rows = hidden_state.shape[0]
+    pieces = []
+    for s in range(row_devs):
+        piece = shift(hidden_state, "rows", s) if s else hidden_state
+        across = swap(piece, "heads", 2)
+        pieces += [piece, swap(piece, "heads", 1), across, swap(across, "heads", 1)]
+    keeps, sends = swiglu(at, pieces, norm_gain, w_gate, w_up, w_down, row_devs, head_devs)
+    total = hidden_state.astype(f32)
+    order = sorted(range(row_devs), key=lambda i: (i == 0, abs(2 * i - row_devs)))
+    for i in order:
+        pair = keeps[i] + swap(sends[i], "heads", 1).astype(f32)
+        part = pair[:rows] + swap(pair[rows:].astype(bf16), "heads", 2).astype(f32)
+        total = total + (shift(part.astype(bf16), "rows", i).astype(f32) if i else part)
+    return total.astype(bf16)
+
+
+def feed_forward_gathered(hidden_state, norm_gain, w_gate, w_up, w_down):
+    model_width = norm_gain.shape[0]
+    full_rows = lax.all_gather(hidden_state, "rows", axis=1, tiled=True)
+    every = lax.all_gather(full_rows, "heads", axis=0, tiled=True).astype(f32)
+    totals = jnp.sum(every * every, axis=1)
+    normed = (every * lax.rsqrt(totals / model_width + norm_eps)[:, None] * norm_gain).astype(bf16)
+    gate = jnp.dot(normed, w_gate, preferred_element_type=f32)
+    up = jnp.dot(normed, w_up, preferred_element_type=f32)
+    inner = (jax.nn.silu(gate) * up).astype(bf16)
+    partial_sum = jnp.dot(inner, w_down, preferred_element_type=f32).astype(bf16)
+    section = lax.psum_scatter(partial_sum, "heads", scatter_dimension=0, tiled=True)
+    ffn = lax.psum_scatter(section, "rows", scatter_dimension=1, tiled=True)
+    return (hidden_state.astype(f32) + ffn.astype(f32)).astype(bf16)
 
 
 def shards(
@@ -310,22 +462,9 @@
         attn_out = attn_out + shift(others[s - 1], "heads", s).astype(f32)
     hidden_state = (resid.astype(f32) + attn_out).astype(bf16)
 
-    as_float = hidden_state.astype(f32)
-    cols_dev = hidden_state.shape[1]
-    model_width = cols_dev * row_devs
-    full_rows = lax.all_gather(hidden_state, "rows", axis=1, tiled=True)
-    piece_rows = lax.all_gather(full_rows, "heads", axis=0, tiled=True).astype(f32)
-    totals = jnp.sum(piece_rows * piece_rows, axis=1)
-    piece_rows = (
-        piece_rows * lax.rsqrt(totals / model_width + norm_eps)[:, None] * norm_gain
-    ).astype(bf16)
-    gate_proj = jnp.dot(piece_rows, w_gate, preferred_element_type=f32)
-    up_proj = jnp.dot(piece_rows, w_up, preferred_element_type=f32)
-    inner_act = (jax.nn.silu(gate_proj) * up_proj).astype(bf16)
-    partial_sum = jnp.dot(inner_act, w_down, preferred_element_type=f32)
-    section_sum = lax.psum_scatter(partial_sum.astype(bf16), "heads", scatter_dimension=0, tiled=True)
-    ffn_out = lax.psum_scatter(section_sum, "rows", scatter_dimension=1, tiled=True).astype(f32)
-    return (as_float + ffn_out).astype(bf16)
+    if head_devs == 4 and hidden_state.shape[1] % hidden_tile == 0:
+        return feed_forward(at, hidden_state, norm_gain, w_gate, w_up, w_down)
+    return feed_forward_gathered(hidden_state, norm_gain, w_gate, w_up, w_down)
 
 
 def solution(mesh):

time: 175 us -> 116 us (0.66)
  waiting for transfers between devices: 87.1 us -> 31.3 us
  starting transfers between devices: 17.4 us -> 37.4 us
  Pallas kernels: 14.8 us -> 34.6 us
  matrix products: 17.3 us -> 0.86 us
  blocking collectives: 15.7 us -> 0 us
  between operations: 13.2 us -> 0.19 us
    reduce_scatter x2 -> x0, waiting for transfers between devices: 49.1 us -> none  [the longest x1 26.6 us: shards(): lax.psum_scatter(partial_sum.astype(bf16), 'heads', scatter_dimension=0,...]
    dot_general x2 -> x0, matrix products: 17.1 us -> none  [the longest x1 11.1 us: shards(): partial_sum = jnp.dot(inner_act, w_down, preferred_element_type=f32)]
    pallas_call x0 -> x1, Pallas kernels: none -> 17.1 us  [swiglu(): pl.pallas_call(functools.partial(swiglu_kernel, row_devs, head_devs), out...]
    all_gather x1 -> x0, blocking collectives: 15.7 us -> none  [shards(): full_rows = lax.all_gather(hidden_state, 'rows', axis=1, tiled=True)]
    all_gather x1 -> x0, waiting for transfers between devices: 15.7 us -> none  [shards(): lax.all_gather(full_rows, 'heads', axis=0, tiled=True).astype(f32)]
    ppermute x0 -> x20, starting transfers between devices: none -> 13.1 us  [swap(): lax.ppermute(x, axis, [(i, i ^ flip) for i in range(lax.axis_size(axis))])]
    ppermute x12 -> x18, starting transfers between devices: 17.3 us -> 24.3 us  [shift(): return lax.ppermute(x, axis, [(i, (i + step) % n) for i in range(n)])]
    ppermute x0 -> x20, waiting for transfers between devices: none -> 4.72 us  [swap(): lax.ppermute(x, axis, [(i, i ^ flip) for i in range(lax.axis_size(axis))])]
  transfers between devices with their start and end apart: 15 -> 38, of which waited for: 12 -> 17; matrix products, arithmetic and copies ran while one was open for 0% -> 4% of each run, Pallas kernels for 0% -> 0%
where the time goes in v2:
time: 116 us
  starting transfers between devices  37.4 us (32%)
  Pallas kernels  34.6 us (30%)
  waiting for transfers between devices  31.3 us (27%)
  local copies, waits for them, and re-layouts  5.63 us (5%)
  other arithmetic  5.46 us (5%)
    ppermute x18, waiting for transfers between devices, shift(): return lax.ppermute(x, axis, [(i, (i + step) % n) for i in range(n)])  26.6 us
    ppermute x18, starting transfers between devices, shift(): return lax.ppermute(x, axis, [(i, (i + step) % n) for i in range(n)])  24.3 us
    pallas_call x1, Pallas kernels, swiglu(): pl.pallas_call(functools.partial(swiglu_kernel, row_devs, head_devs), out...  17.1 us
    ppermute x20, starting transfers between devices, swap(): lax.ppermute(x, axis, [(i, i ^ flip) for i in range(lax.axis_size(axis))])  13.1 us
    pallas_call x1, Pallas kernels, attend(): pl.pallas_call(functools.partial(attend_kernel, count, listed, group, min...  12.6 us
    unnamed x16, local copies, waits for them, and re-layouts  5.58 us
    ppermute x20, waiting for transfers between devices, swap(): lax.ppermute(x, axis, [(i, i ^ flip) for i in range(lax.axis_size(axis))])  4.72 us
    add x4, other arithmetic, feed_forward(): pair = keeps[i] + swap(sends[i], 'heads', 1).astype(f32)  4.04 us
  transfers between devices with their start and end apart: 38, of which 17 were waited for; matrix products, arithmetic and copies ran while one was open for 4% of the time, Pallas kernels for 0%

profile of v2, /device:TPU:0, one launch (start us, length us, event | category | flops | bytes accessed | tf_op | source)
XLA Modules:
  0.0 115.5 jit_solution(13009346544055161672)
XLA Ops:
  0.6 2.2 %dispatch.1 = (bf16[32,64]{1,0:T(8,128)(2,1)}, bf16[16,2176]{1,0:T(8,128)(2,1)}, bf16[16,2176]{1,0:T(8,128)(2,1)}, bf16[16,2176]{1,0:T(8,128)(2,1)}, bf16[16,2176]{1,0:T(8,128)(2,1)}) custom-call(s32[2]{0:T(128)} %pad_add_fusion.me_ref.at_ref, s32[32,32]{1,0:T(8,128)} %ids_ref.1, s32[1,32]{1,0:T(1,128)} %bitcast.6, bf16[32,2048]{1,0:T(8,128)(2,1)} %q_ref.1), custom_call_target="tpu_custom_call" | custom-call | tf_op jit(solution)/shard_map/dispatch/pallas_call | solution.py:70
  2.9 3.0 %collective-permute-start = (bf16[16,2176]{1,0:T(8,128)(2,1)}, bf16[16,2176]{1,0:T(8,128)(2,1)S(1)}, u32[]{:S(2)}, u32[]{:S(2)}) collective-permute-start(bf16[16,2176]{1,0:T(8,128)(2,1)} %get-tuple-element.28), channel_id=1, source_target_pairs={{0,4},{4,8},{8,12},{12,0},{1,5},{5,9},{9,13},{13,1},{2,6},{6,10},{... | collective-permute-start | bytes 208904 | tf_op jit(solution)/shard_map/ppermute | solution.py:396
  5.9 2.6 %collective-permute-start.1 = (bf16[16,2176]{1,0:T(8,128)(2,1)}, bf16[16,2176]{1,0:T(8,128)(2,1)S(1)}, u32[]{:S(2)}, u32[]{:S(2)}) collective-permute-start(bf16[16,2176]{1,0:T(8,128)(2,1)} %get-tuple-element.29), channel_id=1, source_target_pairs={{0,8},{4,12},{8,0},{12,4},{1,9},{5,13},{9,1},{13,5},{2,10},{6,14},... | collective-permute-start | bytes 208904 | tf_op jit(solution)/shard_map/ppermute | solution.py:396
  8.5 1.3 %collective-permute-start.2 = (bf16[16,2176]{1,0:T(8,128)(2,1)}, bf16[16,2176]{1,0:T(8,128)(2,1)S(1)}, u32[]{:S(2)}, u32[]{:S(2)}) collective-permute-start(bf16[16,2176]{1,0:T(8,128)(2,1)} %get-tuple-element.30), channel_id=1, source_target_pairs={{0,12},{4,0},{8,4},{12,8},{1,13},{5,1},{9,5},{13,9},{2,14},{6,2},{... | collective-permute-start | bytes 208904 | tf_op jit(solution)/shard_map/ppermute | solution.py:396
  10.7 2.7 %collective-permute-done.1.refs_2_ = bf16[16,2176]{1,0:T(8,128)(2,1)S(1)} collective-permute-done((bf16[16,2176]{1,0:T(8,128)(2,1)}, bf16[16,2176]{1,0:T(8,128)(2,1)S(1)}, u32[]{:S(2)}, u32[]{:S(2)}) %collective-permute-start.1) | collective-permute-done | bytes 69664 | tf_op jit(solution)/shard_map/ppermute | solution.py:396
  13.6 3.4 %copy-done = bf16[64,2,2,128,128]{4,3,2,1,0:T(8,128)(2,1)S(1)} copy-done((bf16[64,2,2,128,128]{4,3,2,1,0:T(8,128)(2,1)S(1)}, bf16[64,2,2,128,128]{4,3,2,1,0:T(8,128)(2,1)}, u32[]{:S(2)}) %copy-start) | copy-done | bytes 8388632
  18.5 12.6 %attend.1 = (bf16[16,2048]{1,0:T(8,128)(2,1)S(1)}, bf16[16,2048]{1,0:T(8,128)(2,1)S(1)}, bf16[16,2048]{1,0:T(8,128)(2,1)S(1)}, bf16[16,2048]{1,0:T(8,128)(2,1)S(1)}) custom-call(f32[2,2]{1,0:T(2,128)S(1)} %copy-done.6, bf16[64,2,2,128,128]{4,3,2,1,0:T(8,128)(2,1)S(1)} %copy-done, bf16[16,2176]{1,0:T(8,128)(2,1)S(1)} %copy-done.2, ...), custom_call_target="tpu_custom_call" | custom-call | tf_op jit(solution)/shard_map/attend/pallas_call | solution.py:212
  31.2 3.2 %collective-permute-start.4 = (bf16[16,2048]{1,0:T(8,128)(2,1)S(1)}, bf16[16,2048]{1,0:T(8,128)(2,1)S(1)}, u32[]{:S(2)}, u32[]{:S(2)}) collective-permute-start(bf16[16,2048]{1,0:T(8,128)(2,1)S(1)} %get-tuple-element.33), channel_id=1, source_target_pairs={{0,8},{4,12},{8,0},{12,4},{1,9},{5,13},{9,1},{13,5},{2,10},{6,14},... | collective-permute-start | bytes 196616 | tf_op jit(solution)/shard_map/ppermute | solution.py:396
  35.5 5.2 %collective-permute-done.4 = bf16[16,2048]{1,0:T(8,128)(2,1)S(1)} collective-permute-done((bf16[16,2048]{1,0:T(8,128)(2,1)S(1)}, bf16[16,2048]{1,0:T(8,128)(2,1)S(1)}, u32[]{:S(2)}, u32[]{:S(2)}) %collective-permute-start.4) | collective-permute-done | bytes 65568 | tf_op jit(solution)/shard_map/ppermute | solution.py:396
  42.2 1.4 %collective-permute-start.6 = (bf16[32,2048]{1,0:T(8,128)(2,1)S(1)}, bf16[32,2048]{1,0:T(8,128)(2,1)S(1)}, u32[]{:S(2)}, u32[]{:S(2)}) collective-permute-start(bf16[32,2048]{1,0:T(8,128)(2,1)S(1)} %convolution_convert_fusion.refs_0_), channel_id=1, source_target_pairs={{0,4},{4,8},{8,12},{12,0},{1,5},{5,9},{9,13},{13,1},{2,6},{6,10},{... | collective-permute-start | bytes 393224 | tf_op jit(solution)/shard_map/ppermute | solution.py:396
  43.6 3.4 %collective-permute-done.8.refs_3_ = bf16[32,2048]{1,0:T(8,128)(2,1)S(1)} collective-permute-done((bf16[32,2048]{1,0:T(8,128)(2,1)S(1)}, bf16[32,2048]{1,0:T(8,128)(2,1)S(1)}, u32[]{:S(2)}, u32[]{:S(2)}) %collective-permute-start.8) | collective-permute-done | bytes 131104 | tf_op jit(solution)/shard_map/ppermute | solution.py:396
  47.0 6.2 %collective-permute-done.7.refs_2_ = bf16[32,2048]{1,0:T(8,128)(2,1)S(1)} collective-permute-done((bf16[32,2048]{1,0:T(8,128)(2,1)S(1)}, bf16[32,2048]{1,0:T(8,128)(2,1)S(1)}, u32[]{:S(2)}, u32[]{:S(2)}) %collective-permute-start.7) | collective-permute-done | bytes 131104 | tf_op jit(solution)/shard_map/ppermute | solution.py:396
  53.8 2.7 %project.1 = (f32[32,1280]{1,0:T(8,128)S(1)}, bf16[32,1280]{1,0:T(8,128)(2,1)S(1)}, bf16[32,1280]{1,0:T(8,128)(2,1)S(1)}, bf16[32,1280]{1,0:T(8,128)(2,1)S(1)}) custom-call(s32[2]{0:T(128)S(1)} %copy-done.4, bf16[32,2048]{1,0:T(8,128)(2,1)S(1)} %convolution_convert_fusion.refs_0_, bf16[32,2048]{1,0:T(8,128)(2,1)S(1)} %collective-permute-done.6.refs_1_, ...), custom_call_target="tpu_custom_call" | custom-call | tf_op jit(solution)/shard_map/project/pallas_call | solution.py:266
  57.9 1.4 %collective-permute-start.11 = (bf16[32,1280]{1,0:T(8,128)(2,1)S(1)}, bf16[32,1280]{1,0:T(8,128)(2,1)S(1)}, u32[]{:S(2)}, u32[]{:S(2)}) collective-permute-start(bf16[32,1280]{1,0:T(8,128)(2,1)S(1)} %get-tuple-element.38), channel_id=1, source_target_pairs={{0,3},{1,0},{2,1},{3,2},{4,7},{5,4},{6,5},{7,6},{8,11},{9,8},{10,9... | collective-permute-start | bytes 245768 | tf_op jit(solution)/shard_map/ppermute | solution.py:396
  59.3 1.4 %collective-permute-done.9 = bf16[32,1280]{1,0:T(8,128)(2,1)S(1)} collective-permute-done((bf16[32,1280]{1,0:T(8,128)(2,1)S(1)}, bf16[32,1280]{1,0:T(8,128)(2,1)S(1)}, u32[]{:S(2)}, u32[]{:S(2)}) %collective-permute-start.9) | collective-permute-done | bytes 81952 | tf_op jit(solution)/shard_map/ppermute | solution.py:396
  62.0 1.8 %collective-permute-start.19 = (bf16[32,1280]{1,0:T(8,128)(2,1)S(1)}, bf16[32,1280]{1,0:T(8,128)(2,1)S(1)}, u32[]{:S(2)}, u32[]{:S(2)}) collective-permute-start(bf16[32,1280]{1,0:T(8,128)(2,1)S(1)} %add_convert_fusion.refs_0_), channel_id=1, source_target_pairs={{0,8},{4,12},{8,0},{12,4},{1,9},{5,13},{9,1},{13,5},{2,10},{6,14},... | collective-permute-start | bytes 245768 | tf_op jit(solution)/shard_map/ppermute | solution.py:396
  63.9 1.9 %collective-permute-start.15 = (bf16[32,1280]{1,0:T(8,128)(2,1)S(1)}, bf16[32,1280]{1,0:T(8,128)(2,1)S(1)}, u32[]{:S(2)}, u32[]{:S(2)}) collective-permute-start(bf16[32,1280]{1,0:T(8,128)(2,1)S(1)} %add_convert_fusion.refs_0_), channel_id=1, source_target_pairs={{0,4},{4,8},{8,12},{12,0},{1,5},{5,9},{9,13},{13,1},{2,6},{6,10},{... | collective-permute-start | bytes 245768 | tf_op jit(solution)/shard_map/ppermute | solution.py:396
  67.0 1.8 %collective-permute-done.23.refs_12_ = bf16[32,1280]{1,0:T(8,128)(2,1)S(1)} collective-permute-done((bf16[32,1280]{1,0:T(8,128)(2,1)S(1)}, bf16[32,1280]{1,0:T(8,128)(2,1)S(1)}, u32[]{:S(2)}, u32[]{:S(2)}) %collective-permute-start.23) | collective-permute-done | bytes 81952 | tf_op jit(solution)/shard_map/ppermute | solution.py:396
  70.1 2.1 %collective-permute-start.24 = (bf16[32,1280]{1,0:T(8,128)(2,1)S(1)}, bf16[32,1280]{1,0:T(8,128)(2,1)S(1)}, u32[]{:S(2)}, u32[]{:S(2)}) collective-permute-start(bf16[32,1280]{1,0:T(8,128)(2,1)S(1)} %collective-permute-done.23.refs_12_), channel_id=1, source_target_pairs={{0,1},{1,0},{2,3},{3,2},{4,5},{5,4},{6,7},{7,6},{8,9},{9,8},{10,11... | collective-permute-start | bytes 245768 | tf_op jit(solution)/shard_map/ppermute | solution.py:400
  74.9 2.0 %collective-permute-done.21.refs_10_ = bf16[32,1280]{1,0:T(8,128)(2,1)S(1)} collective-permute-done((bf16[32,1280]{1,0:T(8,128)(2,1)S(1)}, bf16[32,1280]{1,0:T(8,128)(2,1)S(1)}, u32[]{:S(2)}, u32[]{:S(2)}) %collective-permute-start.21) | collective-permute-done | bytes 81952 | tf_op jit(solution)/shard_map/ppermute | solution.py:400
  79.7 17.1 %swiglu.1 = (f32[64,1280]{1,0:T(8,128)}, f32[64,1280]{1,0:T(8,128)}, f32[64,1280]{1,0:T(8,128)}, f32[64,1280]{1,0:T(8,128)}, bf16[64,1280]{1,0:T(8,128)(2,1)S(1)...) custom-call(s32[2]{0:T(128)S(1)} %copy-done.5, f32[1,5120]{1,0:T(1,128)S(1)} %bitcast.5, ...), custom_call_target="tpu_custom_call" | custom-call | tf_op jit(solution)/shard_map/swiglu/pallas_call | solution.py:371
  106.7 1.5 %collective-permute-start.29 = (bf16[32,1280]{1,0:T(8,128)(2,1)S(1)}, bf16[32,1280]{1,0:T(8,128)(2,1)S(1)}, u32[]{:S(2)}, u32[]{:S(2)}) collective-permute-start(bf16[32,1280]{1,0:T(8,128)(2,1)S(1)} %fusion.11), channel_id=1, source_target_pairs={{0,8},{4,12},{8,0},{12,4},{1,9},{5,13},{9,1},{13,5},{2,10},{6,14},... | collective-permute-start | bytes 245768 | tf_op jit(solution)/shard_map/ppermute | solution.py:396
  108.5 3.7 %collective-permute-start.35 = (bf16[32,1280]{1,0:T(8,128)(2,1)S(1)}, bf16[32,1280]{1,0:T(8,128)(2,1)S(1)}, u32[]{:S(2)}, u32[]{:S(2)}) collective-permute-start(bf16[32,1280]{1,0:T(8,128)(2,1)S(1)} %fusion.9), channel_id=1, source_target_pairs={{0,12},{4,0},{8,4},{12,8},{1,13},{5,1},{9,5},{13,9},{2,14},{6,2},{... | collective-permute-start | bytes 245768 | tf_op jit(solution)/shard_map/ppermute | solution.py:396
  112.2 1.6 %collective-permute-done.29 = bf16[32,1280]{1,0:T(8,128)(2,1)S(1)} collective-permute-done((bf16[32,1280]{1,0:T(8,128)(2,1)S(1)}, bf16[32,1280]{1,0:T(8,128)(2,1)S(1)}, u32[]{:S(2)}, u32[]{:S(2)}) %collective-permute-start.29) | collective-permute-done | bytes 81952 | tf_op jit(solution)/shard_map/ppermute | solution.py:396
  (87 shorter events, 29.2 us)
Async XLA Ops:
  2.9 7.9 %collective-permute-start = (bf16[16,2176]{1,0:T(8,128)(2,1)}, bf16[16,2176]{1,0:T(8,128)(2,1)S(1)}, u32[]{:S(2)}, u32[]{:S(2)}) collective-permute-start(bf16[16,2176]{1,0:T(8,128)(2,1)} %get-tuple-element.28), channel_id=1, source_target_pairs={{0,4},{4,8},{8,12},{12,0},{1,5},{5,9},{9,13},{13,1},{2,6},{6,10},{... | collective-permute-start | bytes 208904 | tf_op jit(solution)/shard_map/ppermute | solution.py:396
  5.9 7.5 %collective-permute-start.1 = (bf16[16,2176]{1,0:T(8,128)(2,1)}, bf16[16,2176]{1,0:T(8,128)(2,1)S(1)}, u32[]{:S(2)}, u32[]{:S(2)}) collective-permute-start(bf16[16,2176]{1,0:T(8,128)(2,1)} %get-tuple-element.29), channel_id=1, source_target_pairs={{0,8},{4,12},{8,0},{12,4},{1,9},{5,13},{9,1},{13,5},{2,10},{6,14},... | collective-permute-start | bytes 208904 | tf_op jit(solution)/shard_map/ppermute | solution.py:396
  8.5 5.1 %collective-permute-start.2 = (bf16[16,2176]{1,0:T(8,128)(2,1)}, bf16[16,2176]{1,0:T(8,128)(2,1)S(1)}, u32[]{:S(2)}, u32[]{:S(2)}) collective-permute-start(bf16[16,2176]{1,0:T(8,128)(2,1)} %get-tuple-element.30), channel_id=1, source_target_pairs={{0,12},{4,0},{8,4},{12,8},{1,13},{5,1},{9,5},{13,9},{2,14},{6,2},{... | collective-permute-start | bytes 208904 | tf_op jit(solution)/shard_map/ppermute | solution.py:396
  31.2 9.4 %collective-permute-start.4 = (bf16[16,2048]{1,0:T(8,128)(2,1)S(1)}, bf16[16,2048]{1,0:T(8,128)(2,1)S(1)}, u32[]{:S(2)}, u32[]{:S(2)}) collective-permute-start(bf16[16,2048]{1,0:T(8,128)(2,1)S(1)} %get-tuple-element.33), channel_id=1, source_target_pairs={{0,8},{4,12},{8,0},{12,4},{1,9},{5,13},{9,1},{13,5},{2,10},{6,14},... | collective-permute-start | bytes 196616 | tf_op jit(solution)/shard_map/ppermute | solution.py:396
  34.4 6.2 %collective-permute-start.5 = (bf16[16,2048]{1,0:T(8,128)(2,1)S(1)}, bf16[16,2048]{1,0:T(8,128)(2,1)S(1)}, u32[]{:S(2)}, u32[]{:S(2)}) collective-permute-start(bf16[16,2048]{1,0:T(8,128)(2,1)S(1)} %get-tuple-element.34), channel_id=1, source_target_pairs={{0,4},{4,8},{8,12},{12,0},{1,5},{5,9},{9,13},{13,1},{2,6},{6,10},{... | collective-permute-start | bytes 196616 | tf_op jit(solution)/shard_map/ppermute | solution.py:396
  41.5 5.5 %collective-permute-start.8 = (bf16[32,2048]{1,0:T(8,128)(2,1)S(1)}, bf16[32,2048]{1,0:T(8,128)(2,1)S(1)}, u32[]{:S(2)}, u32[]{:S(2)}) collective-permute-start(bf16[32,2048]{1,0:T(8,128)(2,1)S(1)} %convolution_convert_fusion.refs_0_), channel_id=1, source_target_pairs={{0,12},{4,0},{8,4},{12,8},{1,13},{5,1},{9,5},{13,9},{2,14},{6,2},{... | collective-permute-start | bytes 393224 | tf_op jit(solution)/shard_map/ppermute | solution.py:396
  41.6 11.6 %collective-permute-start.7 = (bf16[32,2048]{1,0:T(8,128)(2,1)S(1)}, bf16[32,2048]{1,0:T(8,128)(2,1)S(1)}, u32[]{:S(2)}, u32[]{:S(2)}) collective-permute-start(bf16[32,2048]{1,0:T(8,128)(2,1)S(1)} %convolution_convert_fusion.refs_0_), channel_id=1, source_target_pairs={{0,8},{4,12},{8,0},{12,4},{1,9},{5,13},{9,1},{13,5},{2,10},{6,14},... | collective-permute-start | bytes 393224 | tf_op jit(solution)/shard_map/ppermute | solution.py:396
  42.2 11.0 %collective-permute-start.6 = (bf16[32,2048]{1,0:T(8,128)(2,1)S(1)}, bf16[32,2048]{1,0:T(8,128)(2,1)S(1)}, u32[]{:S(2)}, u32[]{:S(2)}) collective-permute-start(bf16[32,2048]{1,0:T(8,128)(2,1)S(1)} %convolution_convert_fusion.refs_0_), channel_id=1, source_target_pairs={{0,4},{4,8},{8,12},{12,0},{1,5},{5,9},{9,13},{13,1},{2,6},{6,10},{... | collective-permute-start | bytes 393224 | tf_op jit(solution)/shard_map/ppermute | solution.py:396
  56.6 5.3 %collective-permute-start.10 = (bf16[32,1280]{1,0:T(8,128)(2,1)S(1)}, bf16[32,1280]{1,0:T(8,128)(2,1)S(1)}, u32[]{:S(2)}, u32[]{:S(2)}) collective-permute-start(bf16[32,1280]{1,0:T(8,128)(2,1)S(1)} %get-tuple-element.37), channel_id=1, source_target_pairs={{0,2},{1,3},{2,0},{3,1},{4,6},{5,7},{6,4},{7,5},{8,10},{9,11},{10,... | collective-permute-start | bytes 245768 | tf_op jit(solution)/shard_map/ppermute | solution.py:396
  62.0 6.9 %collective-permute-start.23 = (bf16[32,1280]{1,0:T(8,128)(2,1)S(1)}, bf16[32,1280]{1,0:T(8,128)(2,1)S(1)}, u32[]{:S(2)}, u32[]{:S(2)}) collective-permute-start(bf16[32,1280]{1,0:T(8,128)(2,1)S(1)} %add_convert_fusion.refs_0_), channel_id=1, source_target_pairs={{0,12},{4,0},{8,4},{12,8},{1,13},{5,1},{9,5},{13,9},{2,14},{6,2},{... | collective-permute-start | bytes 245768 | tf_op jit(solution)/shard_map/ppermute | solution.py:396
  62.0 8.1 %collective-permute-start.19 = (bf16[32,1280]{1,0:T(8,128)(2,1)S(1)}, bf16[32,1280]{1,0:T(8,128)(2,1)S(1)}, u32[]{:S(2)}, u32[]{:S(2)}) collective-permute-start(bf16[32,1280]{1,0:T(8,128)(2,1)S(1)} %add_convert_fusion.refs_0_), channel_id=1, source_target_pairs={{0,8},{4,12},{8,0},{12,4},{1,9},{5,13},{9,1},{13,5},{2,10},{6,14},... | collective-permute-start | bytes 245768 | tf_op jit(solution)/shard_map/ppermute | solution.py:396
  63.9 8.4 %collective-permute-start.15 = (bf16[32,1280]{1,0:T(8,128)(2,1)S(1)}, bf16[32,1280]{1,0:T(8,128)(2,1)S(1)}, u32[]{:S(2)}, u32[]{:S(2)}) collective-permute-start(bf16[32,1280]{1,0:T(8,128)(2,1)S(1)} %add_convert_fusion.refs_0_), channel_id=1, source_target_pairs={{0,4},{4,8},{8,12},{12,0},{1,5},{5,9},{9,13},{13,1},{2,6},{6,10},{... | collective-permute-start | bytes 245768 | tf_op jit(solution)/shard_map/ppermute | solution.py:396
  65.8 7.6 %collective-permute-start.13 = (bf16[32,1280]{1,0:T(8,128)(2,1)S(1)}, bf16[32,1280]{1,0:T(8,128)(2,1)S(1)}, u32[]{:S(2)}, u32[]{:S(2)}) collective-permute-start(bf16[32,1280]{1,0:T(8,128)(2,1)S(1)} %add_convert_fusion.refs_0_), channel_id=1, source_target_pairs={{0,2},{1,3},{2,0},{3,1},{4,6},{5,7},{6,4},{7,5},{8,10},{9,11},{10,... | collective-permute-start | bytes 245768 | tf_op jit(solution)/shard_map/ppermute | solution.py:400
  67.0 6.4 %collective-permute-start.12 = (bf16[32,1280]{1,0:T(8,128)(2,1)S(1)}, bf16[32,1280]{1,0:T(8,128)(2,1)S(1)}, u32[]{:S(2)}, u32[]{:S(2)}) collective-permute-start(bf16[32,1280]{1,0:T(8,128)(2,1)S(1)} %add_convert_fusion.refs_0_), channel_id=1, source_target_pairs={{0,1},{1,0},{2,3},{3,2},{4,5},{5,4},{6,7},{7,6},{8,9},{9,8},{10,11... | collective-permute-start | bytes 245768 | tf_op jit(solution)/shard_map/ppermute | solution.py:400
  68.9 5.5 %collective-permute-start.25 = (bf16[32,1280]{1,0:T(8,128)(2,1)S(1)}, bf16[32,1280]{1,0:T(8,128)(2,1)S(1)}, u32[]{:S(2)}, u32[]{:S(2)}) collective-permute-start(bf16[32,1280]{1,0:T(8,128)(2,1)S(1)} %collective-permute-done.23.refs_12_), channel_id=1, source_target_pairs={{0,2},{1,3},{2,0},{3,1},{4,6},{5,7},{6,4},{7,5},{8,10},{9,11},{10,... | collective-permute-start | bytes 245768 | tf_op jit(solution)/shard_map/ppermute | solution.py:400
  97.4 5.1 %collective-permute-start.33 = (bf16[64,1280]{1,0:T(8,128)(2,1)S(1)}, bf16[64,1280]{1,0:T(8,128)(2,1)S(1)}, u32[]{:S(2)}, u32[]{:S(2)}) collective-permute-start(bf16[64,1280]{1,0:T(8,128)(2,1)S(1)} %get-tuple-element.44), channel_id=1, source_target_pairs={{0,1},{1,0},{2,3},{3,2},{4,5},{5,4},{6,7},{7,6},{8,9},{9,8},{10,11... | collective-permute-start | bytes 491528 | tf_op jit(solution)/shard_map/ppermute | solution.py:400
  97.5 7.3 %collective-permute-start.36 = (bf16[64,1280]{1,0:T(8,128)(2,1)S(1)}, bf16[64,1280]{1,0:T(8,128)(2,1)S(1)}, u32[]{:S(2)}, u32[]{:S(2)}) collective-permute-start(bf16[64,1280]{1,0:T(8,128)(2,1)S(1)} %get-tuple-element.46), channel_id=1, source_target_pairs={{0,1},{1,0},{2,3},{3,2},{4,5},{5,4},{6,7},{7,6},{8,9},{9,8},{10,11... | collective-permute-start | bytes 491528 | tf_op jit(solution)/shard_map/ppermute | solution.py:400
  99.3 7.4 %collective-permute-start.28 = (bf16[32,1280]{1,0:T(8,128)(2,1)S(1)}, bf16[32,1280]{1,0:T(8,128)(2,1)S(1)}, u32[]{:S(2)}, u32[]{:S(2)}) collective-permute-start(bf16[32,1280]{1,0:T(8,128)(2,1)S(1)} %slice.65), channel_id=1, source_target_pairs={{0,2},{1,3},{2,0},{3,1},{4,6},{5,7},{6,4},{7,5},{8,10},{9,11},{10,... | collective-permute-start | bytes 245768 | tf_op jit(solution)/shard_map/ppermute | solution.py:400
  101.6 6.6 %collective-permute-start.31 = (bf16[32,1280]{1,0:T(8,128)(2,1)S(1)}, bf16[32,1280]{1,0:T(8,128)(2,1)S(1)}, u32[]{:S(2)}, u32[]{:S(2)}) collective-permute-start(bf16[32,1280]{1,0:T(8,128)(2,1)S(1)} %slice.64), channel_id=1, source_target_pairs={{0,2},{1,3},{2,0},{3,1},{4,6},{5,7},{6,4},{7,5},{8,10},{9,11},{10,... | collective-permute-start | bytes 245768 | tf_op jit(solution)/shard_map/ppermute | solution.py:400
  103.5 5.0 %collective-permute-start.34 = (bf16[32,1280]{1,0:T(8,128)(2,1)S(1)}, bf16[32,1280]{1,0:T(8,128)(2,1)S(1)}, u32[]{:S(2)}, u32[]{:S(2)}) collective-permute-start(bf16[32,1280]{1,0:T(8,128)(2,1)S(1)} %slice.63), channel_id=1, source_target_pairs={{0,2},{1,3},{2,0},{3,1},{4,6},{5,7},{6,4},{7,5},{8,10},{9,11},{10,... | collective-permute-start | bytes 245768 | tf_op jit(solution)/shard_map/ppermute | solution.py:400
  105.8 6.4 %collective-permute-start.37 = (bf16[32,1280]{1,0:T(8,128)(2,1)S(1)}, bf16[32,1280]{1,0:T(8,128)(2,1)S(1)}, u32[]{:S(2)}, u32[]{:S(2)}) collective-permute-start(bf16[32,1280]{1,0:T(8,128)(2,1)S(1)} %slice.62), channel_id=1, source_target_pairs={{0,2},{1,3},{2,0},{3,1},{4,6},{5,7},{6,4},{7,5},{8,10},{9,11},{10,... | collective-permute-start | bytes 245768 | tf_op jit(solution)/shard_map/ppermute | solution.py:400
  106.7 7.0 %collective-permute-start.29 = (bf16[32,1280]{1,0:T(8,128)(2,1)S(1)}, bf16[32,1280]{1,0:T(8,128)(2,1)S(1)}, u32[]{:S(2)}, u32[]{:S(2)}) collective-permute-start(bf16[32,1280]{1,0:T(8,128)(2,1)S(1)} %fusion.11), channel_id=1, source_target_pairs={{0,8},{4,12},{8,0},{12,4},{1,9},{5,13},{9,1},{13,5},{2,10},{6,14},... | collective-permute-start | bytes 245768 | tf_op jit(solution)/shard_map/ppermute | solution.py:396
  108.2 6.5 %collective-permute-start.32 = (bf16[32,1280]{1,0:T(8,128)(2,1)S(1)}, bf16[32,1280]{1,0:T(8,128)(2,1)S(1)}, u32[]{:S(2)}, u32[]{:S(2)}) collective-permute-start(bf16[32,1280]{1,0:T(8,128)(2,1)S(1)} %fusion.10), channel_id=1, source_target_pairs={{0,4},{4,8},{8,12},{12,0},{1,5},{5,9},{9,13},{13,1},{2,6},{6,10},{... | collective-permute-start | bytes 245768 | tf_op jit(solution)/shard_map/ppermute | solution.py:396
  108.5 6.3 %collective-permute-start.35 = (bf16[32,1280]{1,0:T(8,128)(2,1)S(1)}, bf16[32,1280]{1,0:T(8,128)(2,1)S(1)}, u32[]{:S(2)}, u32[]{:S(2)}) collective-permute-start(bf16[32,1280]{1,0:T(8,128)(2,1)S(1)} %fusion.9), channel_id=1, source_target_pairs={{0,12},{4,0},{8,4},{12,8},{1,13},{5,1},{9,5},{13,9},{2,14},{6,2},{... | collective-permute-start | bytes 245768 | tf_op jit(solution)/shard_map/ppermute | solution.py:396
  (22 other events, 308.3 us)

commit v3 on v2

--- a/solution.py
+++ b/solution.py
@@ -17,7 +17,11 @@
 
 vmem = functools.partial(pl.BlockSpec, memory_space=pltpu.VMEM)
 smem = functools.partial(pl.BlockSpec, memory_space=pltpu.SMEM)
-hbm = functools.partial(pl.BlockSpec, memory_space=pl.ANY)
+hbm = functools.partial(pl.BlockSpec, memory_space=pltpu.HBM)
+
+
+def stay(x):
+    return pltpu.with_memory_space_constraint(x, pltpu.HBM)
 
 
 def iota(shape, dim):
@@ -26,6 +30,31 @@
 
 def mxu(a, b, contract):
     return lax.dot_general(a, b, ((contract[:1], contract[1:]), ((), ())), preferred_element_type=f32)
+
+
+def fetch_kernel(count, after_ref, *refs):
+    sources, targets, sems = refs[:count], refs[count : 2 * count], refs[2 * count]
+    copies = [pltpu.make_async_copy(sources[i], targets[i], sems.at[i]) for i in range(count)]
+    for copy in copies:
+        copy.start()
+    for copy in copies:
+        copy.wait()
+
+
+def fetch(after, *arrays):
+    count = len(arrays)
+    return pl.pallas_call(
+        functools.partial(fetch_kernel, count),
+        out_shape=[pltpu.VMEM(a.shape, a.dtype) for a in arrays],
+        in_specs=[pl.BlockSpec(memory_space=pl.ANY)] + [hbm()] * count,
+        out_specs=[vmem()] * count,
+        scratch_shapes=[pltpu.SemaphoreType.DMA((count,))],
+        cost_estimate=pl.CostEstimate(
+            flops=0, bytes_accessed=sum(a.size * a.dtype.itemsize for a in arrays), transcendentals=0
+        ),
+        compiler_params=pltpu.CompilerParams(vmem_limit_bytes=1 * mib),
+        name="fetch",
+    )(after, *map(stay, arrays))
 
 
 def dispatch_kernel(blocks_dev, me_ref, ids_ref, len_ref, q_ref, place_ref, *send_refs):
@@ -72,6 +101,7 @@
         out_shape=outs,
         in_specs=[smem(), vmem(), vmem(), vmem()],
         out_specs=[vmem()] * (count + 1),
+        compiler_params=pltpu.CompilerParams(vmem_limit_bytes=8 * mib),
         name="dispatch",
     )(me, row_blocks, row_len.reshape(1, rows), queries)
     return got[0], got[1:]
@@ -80,17 +110,20 @@
 tile_rows = 16
 
 
-def attend_kernel(count, listed, group, step_blocks, scale_ref, kv_ref, *refs):
-    in_refs, out_refs = refs[:count], refs[count : 2 * count]
-    kv, qs, os, lens, ints, scalars, kv_sem, int_sem = refs[2 * count :]
+def attend_kernel(count, later, listed, group, step_blocks, scale_ref, kv, *refs):
+    in_refs, refs = refs[:count], refs[count:]
+    later_refs, refs = refs[:later], refs[later:]
+    out_refs, refs = refs[:count], refs[count:]
+    later_outs, refs = refs[:later], refs[later:]
+    qs, os, lens, ints, scalars, later_sems, int_sem = refs
+    copies = [pltpu.make_async_copy(later_refs[i], later_outs[i], later_sems.at[i]) for i in range(later)]
+    for copy in copies:
+        copy.start()
     slots = out_refs[0].shape[0]
     width = out_refs[0].shape[1]
     total = count * slots
     places = qs.shape[0]
     heads, tok, dim = kv.shape[2:]
-    kv_copy = pltpu.make_async_copy(kv_ref, kv, kv_sem)
-    kv_copy.start()
-
     meta = jnp.concatenate([r[:, width : width + lanes] for r in in_refs], axis=0).astype(f32)
     lane = iota((total, lanes), 1)
     length = jnp.sum(
@@ -141,7 +174,6 @@
     qs[...] = mxu(perm, queries, (1, 0)).astype(bf16)
     os[...] = jnp.zeros_like(os)
     int_copy.wait()
-    kv_copy.wait()
 
     tokens = step_blocks * tok
     tall = group * tile_rows
@@ -201,32 +233,35 @@
     out = mxu(perm, os[...], (0, 0)).astype(bf16)
     for s in range(count):
         out_refs[s][...] = out[s * slots : (s + 1) * slots]
-
-
-def attend(received, kv_codes, kv_scale, listed, group):
+    for copy in copies:
+        copy.wait()
+
+
+def attend(received, kv_codes, kv_scale, later, listed, group):
     count = len(received)
     slots, wide = received[0].shape
     width = wide - lanes
     total = count * slots
     places = total + tile_rows
-    return pl.pallas_call(
-        functools.partial(attend_kernel, count, listed, group, min(8, listed)),
-        out_shape=[jax.ShapeDtypeStruct((slots, width), bf16)] * count,
-        in_specs=[smem(), hbm()] + [vmem()] * count,
-        out_specs=[vmem()] * count,
+    got = pl.pallas_call(
+        functools.partial(attend_kernel, count, len(later), listed, group, min(8, listed)),
+        out_shape=[jax.ShapeDtypeStruct((slots, width), bf16)] * count
+        + [pltpu.VMEM(a.shape, a.dtype) for a in later],
+        in_specs=[smem()] + [vmem()] * (count + 1) + [hbm()] * len(later),
+        out_specs=[vmem()] * (count + len(later)),
         scratch_shapes=[
-            pltpu.VMEM(kv_codes.shape, bf16),
             pltpu.VMEM((places, width), bf16),
             pltpu.VMEM((places, width), bf16),
             pltpu.VMEM((places, lanes), jnp.int32),
             pltpu.VMEM((8, lanes), jnp.int32),
             pltpu.SMEM((8, lanes), jnp.int32),
-            pltpu.SemaphoreType.DMA,
+            pltpu.SemaphoreType.DMA((max(1, len(later)),)),
             pltpu.SemaphoreType.DMA,
         ],
-        compiler_params=pltpu.CompilerParams(vmem_limit_bytes=32 * mib),
+        compiler_params=pltpu.CompilerParams(vmem_limit_bytes=12 * mib),
         name="attend",
-    )(kv_scale, kv_codes, *received)
+    )(kv_scale, kv_codes, *received, *map(stay, later))
+    return got[:count], got[count:]
 
 
 def project_kernel(count, parts, at_ref, *refs):
@@ -271,7 +306,7 @@
         in_specs=[smem()] + [whole] * count + [pl.BlockSpec((depth, wide), lambda j: (0, j))],
         out_specs=[part] * parts,
         scratch_shapes=[pltpu.VMEM((tall, depth), bf16), pltpu.VMEM((tall, wide), f32)],
-        compiler_params=pltpu.CompilerParams(vmem_limit_bytes=32 * mib),
+        compiler_params=pltpu.CompilerParams(vmem_limit_bytes=12 * mib),
         name="project",
     )(at, *pieces, w_out)
     return got[0], got[1:]
@@ -285,28 +320,11 @@
     gate_ref, up_ref, down_ref = refs[row_devs * head_devs : row_devs * head_devs + 3]
     outs = refs[row_devs * head_devs + 3 :]
     keep_refs, send_refs = outs[:row_devs], outs[row_devs : 2 * row_devs]
-    x, gate_w, up_w, down_w, inner, y, gate_sem, up_sem, down_sem = outs[2 * row_devs :]
+    x, inner, y = outs[2 * row_devs :]
     rows, cols = pieces[0].shape
     tall = x.shape[1]
-    hidden = gate_w.shape[1]
+    hidden = gate_ref.shape[1]
     steps = hidden // hidden_tile
-
-    def gate_copy(j):
-        cut = pl.ds(j * hidden_tile, hidden_tile)
-        return (
-            pltpu.make_async_copy(gate_ref.at[:, cut], gate_w.at[:, cut], gate_sem.at[j]),
-            pltpu.make_async_copy(up_ref.at[:, cut], up_w.at[:, cut], up_sem.at[j]),
-        )
-
-    def down_copy(i):
-        cut = pl.ds(i * cols, cols)
-        return pltpu.make_async_copy(down_ref.at[:, cut], down_w.at[i], down_sem.at[i])
-
-    for j in range(steps):
-        for copy in gate_copy(j):
-            copy.start()
-    for i in range(row_devs):
-        down_copy(i).start()
 
     me_row, me_head = at_ref[0], at_ref[1]
 
@@ -332,23 +350,20 @@
         x[z] = (x[z].astype(f32) * inverse * gain_ref[:, z * cols : (z + 1) * cols]).astype(bf16)
 
     for j in range(steps):
-        for copy in gate_copy(j):
-            copy.wait()
         cut = slice(j * hidden_tile, (j + 1) * hidden_tile)
         gate = jnp.zeros((tall, hidden_tile), f32)
         up = jnp.zeros((tall, hidden_tile), f32)
         for z in range(row_devs):
-            gate = gate + mxu(x[z], gate_w[z * cols : (z + 1) * cols, cut], (1, 0))
-            up = up + mxu(x[z], up_w[z * cols : (z + 1) * cols, cut], (1, 0))
+            gate = gate + mxu(x[z], gate_ref[z * cols : (z + 1) * cols, cut], (1, 0))
+            up = up + mxu(x[z], up_ref[z * cols : (z + 1) * cols, cut], (1, 0))
         inner[:, cut] = (gate / (1.0 + jnp.exp(-gate)) * up).astype(bf16)
 
     for i in range(row_devs):
-        down_copy(i).wait()
-
         @pl.loop(0, cols // hidden_tile)
         def _(t):
             cut = pl.ds(pl.multiple_of(t * hidden_tile, hidden_tile), hidden_tile)
-            y[i, :, cut] = mxu(inner[...], down_w[i, :, cut], (1, 0))
+            from_cut = pl.ds(pl.multiple_of(i * cols + t * hidden_tile, hidden_tile), hidden_tile)
+            y[i, :, cut] = mxu(inner[...], down_ref[:, from_cut], (1, 0))
 
     for i in range(row_devs):
         target = me_row + i
@@ -367,25 +382,18 @@
     tall = rows * head_devs
     width, hidden = w_gate.shape
     half = rows * head_devs // 2
-    steps = hidden // hidden_tile
     got = pl.pallas_call(
         functools.partial(swiglu_kernel, row_devs, head_devs),
         out_shape=[jax.ShapeDtypeStruct((half, cols), f32)] * row_devs
         + [jax.ShapeDtypeStruct((half, cols), bf16)] * row_devs,
-        in_specs=[smem(), vmem()] + [vmem()] * len(pieces) + [hbm()] * 3,
+        in_specs=[smem(), vmem()] + [vmem()] * (len(pieces) + 3),
         out_specs=[vmem()] * (2 * row_devs),
         scratch_shapes=[
             pltpu.VMEM((row_devs, tall, cols), bf16),
-            pltpu.VMEM((width, hidden), bf16),
-            pltpu.VMEM((width, hidden), bf16),
-            pltpu.VMEM((row_devs, hidden, cols), bf16),
             pltpu.VMEM((tall, hidden), bf16),
             pltpu.VMEM((row_devs, tall, cols), f32),
-            pltpu.SemaphoreType.DMA((steps,)),
-            pltpu.SemaphoreType.DMA((steps,)),
-            pltpu.SemaphoreType.DMA((row_devs,)),
         ],
-        compiler_params=pltpu.CompilerParams(vmem_limit_bytes=52 * mib),
+        compiler_params=pltpu.CompilerParams(vmem_limit_bytes=12 * mib),
         name="swiglu",
     )(at, gain.reshape(1, width), *pieces, w_gate, w_up, w_down)
     return got[:row_devs], got[row_devs:]
@@ -452,10 +460,12 @@
 
     place, sends = dispatch(at, queries, row_blocks, row_len, row_devs, slots, blocks_dev)
     received = [sends[0]] + [shift(sends[s], "rows", s) for s in range(1, row_devs)]
-    results = attend(received, kv_codes, kv_scale, listed, group)
+    (kv_near,) = fetch(place, kv_codes)
+    results, (w_gate, w_out) = attend(received, kv_near, kv_scale, (w_gate, w_out), listed, group)
     back = [results[0]] + [shift(results[s], "rows", -s) for s in range(1, row_devs)]
     attended = jnp.dot(place, jnp.concatenate(back, axis=0), preferred_element_type=f32).astype(bf16)
     pieces = [attended] + [shift(attended, "rows", s) for s in range(1, row_devs)]
+    pieces, w_up, w_down = lax.optimization_barrier((pieces, *fetch(attended, w_up, w_down)))
     own, others = project(at, pieces, w_out, head_devs)
     attn_out = own
     for s in range(1, head_devs):

time: 116 us -> 100 us (0.86); the launches traced: 116 us -> 101 us
  waiting for transfers between devices: 31.3 us -> 22.8 us
  other arithmetic: 5.46 us -> 1.03 us
  local copies, waits for them, and re-layouts: 5.63 us -> 2.34 us
  Pallas kernels: 34.6 us -> 36.7 us
    ppermute x18, waiting for transfers between devices: 26.6 us -> 15.4 us  [shift(): return lax.ppermute(x, axis, [(i, (i + step) % n) for i in range(n)])]
    pallas_call x1 -> x3, Pallas kernels: 12.6 us -> 23.4 us  [the longest x1 13.1 us: attend(): pl.pallas_call(functools.partial(attend_kernel, count, len(later), listed...]
    pallas_call x1, Pallas kernels: 17.1 us -> 9.46 us  [swiglu(): pl.pallas_call(functools.partial(swiglu_kernel, row_devs, head_devs), out...]
    add x4, other arithmetic: 4.04 us -> 0.15 us  [feed_forward(): pair = keeps[i] + swap(sends[i], 'heads', 1).astype(f32)]
    unnamed x16 -> x12, local copies, waits for them, and re-layouts: 5.58 us -> 2.29 us
    ppermute x20, waiting for transfers between devices: 4.72 us -> 7.4 us  [swap(): lax.ppermute(x, axis, [(i, i ^ flip) for i in range(lax.axis_size(axis))])]
    ppermute x20, starting transfers between devices: 13.1 us -> 14.7 us  [swap(): lax.ppermute(x, axis, [(i, i ^ flip) for i in range(lax.axis_size(axis))])]
    ppermute x18, starting transfers between devices: 24.3 us -> 23 us  [shift(): return lax.ppermute(x, axis, [(i, (i + step) % n) for i in range(n)])]
  transfers between devices with their start and end apart: 38 -> 38, of which waited for: 17 -> 18; matrix products, arithmetic and copies ran while one was open for 4% -> 0% of each run, Pallas kernels for 0% -> 10%
where the time goes in v3:
time: 100 us; the launch traced here: 101 us
  starting transfers between devices  37.7 us (38%)
  Pallas kernels  36.7 us (37%)
  waiting for transfers between devices  22.8 us (23%)
  local copies, waits for them, and re-layouts  2.34 us (2%)
  other arithmetic  1.03 us (1%)
    ppermute x18, starting transfers between devices, shift(): return lax.ppermute(x, axis, [(i, (i + step) % n) for i in range(n)])  23 us
    ppermute x18, waiting for transfers between devices, shift(): return lax.ppermute(x, axis, [(i, (i + step) % n) for i in range(n)])  15.4 us
    ppermute x20, starting transfers between devices, swap(): lax.ppermute(x, axis, [(i, i ^ flip) for i in range(lax.axis_size(axis))])  14.7 us
    pallas_call x1, Pallas kernels, attend(): pl.pallas_call(functools.partial(attend_kernel, count, len(later), listed...  13.1 us
    pallas_call x2, Pallas kernels, fetch(): pl.pallas_call(functools.partial(fetch_kernel, count), out_shape=[pltpu.V...  10.4 us
    pallas_call x1, Pallas kernels, swiglu(): pl.pallas_call(functools.partial(swiglu_kernel, row_devs, head_devs), out...  9.46 us
    ppermute x20, waiting for transfers between devices, swap(): lax.ppermute(x, axis, [(i, i ^ flip) for i in range(lax.axis_size(axis))])  7.4 us
    pallas_call x1, Pallas kernels, project(): pl.pallas_call(functools.partial(project_kernel, count, parts), grid=(col...  2.68 us
  transfers between devices with their start and end apart: 38, of which 18 were waited for; matrix products, arithmetic and copies ran while one was open for 0% of the time, Pallas kernels for 10%

profile of v3, /device:TPU:0, one launch (start us, length us, event | category | flops | bytes accessed | tf_op | source)
XLA Modules:
  0.0 101.0 jit_solution(14136143429835932003)
XLA Ops:
  3.5 3.1 %collective-permute-start = (bf16[16,2176]{1,0:T(8,128)(2,1)S(1)}, bf16[16,2176]{1,0:T(8,128)(2,1)S(1)}, u32[]{:S(2)}, u32[]{:S(2)}) collective-permute-start(bf16[16,2176]{1,0:T(8,128)(2,1)S(1)} %get-tuple-element.38), channel_id=1, source_target_pairs={{0,4},{4,8},{8,12},{12,0},{1,5},{5,9},{9,13},{13,1},{2,6},{6,10},{... | collective-permute-start | bytes 208904 | tf_op jit(solution)/shard_map/ppermute | solution.py:404
  6.6 2.6 %collective-permute-start.1 = (bf16[16,2176]{1,0:T(8,128)(2,1)S(1)}, bf16[16,2176]{1,0:T(8,128)(2,1)S(1)}, u32[]{:S(2)}, u32[]{:S(2)}) collective-permute-start(bf16[16,2176]{1,0:T(8,128)(2,1)S(1)} %get-tuple-element.39), channel_id=1, source_target_pairs={{0,8},{4,12},{8,0},{12,4},{1,9},{5,13},{9,1},{13,5},{2,10},{6,14},... | collective-permute-start | bytes 208904 | tf_op jit(solution)/shard_map/ppermute | solution.py:404
  9.2 1.3 %collective-permute-start.2 = (bf16[16,2176]{1,0:T(8,128)(2,1)S(1)}, bf16[16,2176]{1,0:T(8,128)(2,1)S(1)}, u32[]{:S(2)}, u32[]{:S(2)}) collective-permute-start(bf16[16,2176]{1,0:T(8,128)(2,1)S(1)} %get-tuple-element.40), channel_id=1, source_target_pairs={{0,12},{4,0},{8,4},{12,8},{1,13},{5,1},{9,5},{13,9},{2,14},{6,2},{... | collective-permute-start | bytes 208904 | tf_op jit(solution)/shard_map/ppermute | solution.py:404
  10.5 3.4 %fetch.2.kv = bf16[64,2,2,128,128]{4,3,2,1,0:T(8,128)(2,1)S(1)} custom-call(bf16[32,64]{1,0:T(8,128)(2,1)S(1)} %get-tuple-element.36.after_ref, bf16[64,2,2,128,128]{4,3,2,1,0:T(8,128)(2,1)} %refs_0_.2), custom_call_target="tpu_custom_call" | custom-call | bytes 8388608 | tf_op jit(solution)/shard_map/fetch/pallas_call | solution.py:46
  14.1 13.1 %attend.1 = (bf16[16,2048]{1,0:T(8,128)(2,1)S(1)}, bf16[16,2048]{1,0:T(8,128)(2,1)S(1)}, bf16[16,2048]{1,0:T(8,128)(2,1)S(1)}, bf16[16,2048]{1,0:T(8,128)(2,1)S(...) custom-call(f32[2,2]{1,0:T(2,128)S(1)} %copy-done.3, bf16[64,2,2,128,128]{4,3,2,1,0:T(8,128)(2,1)S(1)} %fetch.2.kv, ...), custom_call_target="tpu_custom_call" | custom-call | tf_op jit(solution)/shard_map/attend/pallas_call | solution.py:246
  27.3 1.9 %collective-permute-start.5 = (bf16[16,2048]{1,0:T(8,128)(2,1)S(1)}, bf16[16,2048]{1,0:T(8,128)(2,1)S(1)}, u32[]{:S(2)}, u32[]{:S(2)}) collective-permute-start(bf16[16,2048]{1,0:T(8,128)(2,1)S(1)} %get-tuple-element.44), channel_id=1, source_target_pairs={{0,4},{4,8},{8,12},{12,0},{1,5},{5,9},{9,13},{13,1},{2,6},{6,10},{... | collective-permute-start | bytes 196616 | tf_op jit(solution)/shard_map/ppermute | solution.py:404
  29.2 2.7 %collective-permute-done.3 = bf16[16,2048]{1,0:T(8,128)(2,1)S(1)} collective-permute-done((bf16[16,2048]{1,0:T(8,128)(2,1)S(1)}, bf16[16,2048]{1,0:T(8,128)(2,1)S(1)}, u32[]{:S(2)}, u32[]{:S(2)}) %collective-permute-start.3) | collective-permute-done | bytes 65568 | tf_op jit(solution)/shard_map/ppermute | solution.py:404
  31.9 3.2 %collective-permute-done.4 = bf16[16,2048]{1,0:T(8,128)(2,1)S(1)} collective-permute-done((bf16[16,2048]{1,0:T(8,128)(2,1)S(1)}, bf16[16,2048]{1,0:T(8,128)(2,1)S(1)}, u32[]{:S(2)}, u32[]{:S(2)}) %collective-permute-start.4) | collective-permute-done | bytes 65568 | tf_op jit(solution)/shard_map/ppermute | solution.py:404
  35.3 1.5 %collective-permute-start.8 = (bf16[32,2048]{1,0:T(8,128)(2,1)S(1)}, bf16[32,2048]{1,0:T(8,128)(2,1)S(1)}, u32[]{:S(2)}, u32[]{:S(2)}) collective-permute-start(bf16[32,2048]{1,0:T(8,128)(2,1)S(1)} %convolution_convert_fusion.after_ref.refs_0_), channel_id=1, source_target_pairs={{0,12},{4,0},{8,4},{12,8},{1,13},{5,1},{9,5},{13,9},{2,14},{6,2},{... | collective-permute-start | bytes 393224 | tf_op jit(solution)/shard_map/ppermute | solution.py:404
  36.8 1.8 %collective-permute-start.6 = (bf16[32,2048]{1,0:T(8,128)(2,1)S(1)}, bf16[32,2048]{1,0:T(8,128)(2,1)S(1)}, u32[]{:S(2)}, u32[]{:S(2)}) collective-permute-start(bf16[32,2048]{1,0:T(8,128)(2,1)S(1)} %convolution_convert_fusion.after_ref.refs_0_), channel_id=1, source_target_pairs={{0,4},{4,8},{8,12},{12,0},{1,5},{5,9},{9,13},{13,1},{2,6},{6,10},{... | collective-permute-start | bytes 393224 | tf_op jit(solution)/shard_map/ppermute | solution.py:404
  38.6 7.0 %fetch.3 = (bf16[5120,1024]{1,0:T(8,128)(2,1)S(1)}, bf16[1024,5120]{1,0:T(8,128)(2,1)S(1)}) custom-call(bf16[32,2048]{1,0:T(8,128)(2,1)S(1)} %convolution_convert_fusion.after_ref.refs_0_, bf16[5120,1024]{1,0:T(8,128)(2,1)} %refs_0_.3, bf16[1024,5120]{1,0:T(8,128)(2,1)} %refs_1_.1), custom_call_target="tpu_custom_call" | custom-call | bytes 20971520 | tf_op jit(solution)/shard_map/fetch/pallas_call | solution.py:46
  45.6 3.1 %collective-permute-done.7.refs_2_ = bf16[32,2048]{1,0:T(8,128)(2,1)S(1)} collective-permute-done((bf16[32,2048]{1,0:T(8,128)(2,1)S(1)}, bf16[32,2048]{1,0:T(8,128)(2,1)S(1)}, u32[]{:S(2)}, u32[]{:S(2)}) %collective-permute-start.7) | collective-permute-done | bytes 131104 | tf_op jit(solution)/shard_map/ppermute | solution.py:404
  48.7 2.7 %project.1 = (f32[32,1280]{1,0:T(8,128)S(1)}, bf16[32,1280]{1,0:T(8,128)(2,1)S(1)}, bf16[32,1280]{1,0:T(8,128)(2,1)S(1)}, bf16[32,1280]{1,0:T(8,128)(2,1)S(1)}) custom-call(s32[2]{0:T(128)S(1)} %pad_add_fusion.me_ref.at_ref, bf16[32,2048]{1,0:T(8,128)(2,1)S(1)} %convolution_convert_fusion.after_ref.refs_0_, ...), custom_call_target="tpu_custom_call" | custom-call | tf_op jit(solution)/shard_map/project/pallas_call | solution.py:301
  52.7 1.4 %collective-permute-start.11 = (bf16[32,1280]{1,0:T(8,128)(2,1)S(1)}, bf16[32,1280]{1,0:T(8,128)(2,1)S(1)}, u32[]{:S(2)}, u32[]{:S(2)}) collective-permute-start(bf16[32,1280]{1,0:T(8,128)(2,1)S(1)} %get-tuple-element.55), channel_id=1, source_target_pairs={{0,3},{1,0},{2,1},{3,2},{4,7},{5,4},{6,5},{7,6},{8,11},{9,8},{10,9... | collective-permute-start | bytes 245768 | tf_op jit(solution)/shard_map/ppermute | solution.py:404
  54.1 1.4 %collective-permute-done.9 = bf16[32,1280]{1,0:T(8,128)(2,1)S(1)} collective-permute-done((bf16[32,1280]{1,0:T(8,128)(2,1)S(1)}, bf16[32,1280]{1,0:T(8,128)(2,1)S(1)}, u32[]{:S(2)}, u32[]{:S(2)}) %collective-permute-start.9) | collective-permute-done | bytes 81952 | tf_op jit(solution)/shard_map/ppermute | solution.py:404
  57.2 1.9 %collective-permute-start.19 = (bf16[32,1280]{1,0:T(8,128)(2,1)S(1)}, bf16[32,1280]{1,0:T(8,128)(2,1)S(1)}, u32[]{:S(2)}, u32[]{:S(2)}) collective-permute-start(bf16[32,1280]{1,0:T(8,128)(2,1)S(1)} %add_convert_fusion.refs_0_), channel_id=1, source_target_pairs={{0,8},{4,12},{8,0},{12,4},{1,9},{5,13},{9,1},{13,5},{2,10},{6,14},... | collective-permute-start | bytes 245768 | tf_op jit(solution)/shard_map/ppermute | solution.py:404
  59.1 1.9 %collective-permute-start.15 = (bf16[32,1280]{1,0:T(8,128)(2,1)S(1)}, bf16[32,1280]{1,0:T(8,128)(2,1)S(1)}, u32[]{:S(2)}, u32[]{:S(2)}) collective-permute-start(bf16[32,1280]{1,0:T(8,128)(2,1)S(1)} %add_convert_fusion.refs_0_), channel_id=1, source_target_pairs={{0,4},{4,8},{8,12},{12,0},{1,5},{5,9},{9,13},{13,1},{2,6},{6,10},{... | collective-permute-start | bytes 245768 | tf_op jit(solution)/shard_map/ppermute | solution.py:404
  63.8 3.6 %collective-permute-start.24 = (bf16[32,1280]{1,0:T(8,128)(2,1)S(1)}, bf16[32,1280]{1,0:T(8,128)(2,1)S(1)}, u32[]{:S(2)}, u32[]{:S(2)}) collective-permute-start(bf16[32,1280]{1,0:T(8,128)(2,1)S(1)} %collective-permute-done.23.refs_12_), channel_id=1, source_target_pairs={{0,1},{1,0},{2,3},{3,2},{4,5},{5,4},{6,7},{7,6},{8,9},{9,8},{10,11... | collective-permute-start | bytes 245768 | tf_op jit(solution)/shard_map/ppermute | solution.py:408
  70.1 1.9 %collective-permute-done.21.refs_10_ = bf16[32,1280]{1,0:T(8,128)(2,1)S(1)} collective-permute-done((bf16[32,1280]{1,0:T(8,128)(2,1)S(1)}, bf16[32,1280]{1,0:T(8,128)(2,1)S(1)}, u32[]{:S(2)}, u32[]{:S(2)}) %collective-permute-start.21) | collective-permute-done | bytes 81952 | tf_op jit(solution)/shard_map/ppermute | solution.py:408
  74.9 9.5 %swiglu.1 = (f32[64,1280]{1,0:T(8,128)S(1)}, f32[64,1280]{1,0:T(8,128)S(1)}, f32[64,1280]{1,0:T(8,128)S(1)}, f32[64,1280]{1,0:T(8,128)S(1)}, bf16[64,1280]{1,0:T...) custom-call(s32[2]{0:T(128)S(1)} %pad_add_fusion.me_ref.at_ref, ...), custom_call_target="tpu_custom_call" | custom-call | tf_op jit(solution)/shard_map/swiglu/pallas_call | solution.py:385
  91.2 1.4 %collective-permute-start.29 = (bf16[32,1280]{1,0:T(8,128)(2,1)S(1)}, bf16[32,1280]{1,0:T(8,128)(2,1)S(1)}, u32[]{:S(2)}, u32[]{:S(2)}) collective-permute-start(bf16[32,1280]{1,0:T(8,128)(2,1)S(1)} %fusion.11), channel_id=1, source_target_pairs={{0,8},{4,12},{8,0},{12,4},{1,9},{5,13},{9,1},{13,5},{2,10},{6,14},... | collective-permute-start | bytes 245768 | tf_op jit(solution)/shard_map/ppermute | solution.py:404
  93.0 1.7 %collective-permute-done.34 = bf16[32,1280]{1,0:T(8,128)(2,1)S(1)} collective-permute-done((bf16[32,1280]{1,0:T(8,128)(2,1)S(1)}, bf16[32,1280]{1,0:T(8,128)(2,1)S(1)}, u32[]{:S(2)}, u32[]{:S(2)}) %collective-permute-start.34) | collective-permute-done | bytes 81952 | tf_op jit(solution)/shard_map/ppermute | solution.py:408
  94.7 2.2 %collective-permute-start.35 = (bf16[32,1280]{1,0:T(8,128)(2,1)S(1)}, bf16[32,1280]{1,0:T(8,128)(2,1)S(1)}, u32[]{:S(2)}, u32[]{:S(2)}) collective-permute-start(bf16[32,1280]{1,0:T(8,128)(2,1)S(1)} %fusion.9), channel_id=1, source_target_pairs={{0,12},{4,0},{8,4},{12,8},{1,13},{5,1},{9,5},{13,9},{2,14},{6,2},{... | collective-permute-start | bytes 245768 | tf_op jit(solution)/shard_map/ppermute | solution.py:404
  96.9 1.4 %collective-permute-done.29 = bf16[32,1280]{1,0:T(8,128)(2,1)S(1)} collective-permute-done((bf16[32,1280]{1,0:T(8,128)(2,1)S(1)}, bf16[32,1280]{1,0:T(8,128)(2,1)S(1)}, u32[]{:S(2)}, u32[]{:S(2)}) %collective-permute-start.29) | collective-permute-done | bytes 81952 | tf_op jit(solution)/shard_map/ppermute | solution.py:404
  (85 shorter events, 25.0 us)
Async XLA Ops:
  3.5 10.4 %collective-permute-start = (bf16[16,2176]{1,0:T(8,128)(2,1)S(1)}, bf16[16,2176]{1,0:T(8,128)(2,1)S(1)}, u32[]{:S(2)}, u32[]{:S(2)}) collective-permute-start(bf16[16,2176]{1,0:T(8,128)(2,1)S(1)} %get-tuple-element.38), channel_id=1, source_target_pairs={{0,4},{4,8},{8,12},{12,0},{1,5},{5,9},{9,13},{13,1},{2,6},{6,10},{... | collective-permute-start | bytes 208904 | tf_op jit(solution)/shard_map/ppermute | solution.py:404
  6.6 7.4 %collective-permute-start.1 = (bf16[16,2176]{1,0:T(8,128)(2,1)S(1)}, bf16[16,2176]{1,0:T(8,128)(2,1)S(1)}, u32[]{:S(2)}, u32[]{:S(2)}) collective-permute-start(bf16[16,2176]{1,0:T(8,128)(2,1)S(1)} %get-tuple-element.39), channel_id=1, source_target_pairs={{0,8},{4,12},{8,0},{12,4},{1,9},{5,13},{9,1},{13,5},{2,10},{6,14},... | collective-permute-start | bytes 208904 | tf_op jit(solution)/shard_map/ppermute | solution.py:404
  9.2 4.9 %collective-permute-start.2 = (bf16[16,2176]{1,0:T(8,128)(2,1)S(1)}, bf16[16,2176]{1,0:T(8,128)(2,1)S(1)}, u32[]{:S(2)}, u32[]{:S(2)}) collective-permute-start(bf16[16,2176]{1,0:T(8,128)(2,1)S(1)} %get-tuple-element.40), channel_id=1, source_target_pairs={{0,12},{4,0},{8,4},{12,8},{1,13},{5,1},{9,5},{13,9},{2,14},{6,2},{... | collective-permute-start | bytes 208904 | tf_op jit(solution)/shard_map/ppermute | solution.py:404
  27.2 7.9 %collective-permute-start.4 = (bf16[16,2048]{1,0:T(8,128)(2,1)S(1)}, bf16[16,2048]{1,0:T(8,128)(2,1)S(1)}, u32[]{:S(2)}, u32[]{:S(2)}) collective-permute-start(bf16[16,2048]{1,0:T(8,128)(2,1)S(1)} %get-tuple-element.43), channel_id=1, source_target_pairs={{0,8},{4,12},{8,0},{12,4},{1,9},{5,13},{9,1},{13,5},{2,10},{6,14},... | collective-permute-start | bytes 196616 | tf_op jit(solution)/shard_map/ppermute | solution.py:404
  27.3 7.8 %collective-permute-start.5 = (bf16[16,2048]{1,0:T(8,128)(2,1)S(1)}, bf16[16,2048]{1,0:T(8,128)(2,1)S(1)}, u32[]{:S(2)}, u32[]{:S(2)}) collective-permute-start(bf16[16,2048]{1,0:T(8,128)(2,1)S(1)} %get-tuple-element.44), channel_id=1, source_target_pairs={{0,4},{4,8},{8,12},{12,0},{1,5},{5,9},{9,13},{13,1},{2,6},{6,10},{... | collective-permute-start | bytes 196616 | tf_op jit(solution)/shard_map/ppermute | solution.py:404
  35.3 10.3 %collective-permute-start.8 = (bf16[32,2048]{1,0:T(8,128)(2,1)S(1)}, bf16[32,2048]{1,0:T(8,128)(2,1)S(1)}, u32[]{:S(2)}, u32[]{:S(2)}) collective-permute-start(bf16[32,2048]{1,0:T(8,128)(2,1)S(1)} %convolution_convert_fusion.after_ref.refs_0_), channel_id=1, source_target_pairs={{0,12},{4,0},{8,4},{12,8},{1,13},{5,1},{9,5},{13,9},{2,14},{6,2},{... | collective-permute-start | bytes 393224 | tf_op jit(solution)/shard_map/ppermute | solution.py:404
  36.7 11.9 %collective-permute-start.7 = (bf16[32,2048]{1,0:T(8,128)(2,1)S(1)}, bf16[32,2048]{1,0:T(8,128)(2,1)S(1)}, u32[]{:S(2)}, u32[]{:S(2)}) collective-permute-start(bf16[32,2048]{1,0:T(8,128)(2,1)S(1)} %convolution_convert_fusion.after_ref.refs_0_), channel_id=1, source_target_pairs={{0,8},{4,12},{8,0},{12,4},{1,9},{5,13},{9,1},{13,5},{2,10},{6,14},... | collective-permute-start | bytes 393224 | tf_op jit(solution)/shard_map/ppermute | solution.py:404
  36.8 11.9 %collective-permute-start.6 = (bf16[32,2048]{1,0:T(8,128)(2,1)S(1)}, bf16[32,2048]{1,0:T(8,128)(2,1)S(1)}, u32[]{:S(2)}, u32[]{:S(2)}) collective-permute-start(bf16[32,2048]{1,0:T(8,128)(2,1)S(1)} %convolution_convert_fusion.after_ref.refs_0_), channel_id=1, source_target_pairs={{0,4},{4,8},{8,12},{12,0},{1,5},{5,9},{9,13},{13,1},{2,6},{6,10},{... | collective-permute-start | bytes 393224 | tf_op jit(solution)/shard_map/ppermute | solution.py:404
  51.4 5.3 %collective-permute-start.10 = (bf16[32,1280]{1,0:T(8,128)(2,1)S(1)}, bf16[32,1280]{1,0:T(8,128)(2,1)S(1)}, u32[]{:S(2)}, u32[]{:S(2)}) collective-permute-start(bf16[32,1280]{1,0:T(8,128)(2,1)S(1)} %get-tuple-element.54), channel_id=1, source_target_pairs={{0,2},{1,3},{2,0},{3,1},{4,6},{5,7},{6,4},{7,5},{8,10},{9,11},{10,... | collective-permute-start | bytes 245768 | tf_op jit(solution)/shard_map/ppermute | solution.py:404
  56.8 5.5 %collective-permute-start.23 = (bf16[32,1280]{1,0:T(8,128)(2,1)S(1)}, bf16[32,1280]{1,0:T(8,128)(2,1)S(1)}, u32[]{:S(2)}, u32[]{:S(2)}) collective-permute-start(bf16[32,1280]{1,0:T(8,128)(2,1)S(1)} %add_convert_fusion.refs_0_), channel_id=1, source_target_pairs={{0,12},{4,0},{8,4},{12,8},{1,13},{5,1},{9,5},{13,9},{2,14},{6,2},{... | collective-permute-start | bytes 245768 | tf_op jit(solution)/shard_map/ppermute | solution.py:404
  57.2 6.6 %collective-permute-start.19 = (bf16[32,1280]{1,0:T(8,128)(2,1)S(1)}, bf16[32,1280]{1,0:T(8,128)(2,1)S(1)}, u32[]{:S(2)}, u32[]{:S(2)}) collective-permute-start(bf16[32,1280]{1,0:T(8,128)(2,1)S(1)} %add_convert_fusion.refs_0_), channel_id=1, source_target_pairs={{0,8},{4,12},{8,0},{12,4},{1,9},{5,13},{9,1},{13,5},{2,10},{6,14},... | collective-permute-start | bytes 245768 | tf_op jit(solution)/shard_map/ppermute | solution.py:404
  59.1 8.4 %collective-permute-start.15 = (bf16[32,1280]{1,0:T(8,128)(2,1)S(1)}, bf16[32,1280]{1,0:T(8,128)(2,1)S(1)}, u32[]{:S(2)}, u32[]{:S(2)}) collective-permute-start(bf16[32,1280]{1,0:T(8,128)(2,1)S(1)} %add_convert_fusion.refs_0_), channel_id=1, source_target_pairs={{0,4},{4,8},{8,12},{12,0},{1,5},{5,9},{9,13},{13,1},{2,6},{6,10},{... | collective-permute-start | bytes 245768 | tf_op jit(solution)/shard_map/ppermute | solution.py:404
  61.0 7.7 %collective-permute-start.13 = (bf16[32,1280]{1,0:T(8,128)(2,1)S(1)}, bf16[32,1280]{1,0:T(8,128)(2,1)S(1)}, u32[]{:S(2)}, u32[]{:S(2)}) collective-permute-start(bf16[32,1280]{1,0:T(8,128)(2,1)S(1)} %add_convert_fusion.refs_0_), channel_id=1, source_target_pairs={{0,2},{1,3},{2,0},{3,1},{4,6},{5,7},{6,4},{7,5},{8,10},{9,11},{10,... | collective-permute-start | bytes 245768 | tf_op jit(solution)/shard_map/ppermute | solution.py:408
  62.3 6.4 %collective-permute-start.12 = (bf16[32,1280]{1,0:T(8,128)(2,1)S(1)}, bf16[32,1280]{1,0:T(8,128)(2,1)S(1)}, u32[]{:S(2)}, u32[]{:S(2)}) collective-permute-start(bf16[32,1280]{1,0:T(8,128)(2,1)S(1)} %add_convert_fusion.refs_0_), channel_id=1, source_target_pairs={{0,1},{1,0},{2,3},{3,2},{4,5},{5,4},{6,7},{7,6},{8,9},{9,8},{10,11... | collective-permute-start | bytes 245768 | tf_op jit(solution)/shard_map/ppermute | solution.py:408
  62.3 7.2 %collective-permute-start.25 = (bf16[32,1280]{1,0:T(8,128)(2,1)S(1)}, bf16[32,1280]{1,0:T(8,128)(2,1)S(1)}, u32[]{:S(2)}, u32[]{:S(2)}) collective-permute-start(bf16[32,1280]{1,0:T(8,128)(2,1)S(1)} %collective-permute-done.23.refs_12_), channel_id=1, source_target_pairs={{0,2},{1,3},{2,0},{3,1},{4,6},{5,7},{6,4},{7,5},{8,10},{9,11},{10,... | collective-permute-start | bytes 245768 | tf_op jit(solution)/shard_map/ppermute | solution.py:408
  63.8 5.9 %collective-permute-start.24 = (bf16[32,1280]{1,0:T(8,128)(2,1)S(1)}, bf16[32,1280]{1,0:T(8,128)(2,1)S(1)}, u32[]{:S(2)}, u32[]{:S(2)}) collective-permute-start(bf16[32,1280]{1,0:T(8,128)(2,1)S(1)} %collective-permute-done.23.refs_12_), channel_id=1, source_target_pairs={{0,1},{1,0},{2,3},{3,2},{4,5},{5,4},{6,7},{7,6},{8,9},{9,8},{10,11... | collective-permute-start | bytes 245768 | tf_op jit(solution)/shard_map/ppermute | solution.py:408
  68.7 4.9 %collective-permute-start.17 = (bf16[32,1280]{1,0:T(8,128)(2,1)S(1)}, bf16[32,1280]{1,0:T(8,128)(2,1)S(1)}, u32[]{:S(2)}, u32[]{:S(2)}) collective-permute-start(bf16[32,1280]{1,0:T(8,128)(2,1)S(1)} %collective-permute-done.15.refs_4_), channel_id=1, source_target_pairs={{0,2},{1,3},{2,0},{3,1},{4,6},{5,7},{6,4},{7,5},{8,10},{9,11},{10,... | collective-permute-start | bytes 245768 | tf_op jit(solution)/shard_map/ppermute | solution.py:408
  85.9 5.2 %collective-permute-start.28 = (bf16[32,1280]{1,0:T(8,128)(2,1)S(1)}, bf16[32,1280]{1,0:T(8,128)(2,1)S(1)}, u32[]{:S(2)}, u32[]{:S(2)}) collective-permute-start(bf16[32,1280]{1,0:T(8,128)(2,1)S(1)} %slice.65), channel_id=1, source_target_pairs={{0,2},{1,3},{2,0},{3,1},{4,6},{5,7},{6,4},{7,5},{8,10},{9,11},{10,... | collective-permute-start | bytes 245768 | tf_op jit(solution)/shard_map/ppermute | solution.py:408
  87.3 5.6 %collective-permute-start.31 = (bf16[32,1280]{1,0:T(8,128)(2,1)S(1)}, bf16[32,1280]{1,0:T(8,128)(2,1)S(1)}, u32[]{:S(2)}, u32[]{:S(2)}) collective-permute-start(bf16[32,1280]{1,0:T(8,128)(2,1)S(1)} %slice.64), channel_id=1, source_target_pairs={{0,2},{1,3},{2,0},{3,1},{4,6},{5,7},{6,4},{7,5},{8,10},{9,11},{10,... | collective-permute-start | bytes 245768 | tf_op jit(solution)/shard_map/ppermute | solution.py:408
  88.2 6.5 %collective-permute-start.34 = (bf16[32,1280]{1,0:T(8,128)(2,1)S(1)}, bf16[32,1280]{1,0:T(8,128)(2,1)S(1)}, u32[]{:S(2)}, u32[]{:S(2)}) collective-permute-start(bf16[32,1280]{1,0:T(8,128)(2,1)S(1)} %slice.63), channel_id=1, source_target_pairs={{0,2},{1,3},{2,0},{3,1},{4,6},{5,7},{6,4},{7,5},{8,10},{9,11},{10,... | collective-permute-start | bytes 245768 | tf_op jit(solution)/shard_map/ppermute | solution.py:408
  89.6 7.3 %collective-permute-start.37 = (bf16[32,1280]{1,0:T(8,128)(2,1)S(1)}, bf16[32,1280]{1,0:T(8,128)(2,1)S(1)}, u32[]{:S(2)}, u32[]{:S(2)}) collective-permute-start(bf16[32,1280]{1,0:T(8,128)(2,1)S(1)} %slice.62), channel_id=1, source_target_pairs={{0,2},{1,3},{2,0},{3,1},{4,6},{5,7},{6,4},{7,5},{8,10},{9,11},{10,... | collective-permute-start | bytes 245768 | tf_op jit(solution)/shard_map/ppermute | solution.py:408
  91.2 7.1 %collective-permute-start.29 = (bf16[32,1280]{1,0:T(8,128)(2,1)S(1)}, bf16[32,1280]{1,0:T(8,128)(2,1)S(1)}, u32[]{:S(2)}, u32[]{:S(2)}) collective-permute-start(bf16[32,1280]{1,0:T(8,128)(2,1)S(1)} %fusion.11), channel_id=1, source_target_pairs={{0,8},{4,12},{8,0},{12,4},{1,9},{5,13},{9,1},{13,5},{2,10},{6,14},... | collective-permute-start | bytes 245768 | tf_op jit(solution)/shard_map/ppermute | solution.py:404
  92.9 6.5 %collective-permute-start.32 = (bf16[32,1280]{1,0:T(8,128)(2,1)S(1)}, bf16[32,1280]{1,0:T(8,128)(2,1)S(1)}, u32[]{:S(2)}, u32[]{:S(2)}) collective-permute-start(bf16[32,1280]{1,0:T(8,128)(2,1)S(1)} %fusion.10), channel_id=1, source_target_pairs={{0,4},{4,8},{8,12},{12,0},{1,5},{5,9},{9,13},{13,1},{2,6},{6,10},{... | collective-permute-start | bytes 245768 | tf_op jit(solution)/shard_map/ppermute | solution.py:404
  94.7 5.6 %collective-permute-start.35 = (bf16[32,1280]{1,0:T(8,128)(2,1)S(1)}, bf16[32,1280]{1,0:T(8,128)(2,1)S(1)}, u32[]{:S(2)}, u32[]{:S(2)}) collective-permute-start(bf16[32,1280]{1,0:T(8,128)(2,1)S(1)} %fusion.9), channel_id=1, source_target_pairs={{0,12},{4,0},{8,4},{12,8},{1,13},{5,1},{9,5},{13,9},{2,14},{6,2},{... | collective-permute-start | bytes 245768 | tf_op jit(solution)/shard_map/ppermute | solution.py:404
  (20 other events, 122.5 us)

commit v4 on v3

--- a/solution.py
+++ b/solution.py
@@ -57,12 +57,20 @@
     )(after, *map(stay, arrays))
 
 
-def dispatch_kernel(blocks_dev, me_ref, ids_ref, len_ref, q_ref, place_ref, *send_refs):
+def dispatch_kernel(blocks_dev, me_ref, ids_hbm, len_hbm, q_hbm, place_ref, *refs):
+    send_refs, (ids_ref, len_ref, q_ref, sems) = refs[:-4], refs[-4:]
+    ids_copy = pltpu.make_async_copy(ids_hbm, ids_ref, sems.at[0])
+    len_copy = pltpu.make_async_copy(len_hbm, len_ref, sems.at[1])
+    q_copy = pltpu.make_async_copy(q_hbm, q_ref, sems.at[2])
+    for copy in (ids_copy, len_copy, q_copy):
+        copy.start()
     count = len(send_refs)
     slots = send_refs[0].shape[0]
     width = q_ref.shape[1]
     rows, listed = ids_ref.shape
     me = me_ref[0]
+    ids_copy.wait()
+    len_copy.wait()
     ids = ids_ref[...].astype(f32)
     owner = jnp.floor((ids[:, 0:1] + 0.5) * (1.0 / blocks_dev))
     ahead = owner - me.astype(f32)
@@ -85,6 +93,7 @@
     high = jnp.floor(length * (1.0 / 64))
     meta = jnp.where(lane == listed, high, meta)
     meta = jnp.where(lane == listed + 1, length - high * 64, meta)
+    q_copy.wait()
     send = mxu(place, q_ref[...], (0, 0)).astype(bf16)
     send_meta = mxu(place, meta.astype(bf16), (0, 0)).astype(bf16)
     for s in range(count):
@@ -99,18 +108,24 @@
     got = pl.pallas_call(
         functools.partial(dispatch_kernel, blocks_dev),
         out_shape=outs,
-        in_specs=[smem(), vmem(), vmem(), vmem()],
+        in_specs=[smem(), hbm(), hbm(), hbm()],
         out_specs=[vmem()] * (count + 1),
+        scratch_shapes=[
+            pltpu.VMEM(row_blocks.shape, jnp.int32),
+            pltpu.VMEM((1, rows), jnp.int32),
+            pltpu.VMEM((rows, width), bf16),
+            pltpu.SemaphoreType.DMA((3,)),
+        ],
         compiler_params=pltpu.CompilerParams(vmem_limit_bytes=8 * mib),
         name="dispatch",
-    )(me, row_blocks, row_len.reshape(1, rows), queries)
+    )(me, stay(row_blocks), stay(row_len.reshape(1, rows)), stay(queries))
     return got[0], got[1:]
 
 
 tile_rows = 16
 
 
-def attend_kernel(count, later, listed, group, step_blocks, scale_ref, kv, *refs):
+def attend_kernel(count, later, listed, group, long_blocks, scale_ref, kv, *refs):
     in_refs, refs = refs[:count], refs[count:]
     later_refs, refs = refs[:later], refs[later:]
     out_refs, refs = refs[:count], refs[count:]
@@ -175,10 +190,10 @@
     os[...] = jnp.zeros_like(os)
     int_copy.wait()
 
-    tokens = step_blocks * tok
     tall = group * tile_rows
     factors = [scale_ref[0, k] * (log2_e / math.sqrt(dim)) for k in range(heads)]
-    spread = iota((tall, tokens), 1)
+    short_blocks = max(1, long_blocks // 2)
+    long_tokens, short_tokens = long_blocks * tok, short_blocks * tok
 
     def tile_body(t, _):
         top = scalars[2, t]
@@ -193,9 +208,9 @@
             for k in range(heads)
         ]
 
-        def step(c, carry):
-            keep = spread < spans - c * tokens
-            blocks = [scalars[doc, c * step_blocks + j] for j in range(step_blocks)]
+        def step(blocks_in, first, carry):
+            keep = iota((tall, blocks_in * tok), 1) < spans - first * tok
+            blocks = [scalars[doc, first + j] for j in range(blocks_in)]
             after = []
             for k in range(heads):
                 peak, denom, acc = carry[k]
@@ -215,11 +230,13 @@
             (jnp.full((tall, 1), -1e30, f32), jnp.zeros((tall, 1), f32), jnp.zeros((tall, dim), f32))
             for _ in range(heads)
         )
-        steps = (top + (tokens - 1)) // tokens
-
-        @pl.when(steps > 0)
+        longs = (top + (long_tokens - short_tokens - 1)) // long_tokens
+        shorts = jnp.where(top > longs * long_tokens, 1, 0)
+
+        @pl.when(top > 0)
         def _():
-            done = lax.fori_loop(0, steps, step, start)
+            done = lax.fori_loop(0, longs, lambda c, carry: step(long_blocks, c * long_blocks, carry), start)
+            done = lax.fori_loop(0, shorts, lambda c, carry: step(short_blocks, longs * long_blocks, carry), done)
             for k in range(heads):
                 _, denom, acc = done[k]
                 out = (acc * (scale_ref[1, k] / denom)).astype(bf16)
@@ -244,7 +261,7 @@
     total = count * slots
     places = total + tile_rows
     got = pl.pallas_call(
-        functools.partial(attend_kernel, count, len(later), listed, group, min(8, listed)),
+        functools.partial(attend_kernel, count, len(later), listed, group, min(32, listed)),
         out_shape=[jax.ShapeDtypeStruct((slots, width), bf16)] * count
         + [pltpu.VMEM(a.shape, a.dtype) for a in later],
         in_specs=[smem()] + [vmem()] * (count + 1) + [hbm()] * len(later),
@@ -271,14 +288,14 @@
     rows = in_refs[0].shape[0]
     piece = own_ref.shape[0]
 
-    @pl.when(pl.program_id(0) == 0)
-    def _():
-        for s in range(count):
-            source = at_ref[0] - s
-            source = jnp.where(source < 0, source + count, source)
-            x[pl.ds(pl.multiple_of(source * rows, rows), rows), :] = in_refs[s][...]
-
-    y[...] = mxu(x[...], w_ref[...], (1, 0))
+    for s in range(count):
+        source = at_ref[0] - s
+        source = jnp.where(source < 0, source + count, source)
+        x[pl.ds(pl.multiple_of(source * rows, rows), rows), :] = in_refs[s][...]
+    cols = w_ref.shape[1]
+    wide = 256 if cols % 256 == 0 else cols
+    for c in range(0, cols, wide):
+        y[:, c : c + wide] = mxu(x[...], w_ref[:, c : c + wide], (1, 0))
     for s in range(parts):
         target = at_ref[1] + s
         target = jnp.where(target >= parts, target - parts, target)
@@ -295,17 +312,13 @@
     cols = w_out.shape[1]
     tall = rows * count
     piece = tall // parts
-    wide = 256 if cols % 256 == 0 else cols
-    whole = pl.BlockSpec((rows, depth), lambda j: (0, 0))
-    part = pl.BlockSpec((piece, wide), lambda j: (0, j))
     got = pl.pallas_call(
         functools.partial(project_kernel, count, parts),
-        grid=(cols // wide,),
         out_shape=[jax.ShapeDtypeStruct((piece, cols), f32)]
         + [jax.ShapeDtypeStruct((piece, cols), bf16)] * (parts - 1),
-        in_specs=[smem()] + [whole] * count + [pl.BlockSpec((depth, wide), lambda j: (0, j))],
-        out_specs=[part] * parts,
-        scratch_shapes=[pltpu.VMEM((tall, depth), bf16), pltpu.VMEM((tall, wide), f32)],
+        in_specs=[smem()] + [vmem()] * (count + 1),
+        out_specs=[vmem()] * parts,
+        scratch_shapes=[pltpu.VMEM((tall, depth), bf16), pltpu.VMEM((tall, cols), f32)],
         compiler_params=pltpu.CompilerParams(vmem_limit_bytes=12 * mib),
         name="project",
     )(at, *pieces, w_out)

time: 100 us -> 94.5 us (0.945)
  Pallas kernels: 36.7 us -> 32.6 us
  local copies, waits for them, and re-layouts: 2.34 us -> 0.06 us
    pallas_call x1, Pallas kernels: 13.1 us -> 9.34 us  [attend(): pl.pallas_call(functools.partial(attend_kernel, count, len(later), listed...]
    unnamed x12 -> x6, local copies, waits for them, and re-layouts: 2.29 us -> 0.02 us
    pallas_call x1, Pallas kernels: 2.68 us -> 1.52 us  [project(): pl.pallas_call(functools.partial(project_kernel, count, parts), out_shape...]
  transfers between devices with their start and end apart: 38 -> 38, of which waited for: 18 -> 18; matrix products, arithmetic and copies ran while one was open for 0% -> 0% of each run, Pallas kernels for 10% -> 11%
where the time goes in v4:
time: 94.5 us; the launch traced here: 94.6 us
  starting transfers between devices  37 us (39%)
  Pallas kernels  32.6 us (34%)
  waiting for transfers between devices  23.5 us (25%)
  other arithmetic  1.03 us (1%)
    ppermute x18, starting transfers between devices, shift(): return lax.ppermute(x, axis, [(i, (i + step) % n) for i in range(n)])  22.8 us
    ppermute x18, waiting for transfers between devices, shift(): return lax.ppermute(x, axis, [(i, (i + step) % n) for i in range(n)])  16 us
    ppermute x20, starting transfers between devices, swap(): lax.ppermute(x, axis, [(i, i ^ flip) for i in range(lax.axis_size(axis))])  14.2 us
    pallas_call x2, Pallas kernels, fetch(): pl.pallas_call(functools.partial(fetch_kernel, count), out_shape=[pltpu.V...  10.4 us
    pallas_call x1, Pallas kernels, swiglu(): pl.pallas_call(functools.partial(swiglu_kernel, row_devs, head_devs), out...  9.47 us
    pallas_call x1, Pallas kernels, attend(): pl.pallas_call(functools.partial(attend_kernel, count, len(later), listed...  9.34 us
    ppermute x20, waiting for transfers between devices, swap(): lax.ppermute(x, axis, [(i, i ^ flip) for i in range(lax.axis_size(axis))])  7.54 us
    pallas_call x1, Pallas kernels, dispatch(): pl.pallas_call(functools.partial(dispatch_kernel, blocks_dev), out_shape=...  1.89 us
  transfers between devices with their start and end apart: 38, of which 18 were waited for; matrix products, arithmetic and copies ran while one was open for 0% of the time, Pallas kernels for 11%

profile of v4, /device:TPU:0, one launch (start us, length us, event | category | flops | bytes accessed | tf_op | source)
XLA Modules:
  0.0 94.6 jit_solution(10899727658294641638)
XLA Ops:
  0.1 1.9 %dispatch.1 = (bf16[32,64]{1,0:T(8,128)(2,1)S(1)}, bf16[16,2176]{1,0:T(8,128)(2,1)S(1)}, bf16[16,2176]{1,0:T(8,128)(2,1)S(1)}, bf16[16,2176]{1,0:T(8,128)(2,1)S(1)}, bf16[16,2176]{1,0:T(8,128)(2,1)S(1)}) custom-call(s32[2]{0:T(128)S(1)} %pad_add_fusion.me_ref.at_ref, s32[32,32]{1,0:T(8,128)} %ids_hbm.1, s32[1,32]{1,0:T(1,128)} %bitcast.6, bf16[32,2048]{1,0:T(8,128)(2,1)} %q_hbm.1), custom_call_target="tpu_custom_call" | custom-call | tf_op jit(solution)/shard_map/dispatch/pallas_call | solution.py:108
  2.0 3.1 %collective-permute-start = (bf16[16,2176]{1,0:T(8,128)(2,1)S(1)}, bf16[16,2176]{1,0:T(8,128)(2,1)S(1)}, u32[]{:S(2)}, u32[]{:S(2)}) collective-permute-start(bf16[16,2176]{1,0:T(8,128)(2,1)S(1)} %get-tuple-element.38), channel_id=1, source_target_pairs={{0,4},{4,8},{8,12},{12,0},{1,5},{5,9},{9,13},{13,1},{2,6},{6,10},{... | collective-permute-start | bytes 208904 | tf_op jit(solution)/shard_map/ppermute | solution.py:417
  5.0 2.6 %collective-permute-start.1 = (bf16[16,2176]{1,0:T(8,128)(2,1)S(1)}, bf16[16,2176]{1,0:T(8,128)(2,1)S(1)}, u32[]{:S(2)}, u32[]{:S(2)}) collective-permute-start(bf16[16,2176]{1,0:T(8,128)(2,1)S(1)} %get-tuple-element.39), channel_id=1, source_target_pairs={{0,8},{4,12},{8,0},{12,4},{1,9},{5,13},{9,1},{13,5},{2,10},{6,14},... | collective-permute-start | bytes 208904 | tf_op jit(solution)/shard_map/ppermute | solution.py:417
  7.6 1.3 %collective-permute-start.2 = (bf16[16,2176]{1,0:T(8,128)(2,1)S(1)}, bf16[16,2176]{1,0:T(8,128)(2,1)S(1)}, u32[]{:S(2)}, u32[]{:S(2)}) collective-permute-start(bf16[16,2176]{1,0:T(8,128)(2,1)S(1)} %get-tuple-element.40), channel_id=1, source_target_pairs={{0,12},{4,0},{8,4},{12,8},{1,13},{5,1},{9,5},{13,9},{2,14},{6,2},{... | collective-permute-start | bytes 208904 | tf_op jit(solution)/shard_map/ppermute | solution.py:417
  9.0 3.4 %fetch.2.kv = bf16[64,2,2,128,128]{4,3,2,1,0:T(8,128)(2,1)S(1)} custom-call(bf16[32,64]{1,0:T(8,128)(2,1)S(1)} %get-tuple-element.36.after_ref, bf16[64,2,2,128,128]{4,3,2,1,0:T(8,128)(2,1)} %refs_0_.2), custom_call_target="tpu_custom_call" | custom-call | bytes 8388608 | tf_op jit(solution)/shard_map/fetch/pallas_call | solution.py:46
  12.5 9.3 %attend.1 = (bf16[16,2048]{1,0:T(8,128)(2,1)S(1)}, bf16[16,2048]{1,0:T(8,128)(2,1)S(1)}, bf16[16,2048]{1,0:T(8,128)(2,1)S(1)}, bf16[16,2048]{1,0:T(8,128)(2,1)S(...) custom-call(f32[2,2]{1,0:T(2,128)S(1)} %copy-done.1, bf16[64,2,2,128,128]{4,3,2,1,0:T(8,128)(2,1)S(1)} %fetch.2.kv, ...), custom_call_target="tpu_custom_call" | custom-call | tf_op jit(solution)/shard_map/attend/pallas_call | solution.py:263
  22.5 1.5 %collective-permute-start.5 = (bf16[16,2048]{1,0:T(8,128)(2,1)S(1)}, bf16[16,2048]{1,0:T(8,128)(2,1)S(1)}, u32[]{:S(2)}, u32[]{:S(2)}) collective-permute-start(bf16[16,2048]{1,0:T(8,128)(2,1)S(1)} %get-tuple-element.44), channel_id=1, source_target_pairs={{0,4},{4,8},{8,12},{12,0},{1,5},{5,9},{9,13},{13,1},{2,6},{6,10},{... | collective-permute-start | bytes 196616 | tf_op jit(solution)/shard_map/ppermute | solution.py:417
  24.0 2.7 %collective-permute-done.3 = bf16[16,2048]{1,0:T(8,128)(2,1)S(1)} collective-permute-done((bf16[16,2048]{1,0:T(8,128)(2,1)S(1)}, bf16[16,2048]{1,0:T(8,128)(2,1)S(1)}, u32[]{:S(2)}, u32[]{:S(2)}) %collective-permute-start.3) | collective-permute-done | bytes 65568 | tf_op jit(solution)/shard_map/ppermute | solution.py:417
  26.6 3.2 %collective-permute-done.4 = bf16[16,2048]{1,0:T(8,128)(2,1)S(1)} collective-permute-done((bf16[16,2048]{1,0:T(8,128)(2,1)S(1)}, bf16[16,2048]{1,0:T(8,128)(2,1)S(1)}, u32[]{:S(2)}, u32[]{:S(2)}) %collective-permute-start.4) | collective-permute-done | bytes 65568 | tf_op jit(solution)/shard_map/ppermute | solution.py:417
  30.1 1.5 %collective-permute-start.8 = (bf16[32,2048]{1,0:T(8,128)(2,1)S(1)}, bf16[32,2048]{1,0:T(8,128)(2,1)S(1)}, u32[]{:S(2)}, u32[]{:S(2)}) collective-permute-start(bf16[32,2048]{1,0:T(8,128)(2,1)S(1)} %convolution_convert_fusion.after_ref.refs_0_), channel_id=1, source_target_pairs={{0,12},{4,0},{8,4},{12,8},{1,13},{5,1},{9,5},{13,9},{2,14},{6,2},{... | collective-permute-start | bytes 393224 | tf_op jit(solution)/shard_map/ppermute | solution.py:417
  31.5 1.8 %collective-permute-start.6 = (bf16[32,2048]{1,0:T(8,128)(2,1)S(1)}, bf16[32,2048]{1,0:T(8,128)(2,1)S(1)}, u32[]{:S(2)}, u32[]{:S(2)}) collective-permute-start(bf16[32,2048]{1,0:T(8,128)(2,1)S(1)} %convolution_convert_fusion.after_ref.refs_0_), channel_id=1, source_target_pairs={{0,4},{4,8},{8,12},{12,0},{1,5},{5,9},{9,13},{13,1},{2,6},{6,10},{... | collective-permute-start | bytes 393224 | tf_op jit(solution)/shard_map/ppermute | solution.py:417
  33.3 7.0 %fetch.3 = (bf16[5120,1024]{1,0:T(8,128)(2,1)S(1)}, bf16[1024,5120]{1,0:T(8,128)(2,1)S(1)}) custom-call(bf16[32,2048]{1,0:T(8,128)(2,1)S(1)} %convolution_convert_fusion.after_ref.refs_0_, bf16[5120,1024]{1,0:T(8,128)(2,1)} %refs_0_.3, bf16[1024,5120]{1,0:T(8,128)(2,1)} %refs_1_.1), custom_call_target="tpu_custom_call" | custom-call | bytes 20971520 | tf_op jit(solution)/shard_map/fetch/pallas_call | solution.py:46
  40.3 3.1 %collective-permute-done.7.refs_2_ = bf16[32,2048]{1,0:T(8,128)(2,1)S(1)} collective-permute-done((bf16[32,2048]{1,0:T(8,128)(2,1)S(1)}, bf16[32,2048]{1,0:T(8,128)(2,1)S(1)}, u32[]{:S(2)}, u32[]{:S(2)}) %collective-permute-start.7) | collective-permute-done | bytes 131104 | tf_op jit(solution)/shard_map/ppermute | solution.py:417
  43.4 1.5 %project.1 = (f32[32,1280]{1,0:T(8,128)S(1)}, bf16[32,1280]{1,0:T(8,128)(2,1)S(1)}, bf16[32,1280]{1,0:T(8,128)(2,1)S(1)}, bf16[32,1280]{1,0:T(8,128)(2,1)S(1)}) custom-call(s32[2]{0:T(128)S(1)} %pad_add_fusion.me_ref.at_ref, bf16[32,2048]{1,0:T(8,128)(2,1)S(1)} %convolution_convert_fusion.after_ref.refs_0_, ...), custom_call_target="tpu_custom_call" | custom-call | tf_op jit(solution)/shard_map/project/pallas_call | solution.py:315
  46.1 1.4 %collective-permute-start.11 = (bf16[32,1280]{1,0:T(8,128)(2,1)S(1)}, bf16[32,1280]{1,0:T(8,128)(2,1)S(1)}, u32[]{:S(2)}, u32[]{:S(2)}) collective-permute-start(bf16[32,1280]{1,0:T(8,128)(2,1)S(1)} %get-tuple-element.55), channel_id=1, source_target_pairs={{0,3},{1,0},{2,1},{3,2},{4,7},{5,4},{6,5},{7,6},{8,11},{9,8},{10,9... | collective-permute-start | bytes 245768 | tf_op jit(solution)/shard_map/ppermute | solution.py:417
  47.5 1.6 %collective-permute-done.9 = bf16[32,1280]{1,0:T(8,128)(2,1)S(1)} collective-permute-done((bf16[32,1280]{1,0:T(8,128)(2,1)S(1)}, bf16[32,1280]{1,0:T(8,128)(2,1)S(1)}, u32[]{:S(2)}, u32[]{:S(2)}) %collective-permute-start.9) | collective-permute-done | bytes 81952 | tf_op jit(solution)/shard_map/ppermute | solution.py:417
  50.8 1.9 %collective-permute-start.19 = (bf16[32,1280]{1,0:T(8,128)(2,1)S(1)}, bf16[32,1280]{1,0:T(8,128)(2,1)S(1)}, u32[]{:S(2)}, u32[]{:S(2)}) collective-permute-start(bf16[32,1280]{1,0:T(8,128)(2,1)S(1)} %add_convert_fusion.refs_0_), channel_id=1, source_target_pairs={{0,8},{4,12},{8,0},{12,4},{1,9},{5,13},{9,1},{13,5},{2,10},{6,14},... | collective-permute-start | bytes 245768 | tf_op jit(solution)/shard_map/ppermute | solution.py:417
  52.7 1.9 %collective-permute-start.15 = (bf16[32,1280]{1,0:T(8,128)(2,1)S(1)}, bf16[32,1280]{1,0:T(8,128)(2,1)S(1)}, u32[]{:S(2)}, u32[]{:S(2)}) collective-permute-start(bf16[32,1280]{1,0:T(8,128)(2,1)S(1)} %add_convert_fusion.refs_0_), channel_id=1, source_target_pairs={{0,4},{4,8},{8,12},{12,0},{1,5},{5,9},{9,13},{13,1},{2,6},{6,10},{... | collective-permute-start | bytes 245768 | tf_op jit(solution)/shard_map/ppermute | solution.py:417
  57.4 3.6 %collective-permute-start.24 = (bf16[32,1280]{1,0:T(8,128)(2,1)S(1)}, bf16[32,1280]{1,0:T(8,128)(2,1)S(1)}, u32[]{:S(2)}, u32[]{:S(2)}) collective-permute-start(bf16[32,1280]{1,0:T(8,128)(2,1)S(1)} %collective-permute-done.23.refs_12_), channel_id=1, source_target_pairs={{0,1},{1,0},{2,3},{3,2},{4,5},{5,4},{6,7},{7,6},{8,9},{9,8},{10,11... | collective-permute-start | bytes 245768 | tf_op jit(solution)/shard_map/ppermute | solution.py:421
  63.7 2.2 %collective-permute-done.21.refs_10_ = bf16[32,1280]{1,0:T(8,128)(2,1)S(1)} collective-permute-done((bf16[32,1280]{1,0:T(8,128)(2,1)S(1)}, bf16[32,1280]{1,0:T(8,128)(2,1)S(1)}, u32[]{:S(2)}, u32[]{:S(2)}) %collective-permute-start.21) | collective-permute-done | bytes 81952 | tf_op jit(solution)/shard_map/ppermute | solution.py:421
  68.5 9.5 %swiglu.1 = (f32[64,1280]{1,0:T(8,128)S(1)}, f32[64,1280]{1,0:T(8,128)S(1)}, f32[64,1280]{1,0:T(8,128)S(1)}, f32[64,1280]{1,0:T(8,128)S(1)}, bf16[64,1280]{1,0:T...) custom-call(s32[2]{0:T(128)S(1)} %pad_add_fusion.me_ref.at_ref, ...), custom_call_target="tpu_custom_call" | custom-call | tf_op jit(solution)/shard_map/swiglu/pallas_call | solution.py:398
  84.9 1.4 %collective-permute-start.29 = (bf16[32,1280]{1,0:T(8,128)(2,1)S(1)}, bf16[32,1280]{1,0:T(8,128)(2,1)S(1)}, u32[]{:S(2)}, u32[]{:S(2)}) collective-permute-start(bf16[32,1280]{1,0:T(8,128)(2,1)S(1)} %fusion.11), channel_id=1, source_target_pairs={{0,8},{4,12},{8,0},{12,4},{1,9},{5,13},{9,1},{13,5},{2,10},{6,14},... | collective-permute-start | bytes 245768 | tf_op jit(solution)/shard_map/ppermute | solution.py:417
  86.7 1.7 %collective-permute-done.34 = bf16[32,1280]{1,0:T(8,128)(2,1)S(1)} collective-permute-done((bf16[32,1280]{1,0:T(8,128)(2,1)S(1)}, bf16[32,1280]{1,0:T(8,128)(2,1)S(1)}, u32[]{:S(2)}, u32[]{:S(2)}) %collective-permute-start.34) | collective-permute-done | bytes 81952 | tf_op jit(solution)/shard_map/ppermute | solution.py:421
  88.4 2.2 %collective-permute-start.35 = (bf16[32,1280]{1,0:T(8,128)(2,1)S(1)}, bf16[32,1280]{1,0:T(8,128)(2,1)S(1)}, u32[]{:S(2)}, u32[]{:S(2)}) collective-permute-start(bf16[32,1280]{1,0:T(8,128)(2,1)S(1)} %fusion.9), channel_id=1, source_target_pairs={{0,12},{4,0},{8,4},{12,8},{1,13},{5,1},{9,5},{13,9},{2,14},{6,2},{... | collective-permute-start | bytes 245768 | tf_op jit(solution)/shard_map/ppermute | solution.py:417
  (79 shorter events, 23.0 us)
Async XLA Ops:
  2.0 10.4 %collective-permute-start = (bf16[16,2176]{1,0:T(8,128)(2,1)S(1)}, bf16[16,2176]{1,0:T(8,128)(2,1)S(1)}, u32[]{:S(2)}, u32[]{:S(2)}) collective-permute-start(bf16[16,2176]{1,0:T(8,128)(2,1)S(1)} %get-tuple-element.38), channel_id=1, source_target_pairs={{0,4},{4,8},{8,12},{12,0},{1,5},{5,9},{9,13},{13,1},{2,6},{6,10},{... | collective-permute-start | bytes 208904 | tf_op jit(solution)/shard_map/ppermute | solution.py:417
  5.0 7.4 %collective-permute-start.1 = (bf16[16,2176]{1,0:T(8,128)(2,1)S(1)}, bf16[16,2176]{1,0:T(8,128)(2,1)S(1)}, u32[]{:S(2)}, u32[]{:S(2)}) collective-permute-start(bf16[16,2176]{1,0:T(8,128)(2,1)S(1)} %get-tuple-element.39), channel_id=1, source_target_pairs={{0,8},{4,12},{8,0},{12,4},{1,9},{5,13},{9,1},{13,5},{2,10},{6,14},... | collective-permute-start | bytes 208904 | tf_op jit(solution)/shard_map/ppermute | solution.py:417
  7.6 4.9 %collective-permute-start.2 = (bf16[16,2176]{1,0:T(8,128)(2,1)S(1)}, bf16[16,2176]{1,0:T(8,128)(2,1)S(1)}, u32[]{:S(2)}, u32[]{:S(2)}) collective-permute-start(bf16[16,2176]{1,0:T(8,128)(2,1)S(1)} %get-tuple-element.40), channel_id=1, source_target_pairs={{0,12},{4,0},{8,4},{12,8},{1,13},{5,1},{9,5},{13,9},{2,14},{6,2},{... | collective-permute-start | bytes 208904 | tf_op jit(solution)/shard_map/ppermute | solution.py:417
  22.4 7.4 %collective-permute-start.4 = (bf16[16,2048]{1,0:T(8,128)(2,1)S(1)}, bf16[16,2048]{1,0:T(8,128)(2,1)S(1)}, u32[]{:S(2)}, u32[]{:S(2)}) collective-permute-start(bf16[16,2048]{1,0:T(8,128)(2,1)S(1)} %get-tuple-element.43), channel_id=1, source_target_pairs={{0,8},{4,12},{8,0},{12,4},{1,9},{5,13},{9,1},{13,5},{2,10},{6,14},... | collective-permute-start | bytes 196616 | tf_op jit(solution)/shard_map/ppermute | solution.py:417
  22.5 7.4 %collective-permute-start.5 = (bf16[16,2048]{1,0:T(8,128)(2,1)S(1)}, bf16[16,2048]{1,0:T(8,128)(2,1)S(1)}, u32[]{:S(2)}, u32[]{:S(2)}) collective-permute-start(bf16[16,2048]{1,0:T(8,128)(2,1)S(1)} %get-tuple-element.44), channel_id=1, source_target_pairs={{0,4},{4,8},{8,12},{12,0},{1,5},{5,9},{9,13},{13,1},{2,6},{6,10},{... | collective-permute-start | bytes 196616 | tf_op jit(solution)/shard_map/ppermute | solution.py:417
  30.1 10.3 %collective-permute-start.8 = (bf16[32,2048]{1,0:T(8,128)(2,1)S(1)}, bf16[32,2048]{1,0:T(8,128)(2,1)S(1)}, u32[]{:S(2)}, u32[]{:S(2)}) collective-permute-start(bf16[32,2048]{1,0:T(8,128)(2,1)S(1)} %convolution_convert_fusion.after_ref.refs_0_), channel_id=1, source_target_pairs={{0,12},{4,0},{8,4},{12,8},{1,13},{5,1},{9,5},{13,9},{2,14},{6,2},{... | collective-permute-start | bytes 393224 | tf_op jit(solution)/shard_map/ppermute | solution.py:417
  31.5 11.9 %collective-permute-start.7 = (bf16[32,2048]{1,0:T(8,128)(2,1)S(1)}, bf16[32,2048]{1,0:T(8,128)(2,1)S(1)}, u32[]{:S(2)}, u32[]{:S(2)}) collective-permute-start(bf16[32,2048]{1,0:T(8,128)(2,1)S(1)} %convolution_convert_fusion.after_ref.refs_0_), channel_id=1, source_target_pairs={{0,8},{4,12},{8,0},{12,4},{1,9},{5,13},{9,1},{13,5},{2,10},{6,14},... | collective-permute-start | bytes 393224 | tf_op jit(solution)/shard_map/ppermute | solution.py:417
  31.5 11.9 %collective-permute-start.6 = (bf16[32,2048]{1,0:T(8,128)(2,1)S(1)}, bf16[32,2048]{1,0:T(8,128)(2,1)S(1)}, u32[]{:S(2)}, u32[]{:S(2)}) collective-permute-start(bf16[32,2048]{1,0:T(8,128)(2,1)S(1)} %convolution_convert_fusion.after_ref.refs_0_), channel_id=1, source_target_pairs={{0,4},{4,8},{8,12},{12,0},{1,5},{5,9},{9,13},{13,1},{2,6},{6,10},{... | collective-permute-start | bytes 393224 | tf_op jit(solution)/shard_map/ppermute | solution.py:417
  45.0 5.3 %collective-permute-start.10 = (bf16[32,1280]{1,0:T(8,128)(2,1)S(1)}, bf16[32,1280]{1,0:T(8,128)(2,1)S(1)}, u32[]{:S(2)}, u32[]{:S(2)}) collective-permute-start(bf16[32,1280]{1,0:T(8,128)(2,1)S(1)} %get-tuple-element.54), channel_id=1, source_target_pairs={{0,2},{1,3},{2,0},{3,1},{4,6},{5,7},{6,4},{7,5},{8,10},{9,11},{10,... | collective-permute-start | bytes 245768 | tf_op jit(solution)/shard_map/ppermute | solution.py:417
  50.4 5.5 %collective-permute-start.23 = (bf16[32,1280]{1,0:T(8,128)(2,1)S(1)}, bf16[32,1280]{1,0:T(8,128)(2,1)S(1)}, u32[]{:S(2)}, u32[]{:S(2)}) collective-permute-start(bf16[32,1280]{1,0:T(8,128)(2,1)S(1)} %add_convert_fusion.refs_0_), channel_id=1, source_target_pairs={{0,12},{4,0},{8,4},{12,8},{1,13},{5,1},{9,5},{13,9},{2,14},{6,2},{... | collective-permute-start | bytes 245768 | tf_op jit(solution)/shard_map/ppermute | solution.py:417
  50.8 6.6 %collective-permute-start.19 = (bf16[32,1280]{1,0:T(8,128)(2,1)S(1)}, bf16[32,1280]{1,0:T(8,128)(2,1)S(1)}, u32[]{:S(2)}, u32[]{:S(2)}) collective-permute-start(bf16[32,1280]{1,0:T(8,128)(2,1)S(1)} %add_convert_fusion.refs_0_), channel_id=1, source_target_pairs={{0,8},{4,12},{8,0},{12,4},{1,9},{5,13},{9,1},{13,5},{2,10},{6,14},... | collective-permute-start | bytes 245768 | tf_op jit(solution)/shard_map/ppermute | solution.py:417
  52.7 8.4 %collective-permute-start.15 = (bf16[32,1280]{1,0:T(8,128)(2,1)S(1)}, bf16[32,1280]{1,0:T(8,128)(2,1)S(1)}, u32[]{:S(2)}, u32[]{:S(2)}) collective-permute-start(bf16[32,1280]{1,0:T(8,128)(2,1)S(1)} %add_convert_fusion.refs_0_), channel_id=1, source_target_pairs={{0,4},{4,8},{8,12},{12,0},{1,5},{5,9},{9,13},{13,1},{2,6},{6,10},{... | collective-permute-start | bytes 245768 | tf_op jit(solution)/shard_map/ppermute | solution.py:417
  54.6 7.4 %collective-permute-start.13 = (bf16[32,1280]{1,0:T(8,128)(2,1)S(1)}, bf16[32,1280]{1,0:T(8,128)(2,1)S(1)}, u32[]{:S(2)}, u32[]{:S(2)}) collective-permute-start(bf16[32,1280]{1,0:T(8,128)(2,1)S(1)} %add_convert_fusion.refs_0_), channel_id=1, source_target_pairs={{0,2},{1,3},{2,0},{3,1},{4,6},{5,7},{6,4},{7,5},{8,10},{9,11},{10,... | collective-permute-start | bytes 245768 | tf_op jit(solution)/shard_map/ppermute | solution.py:421
  55.7 6.4 %collective-permute-start.12 = (bf16[32,1280]{1,0:T(8,128)(2,1)S(1)}, bf16[32,1280]{1,0:T(8,128)(2,1)S(1)}, u32[]{:S(2)}, u32[]{:S(2)}) collective-permute-start(bf16[32,1280]{1,0:T(8,128)(2,1)S(1)} %add_convert_fusion.refs_0_), channel_id=1, source_target_pairs={{0,1},{1,0},{2,3},{3,2},{4,5},{5,4},{6,7},{7,6},{8,9},{9,8},{10,11... | collective-permute-start | bytes 245768 | tf_op jit(solution)/shard_map/ppermute | solution.py:421
  55.9 7.2 %collective-permute-start.25 = (bf16[32,1280]{1,0:T(8,128)(2,1)S(1)}, bf16[32,1280]{1,0:T(8,128)(2,1)S(1)}, u32[]{:S(2)}, u32[]{:S(2)}) collective-permute-start(bf16[32,1280]{1,0:T(8,128)(2,1)S(1)} %collective-permute-done.23.refs_12_), channel_id=1, source_target_pairs={{0,2},{1,3},{2,0},{3,1},{4,6},{5,7},{6,4},{7,5},{8,10},{9,11},{10,... | collective-permute-start | bytes 245768 | tf_op jit(solution)/shard_map/ppermute | solution.py:421
  57.4 5.9 %collective-permute-start.24 = (bf16[32,1280]{1,0:T(8,128)(2,1)S(1)}, bf16[32,1280]{1,0:T(8,128)(2,1)S(1)}, u32[]{:S(2)}, u32[]{:S(2)}) collective-permute-start(bf16[32,1280]{1,0:T(8,128)(2,1)S(1)} %collective-permute-done.23.refs_12_), channel_id=1, source_target_pairs={{0,1},{1,0},{2,3},{3,2},{4,5},{5,4},{6,7},{7,6},{8,9},{9,8},{10,11... | collective-permute-start | bytes 245768 | tf_op jit(solution)/shard_map/ppermute | solution.py:421
  62.1 5.2 %collective-permute-start.17 = (bf16[32,1280]{1,0:T(8,128)(2,1)S(1)}, bf16[32,1280]{1,0:T(8,128)(2,1)S(1)}, u32[]{:S(2)}, u32[]{:S(2)}) collective-permute-start(bf16[32,1280]{1,0:T(8,128)(2,1)S(1)} %collective-permute-done.15.refs_4_), channel_id=1, source_target_pairs={{0,2},{1,3},{2,0},{3,1},{4,6},{5,7},{6,4},{7,5},{8,10},{9,11},{10,... | collective-permute-start | bytes 245768 | tf_op jit(solution)/shard_map/ppermute | solution.py:421
  79.5 5.4 %collective-permute-start.28 = (bf16[32,1280]{1,0:T(8,128)(2,1)S(1)}, bf16[32,1280]{1,0:T(8,128)(2,1)S(1)}, u32[]{:S(2)}, u32[]{:S(2)}) collective-permute-start(bf16[32,1280]{1,0:T(8,128)(2,1)S(1)} %slice.65), channel_id=1, source_target_pairs={{0,2},{1,3},{2,0},{3,1},{4,6},{5,7},{6,4},{7,5},{8,10},{9,11},{10,... | collective-permute-start | bytes 245768 | tf_op jit(solution)/shard_map/ppermute | solution.py:421
  80.7 6.0 %collective-permute-start.31 = (bf16[32,1280]{1,0:T(8,128)(2,1)S(1)}, bf16[32,1280]{1,0:T(8,128)(2,1)S(1)}, u32[]{:S(2)}, u32[]{:S(2)}) collective-permute-start(bf16[32,1280]{1,0:T(8,128)(2,1)S(1)} %slice.64), channel_id=1, source_target_pairs={{0,2},{1,3},{2,0},{3,1},{4,6},{5,7},{6,4},{7,5},{8,10},{9,11},{10,... | collective-permute-start | bytes 245768 | tf_op jit(solution)/shard_map/ppermute | solution.py:421
  81.8 6.6 %collective-permute-start.34 = (bf16[32,1280]{1,0:T(8,128)(2,1)S(1)}, bf16[32,1280]{1,0:T(8,128)(2,1)S(1)}, u32[]{:S(2)}, u32[]{:S(2)}) collective-permute-start(bf16[32,1280]{1,0:T(8,128)(2,1)S(1)} %slice.63), channel_id=1, source_target_pairs={{0,2},{1,3},{2,0},{3,1},{4,6},{5,7},{6,4},{7,5},{8,10},{9,11},{10,... | collective-permute-start | bytes 245768 | tf_op jit(solution)/shard_map/ppermute | solution.py:421
  82.9 7.7 %collective-permute-start.37 = (bf16[32,1280]{1,0:T(8,128)(2,1)S(1)}, bf16[32,1280]{1,0:T(8,128)(2,1)S(1)}, u32[]{:S(2)}, u32[]{:S(2)}) collective-permute-start(bf16[32,1280]{1,0:T(8,128)(2,1)S(1)} %slice.62), channel_id=1, source_target_pairs={{0,2},{1,3},{2,0},{3,1},{4,6},{5,7},{6,4},{7,5},{8,10},{9,11},{10,... | collective-permute-start | bytes 245768 | tf_op jit(solution)/shard_map/ppermute | solution.py:421
  84.9 7.0 %collective-permute-start.29 = (bf16[32,1280]{1,0:T(8,128)(2,1)S(1)}, bf16[32,1280]{1,0:T(8,128)(2,1)S(1)}, u32[]{:S(2)}, u32[]{:S(2)}) collective-permute-start(bf16[32,1280]{1,0:T(8,128)(2,1)S(1)} %fusion.11), channel_id=1, source_target_pairs={{0,8},{4,12},{8,0},{12,4},{1,9},{5,13},{9,1},{13,5},{2,10},{6,14},... | collective-permute-start | bytes 245768 | tf_op jit(solution)/shard_map/ppermute | solution.py:417
  86.6 6.5 %collective-permute-start.32 = (bf16[32,1280]{1,0:T(8,128)(2,1)S(1)}, bf16[32,1280]{1,0:T(8,128)(2,1)S(1)}, u32[]{:S(2)}, u32[]{:S(2)}) collective-permute-start(bf16[32,1280]{1,0:T(8,128)(2,1)S(1)} %fusion.10), channel_id=1, source_target_pairs={{0,4},{4,8},{8,12},{12,0},{1,5},{5,9},{9,13},{13,1},{2,6},{6,10},{... | collective-permute-start | bytes 245768 | tf_op jit(solution)/shard_map/ppermute | solution.py:417
  88.4 5.5 %collective-permute-start.35 = (bf16[32,1280]{1,0:T(8,128)(2,1)S(1)}, bf16[32,1280]{1,0:T(8,128)(2,1)S(1)}, u32[]{:S(2)}, u32[]{:S(2)}) collective-permute-start(bf16[32,1280]{1,0:T(8,128)(2,1)S(1)} %fusion.9), channel_id=1, source_target_pairs={{0,12},{4,0},{8,4},{12,8},{1,13},{5,1},{9,5},{13,9},{2,14},{6,2},{... | collective-permute-start | bytes 245768 | tf_op jit(solution)/shard_map/ppermute | solution.py:417
  (17 other events, 116.4 us)

commit v5 on v4

--- a/solution.py
+++ b/solution.py
@@ -329,65 +329,44 @@
 
 
 def swiglu_kernel(row_devs, head_devs, at_ref, gain_ref, *refs):
-    pieces = refs[: row_devs * head_devs]
-    gate_ref, up_ref, down_ref = refs[row_devs * head_devs : row_devs * head_devs + 3]
-    outs = refs[row_devs * head_devs + 3 :]
-    keep_refs, send_refs = outs[:row_devs], outs[row_devs : 2 * row_devs]
-    x, inner, y = outs[2 * row_devs :]
+    count = row_devs * head_devs
+    pieces, refs = refs[:count], refs[count:]
+    gate_ref, up_ref, down_ref = refs[:3]
+    keep_refs, send_refs = refs[3 : 3 + row_devs], refs[3 + row_devs : 3 + 2 * row_devs]
+    x, inner = refs[3 + 2 * row_devs :]
     rows, cols = pieces[0].shape
-    tall = x.shape[1]
-    hidden = gate_ref.shape[1]
-    steps = hidden // hidden_tile
-
-    me_row, me_head = at_ref[0], at_ref[1]
-
-    def flip(j):
-        return me_head + (j & 1) * (1 - 2 * lax.rem(me_head, 2)) + (j & 2) * (1 - lax.rem(lax.div(me_head, 2), 2) * 2)
-
-    def start_of(j):
-        return pl.multiple_of(flip(j) * rows, rows)
-
-    def behind(s):
-        source = me_row - s
-        return jnp.where(source < 0, source + row_devs, source)
-
-    for s in range(row_devs):
-        for j in range(head_devs):
-            x[behind(s), pl.ds(start_of(j), rows), :] = pieces[s * head_devs + j][...]
-    squares = jnp.zeros((tall, 1), f32)
-    for z in range(row_devs):
-        value = x[z].astype(f32)
-        squares = squares + jnp.sum(value * value, axis=1, keepdims=True)
-    inverse = lax.rsqrt(squares / (row_devs * cols) + norm_eps)
-    for z in range(row_devs):
-        x[z] = (x[z].astype(f32) * inverse * gain_ref[:, z * cols : (z + 1) * cols]).astype(bf16)
-
-    for j in range(steps):
-        cut = slice(j * hidden_tile, (j + 1) * hidden_tile)
+    tall, hidden = inner.shape
+    width = row_devs * cols
+    order = [*range(0, head_devs, 2), *range(1, head_devs, 2)]
+
+    def turned(n):
+        n = at_ref[0] + n % row_devs
+        n = jnp.where(n >= row_devs, n - row_devs, n)
+        return pl.multiple_of(n * cols, cols)
+
+    for at, j in enumerate(order):
+        values = [pieces[s * head_devs + j][...].astype(f32) for s in range(row_devs)]
+        squares = sum(jnp.sum(v * v, axis=1, keepdims=True) for v in values)
+        inverse = lax.rsqrt(squares / width + norm_eps)
+        for s in range(row_devs):
+            value = values[s] * inverse * gain_ref[:, pl.ds(turned(-s), cols)]
+            x[s, at * rows : (at + 1) * rows, :] = value.astype(bf16)
+
+    for c in range(0, hidden, hidden_tile):
+        cut = slice(c, c + hidden_tile)
         gate = jnp.zeros((tall, hidden_tile), f32)
         up = jnp.zeros((tall, hidden_tile), f32)
-        for z in range(row_devs):
-            gate = gate + mxu(x[z], gate_ref[z * cols : (z + 1) * cols, cut], (1, 0))
-            up = up + mxu(x[z], up_ref[z * cols : (z + 1) * cols, cut], (1, 0))
+        for s in range(row_devs):
+            gate = gate + mxu(x[s], gate_ref[pl.ds(turned(-s), cols), cut], (1, 0))
+            up = up + mxu(x[s], up_ref[pl.ds(turned(-s), cols), cut], (1, 0))
         inner[:, cut] = (gate / (1.0 + jnp.exp(-gate)) * up).astype(bf16)
 
     for i in range(row_devs):
-        @pl.loop(0, cols // hidden_tile)
-        def _(t):
-            cut = pl.ds(pl.multiple_of(t * hidden_tile, hidden_tile), hidden_tile)
-            from_cut = pl.ds(pl.multiple_of(i * cols + t * hidden_tile, hidden_tile), hidden_tile)
-            y[i, :, cut] = mxu(inner[...], down_ref[:, from_cut], (1, 0))
-
-    for i in range(row_devs):
-        target = me_row + i
-        target = jnp.where(target >= row_devs, target - row_devs, target)
-        for j in range(head_devs):
-            value = y[target, pl.ds(start_of(j), rows), :]
-            half = slice((j // 2) * rows, (j // 2 + 1) * rows)
-            if j % 2 == 0:
-                keep_refs[i][half, :] = value
-            else:
-                send_refs[i][half, :] = value.astype(bf16)
+        for c in range(0, cols, hidden_tile):
+            cut = slice(c, c + hidden_tile)
+            y = mxu(inner[...], down_ref[:, pl.ds(pl.multiple_of(turned(i) + c, hidden_tile), hidden_tile)], (1, 0))
+            keep_refs[i][:, cut] = y[: tall // 2]
+            send_refs[i][:, cut] = y[tall // 2 :].astype(bf16)
 
 
 def swiglu(at, pieces, gain, w_gate, w_up, w_down, row_devs, head_devs):
@@ -404,7 +383,6 @@
         scratch_shapes=[
             pltpu.VMEM((row_devs, tall, cols), bf16),
             pltpu.VMEM((tall, hidden), bf16),
-            pltpu.VMEM((row_devs, tall, cols), f32),
         ],
         compiler_params=pltpu.CompilerParams(vmem_limit_bytes=12 * mib),
         name="swiglu",

time: 94.5 us -> 90.6 us (0.959)
  Pallas kernels: 32.6 us -> 26.1 us
  starting transfers between devices: 37 us -> 38.4 us
    pallas_call x1, Pallas kernels: 9.47 us -> 5.66 us  [swiglu(): pl.pallas_call(functools.partial(swiglu_kernel, row_devs, head_devs), out...]
    pallas_call x1, Pallas kernels: 9.34 us -> 6.65 us  [attend(): pl.pallas_call(functools.partial(attend_kernel, count, len(later), listed...]
    ppermute x18, starting transfers between devices: 22.8 us -> 25.4 us  [shift(): return lax.ppermute(x, axis, [(i, (i + step) % n) for i in range(n)])]
    ppermute x20, starting transfers between devices: 14.2 us -> 13 us  [swap(): lax.ppermute(x, axis, [(i, i ^ flip) for i in range(lax.axis_size(axis))])]
  transfers between devices with their start and end apart: 38 -> 38, of which waited for: 18 -> 17; matrix products, arithmetic and copies ran while one was open for 0% -> 0% of each run, Pallas kernels for 11% -> 11%
where the time goes in v5:
time: 90.6 us; the launch traced here: 90.3 us
  starting transfers between devices  38.4 us (42%)
  Pallas kernels  26.1 us (29%)
  waiting for transfers between devices  24.4 us (27%)
  other arithmetic  1.03 us (1%)
    ppermute x18, starting transfers between devices, shift(): return lax.ppermute(x, axis, [(i, (i + step) % n) for i in range(n)])  25.4 us
    ppermute x18, waiting for transfers between devices, shift(): return lax.ppermute(x, axis, [(i, (i + step) % n) for i in range(n)])  16.8 us
    ppermute x20, starting transfers between devices, swap(): lax.ppermute(x, axis, [(i, i ^ flip) for i in range(lax.axis_size(axis))])  13 us
    pallas_call x2, Pallas kernels, fetch(): pl.pallas_call(functools.partial(fetch_kernel, count), out_shape=[pltpu.V...  10.4 us
    ppermute x20, waiting for transfers between devices, swap(): lax.ppermute(x, axis, [(i, i ^ flip) for i in range(lax.axis_size(axis))])  7.51 us
    pallas_call x1, Pallas kernels, attend(): pl.pallas_call(functools.partial(attend_kernel, count, len(later), listed...  6.65 us
    pallas_call x1, Pallas kernels, swiglu(): pl.pallas_call(functools.partial(swiglu_kernel, row_devs, head_devs), out...  5.66 us
    pallas_call x1, Pallas kernels, dispatch(): pl.pallas_call(functools.partial(dispatch_kernel, blocks_dev), out_shape=...  1.89 us
  transfers between devices with their start and end apart: 38, of which 17 were waited for; matrix products, arithmetic and copies ran while one was open for 0% of the time, Pallas kernels for 11%

profile of v5, /device:TPU:0, one launch (start us, length us, event | category | flops | bytes accessed | tf_op | source)
XLA Modules:
  0.0 90.3 jit_solution(684606833466110325)
XLA Ops:
  0.1 1.9 %dispatch.1 = (bf16[32,64]{1,0:T(8,128)(2,1)S(1)}, bf16[16,2176]{1,0:T(8,128)(2,1)S(1)}, bf16[16,2176]{1,0:T(8,128)(2,1)S(1)}, bf16[16,2176]{1,0:T(8,128)(2,1)S(1)}, bf16[16,2176]{1,0:T(8,128)(2,1)S(1)}) custom-call(s32[2]{0:T(128)S(1)} %pad_add_fusion.me_ref.at_ref, s32[32,32]{1,0:T(8,128)} %ids_hbm.1, s32[1,32]{1,0:T(1,128)} %bitcast.6, bf16[32,2048]{1,0:T(8,128)(2,1)} %q_hbm.1), custom_call_target="tpu_custom_call" | custom-call | tf_op jit(solution)/shard_map/dispatch/pallas_call | solution.py:108
  2.0 3.1 %collective-permute-start = (bf16[16,2176]{1,0:T(8,128)(2,1)S(1)}, bf16[16,2176]{1,0:T(8,128)(2,1)S(1)}, u32[]{:S(2)}, u32[]{:S(2)}) collective-permute-start(bf16[16,2176]{1,0:T(8,128)(2,1)S(1)} %get-tuple-element.38), channel_id=1, source_target_pairs={{0,4},{4,8},{8,12},{12,0},{1,5},{5,9},{9,13},{13,1},{2,6},{6,10},{... | collective-permute-start | bytes 208904 | tf_op jit(solution)/shard_map/ppermute | solution.py:395
  5.0 2.6 %collective-permute-start.1 = (bf16[16,2176]{1,0:T(8,128)(2,1)S(1)}, bf16[16,2176]{1,0:T(8,128)(2,1)S(1)}, u32[]{:S(2)}, u32[]{:S(2)}) collective-permute-start(bf16[16,2176]{1,0:T(8,128)(2,1)S(1)} %get-tuple-element.39), channel_id=1, source_target_pairs={{0,8},{4,12},{8,0},{12,4},{1,9},{5,13},{9,1},{13,5},{2,10},{6,14},... | collective-permute-start | bytes 208904 | tf_op jit(solution)/shard_map/ppermute | solution.py:395
  7.6 1.3 %collective-permute-start.2 = (bf16[16,2176]{1,0:T(8,128)(2,1)S(1)}, bf16[16,2176]{1,0:T(8,128)(2,1)S(1)}, u32[]{:S(2)}, u32[]{:S(2)}) collective-permute-start(bf16[16,2176]{1,0:T(8,128)(2,1)S(1)} %get-tuple-element.40), channel_id=1, source_target_pairs={{0,12},{4,0},{8,4},{12,8},{1,13},{5,1},{9,5},{13,9},{2,14},{6,2},{... | collective-permute-start | bytes 208904 | tf_op jit(solution)/shard_map/ppermute | solution.py:395
  9.0 3.4 %fetch.2.kv = bf16[64,2,2,128,128]{4,3,2,1,0:T(8,128)(2,1)S(1)} custom-call(bf16[32,64]{1,0:T(8,128)(2,1)S(1)} %get-tuple-element.36.after_ref, bf16[64,2,2,128,128]{4,3,2,1,0:T(8,128)(2,1)} %refs_0_.2), custom_call_target="tpu_custom_call" | custom-call | bytes 8388608 | tf_op jit(solution)/shard_map/fetch/pallas_call | solution.py:46
  12.5 6.6 %attend.1 = (bf16[16,2048]{1,0:T(8,128)(2,1)S(1)}, bf16[16,2048]{1,0:T(8,128)(2,1)S(1)}, bf16[16,2048]{1,0:T(8,128)(2,1)S(1)}, bf16[16,2048]{1,0:T(8,128)(2,1)S(...) custom-call(f32[2,2]{1,0:T(2,128)S(1)} %copy-done.1, bf16[64,2,2,128,128]{4,3,2,1,0:T(8,128)(2,1)S(1)} %fetch.2.kv, ...), custom_call_target="tpu_custom_call" | custom-call | tf_op jit(solution)/shard_map/attend/pallas_call | solution.py:263
  19.2 3.2 %collective-permute-start.3 = (bf16[16,2048]{1,0:T(8,128)(2,1)S(1)}, bf16[16,2048]{1,0:T(8,128)(2,1)S(1)}, u32[]{:S(2)}, u32[]{:S(2)}) collective-permute-start(bf16[16,2048]{1,0:T(8,128)(2,1)S(1)} %get-tuple-element.42), channel_id=1, source_target_pairs={{0,12},{4,0},{8,4},{12,8},{1,13},{5,1},{9,5},{13,9},{2,14},{6,2},{... | collective-permute-start | bytes 196616 | tf_op jit(solution)/shard_map/ppermute | solution.py:395
  22.4 2.7 %collective-permute-start.4 = (bf16[16,2048]{1,0:T(8,128)(2,1)S(1)}, bf16[16,2048]{1,0:T(8,128)(2,1)S(1)}, u32[]{:S(2)}, u32[]{:S(2)}) collective-permute-start(bf16[16,2048]{1,0:T(8,128)(2,1)S(1)} %get-tuple-element.43), channel_id=1, source_target_pairs={{0,8},{4,12},{8,0},{12,4},{1,9},{5,13},{9,1},{13,5},{2,10},{6,14},... | collective-permute-start | bytes 196616 | tf_op jit(solution)/shard_map/ppermute | solution.py:395
  26.0 5.4 %collective-permute-done.4 = bf16[16,2048]{1,0:T(8,128)(2,1)S(1)} collective-permute-done((bf16[16,2048]{1,0:T(8,128)(2,1)S(1)}, bf16[16,2048]{1,0:T(8,128)(2,1)S(1)}, u32[]{:S(2)}, u32[]{:S(2)}) %collective-permute-start.4) | collective-permute-done | bytes 65568 | tf_op jit(solution)/shard_map/ppermute | solution.py:395
  32.3 1.4 %collective-permute-start.6 = (bf16[32,2048]{1,0:T(8,128)(2,1)S(1)}, bf16[32,2048]{1,0:T(8,128)(2,1)S(1)}, u32[]{:S(2)}, u32[]{:S(2)}) collective-permute-start(bf16[32,2048]{1,0:T(8,128)(2,1)S(1)} %convolution_convert_fusion.after_ref.refs_0_), channel_id=1, source_target_pairs={{0,4},{4,8},{8,12},{12,0},{1,5},{5,9},{9,13},{13,1},{2,6},{6,10},{... | collective-permute-start | bytes 393224 | tf_op jit(solution)/shard_map/ppermute | solution.py:395
  33.7 7.0 %fetch.3 = (bf16[5120,1024]{1,0:T(8,128)(2,1)S(1)}, bf16[1024,5120]{1,0:T(8,128)(2,1)S(1)}) custom-call(bf16[32,2048]{1,0:T(8,128)(2,1)S(1)} %convolution_convert_fusion.after_ref.refs_0_, bf16[5120,1024]{1,0:T(8,128)(2,1)} %refs_0_.3, bf16[1024,5120]{1,0:T(8,128)(2,1)} %refs_1_.1), custom_call_target="tpu_custom_call" | custom-call | bytes 20971520 | tf_op jit(solution)/shard_map/fetch/pallas_call | solution.py:46
  40.7 2.6 %collective-permute-done.7.refs_2_ = bf16[32,2048]{1,0:T(8,128)(2,1)S(1)} collective-permute-done((bf16[32,2048]{1,0:T(8,128)(2,1)S(1)}, bf16[32,2048]{1,0:T(8,128)(2,1)S(1)}, u32[]{:S(2)}, u32[]{:S(2)}) %collective-permute-start.7) | collective-permute-done | bytes 131104 | tf_op jit(solution)/shard_map/ppermute | solution.py:395
  43.3 1.5 %project.1 = (f32[32,1280]{1,0:T(8,128)S(1)}, bf16[32,1280]{1,0:T(8,128)(2,1)S(1)}, bf16[32,1280]{1,0:T(8,128)(2,1)S(1)}, bf16[32,1280]{1,0:T(8,128)(2,1)S(1)}) custom-call(s32[2]{0:T(128)S(1)} %pad_add_fusion.me_ref.at_ref, bf16[32,2048]{1,0:T(8,128)(2,1)S(1)} %convolution_convert_fusion.after_ref.refs_0_, ...), custom_call_target="tpu_custom_call" | custom-call | tf_op jit(solution)/shard_map/project/pallas_call | solution.py:315
  46.2 1.4 %collective-permute-start.11 = (bf16[32,1280]{1,0:T(8,128)(2,1)S(1)}, bf16[32,1280]{1,0:T(8,128)(2,1)S(1)}, u32[]{:S(2)}, u32[]{:S(2)}) collective-permute-start(bf16[32,1280]{1,0:T(8,128)(2,1)S(1)} %get-tuple-element.55), channel_id=1, source_target_pairs={{0,3},{1,0},{2,1},{3,2},{4,7},{5,4},{6,5},{7,6},{8,11},{9,8},{10,9... | collective-permute-start | bytes 245768 | tf_op jit(solution)/shard_map/ppermute | solution.py:395
  47.6 1.5 %collective-permute-done.9 = bf16[32,1280]{1,0:T(8,128)(2,1)S(1)} collective-permute-done((bf16[32,1280]{1,0:T(8,128)(2,1)S(1)}, bf16[32,1280]{1,0:T(8,128)(2,1)S(1)}, u32[]{:S(2)}, u32[]{:S(2)}) %collective-permute-start.9) | collective-permute-done | bytes 81952 | tf_op jit(solution)/shard_map/ppermute | solution.py:395
  50.4 1.8 %collective-permute-start.19 = (bf16[32,1280]{1,0:T(8,128)(2,1)S(1)}, bf16[32,1280]{1,0:T(8,128)(2,1)S(1)}, u32[]{:S(2)}, u32[]{:S(2)}) collective-permute-start(bf16[32,1280]{1,0:T(8,128)(2,1)S(1)} %add_convert_fusion.refs_0_), channel_id=1, source_target_pairs={{0,8},{4,12},{8,0},{12,4},{1,9},{5,13},{9,1},{13,5},{2,10},{6,14},... | collective-permute-start | bytes 245768 | tf_op jit(solution)/shard_map/ppermute | solution.py:395
  52.2 1.9 %collective-permute-start.15 = (bf16[32,1280]{1,0:T(8,128)(2,1)S(1)}, bf16[32,1280]{1,0:T(8,128)(2,1)S(1)}, u32[]{:S(2)}, u32[]{:S(2)}) collective-permute-start(bf16[32,1280]{1,0:T(8,128)(2,1)S(1)} %add_convert_fusion.refs_0_), channel_id=1, source_target_pairs={{0,4},{4,8},{8,12},{12,0},{1,5},{5,9},{9,13},{13,1},{2,6},{6,10},{... | collective-permute-start | bytes 245768 | tf_op jit(solution)/shard_map/ppermute | solution.py:395
  55.3 1.9 %collective-permute-done.23.refs_12_ = bf16[32,1280]{1,0:T(8,128)(2,1)S(1)} collective-permute-done((bf16[32,1280]{1,0:T(8,128)(2,1)S(1)}, bf16[32,1280]{1,0:T(8,128)(2,1)S(1)}, u32[]{:S(2)}, u32[]{:S(2)}) %collective-permute-start.23) | collective-permute-done | bytes 81952 | tf_op jit(solution)/shard_map/ppermute | solution.py:395
  58.4 2.2 %collective-permute-start.24 = (bf16[32,1280]{1,0:T(8,128)(2,1)S(1)}, bf16[32,1280]{1,0:T(8,128)(2,1)S(1)}, u32[]{:S(2)}, u32[]{:S(2)}) collective-permute-start(bf16[32,1280]{1,0:T(8,128)(2,1)S(1)} %collective-permute-done.23.refs_12_), channel_id=1, source_target_pairs={{0,1},{1,0},{2,3},{3,2},{4,5},{5,4},{6,7},{7,6},{8,9},{9,8},{10,11... | collective-permute-start | bytes 245768 | tf_op jit(solution)/shard_map/ppermute | solution.py:399
  63.2 2.1 %collective-permute-done.21.refs_10_ = bf16[32,1280]{1,0:T(8,128)(2,1)S(1)} collective-permute-done((bf16[32,1280]{1,0:T(8,128)(2,1)S(1)}, bf16[32,1280]{1,0:T(8,128)(2,1)S(1)}, u32[]{:S(2)}, u32[]{:S(2)}) %collective-permute-start.21) | collective-permute-done | bytes 81952 | tf_op jit(solution)/shard_map/ppermute | solution.py:399
  68.0 5.7 %swiglu.1 = (f32[64,1280]{1,0:T(8,128)S(1)}, f32[64,1280]{1,0:T(8,128)S(1)}, f32[64,1280]{1,0:T(8,128)S(1)}, f32[64,1280]{1,0:T(8,128)S(1)}, bf16[64,1280]{1,0:T...) custom-call(s32[2]{0:T(128)S(1)} %pad_add_fusion.me_ref.at_ref, ...), custom_call_target="tpu_custom_call" | custom-call | tf_op jit(solution)/shard_map/swiglu/pallas_call | solution.py:377
  80.6 1.4 %collective-permute-start.29 = (bf16[32,1280]{1,0:T(8,128)(2,1)S(1)}, bf16[32,1280]{1,0:T(8,128)(2,1)S(1)}, u32[]{:S(2)}, u32[]{:S(2)}) collective-permute-start(bf16[32,1280]{1,0:T(8,128)(2,1)S(1)} %fusion.11), channel_id=1, source_target_pairs={{0,8},{4,12},{8,0},{12,4},{1,9},{5,13},{9,1},{13,5},{2,10},{6,14},... | collective-permute-start | bytes 245768 | tf_op jit(solution)/shard_map/ppermute | solution.py:395
  82.4 1.7 %collective-permute-done.34 = bf16[32,1280]{1,0:T(8,128)(2,1)S(1)} collective-permute-done((bf16[32,1280]{1,0:T(8,128)(2,1)S(1)}, bf16[32,1280]{1,0:T(8,128)(2,1)S(1)}, u32[]{:S(2)}, u32[]{:S(2)}) %collective-permute-start.34) | collective-permute-done | bytes 81952 | tf_op jit(solution)/shard_map/ppermute | solution.py:399
  84.1 2.2 %collective-permute-start.35 = (bf16[32,1280]{1,0:T(8,128)(2,1)S(1)}, bf16[32,1280]{1,0:T(8,128)(2,1)S(1)}, u32[]{:S(2)}, u32[]{:S(2)}) collective-permute-start(bf16[32,1280]{1,0:T(8,128)(2,1)S(1)} %fusion.9), channel_id=1, source_target_pairs={{0,12},{4,0},{8,4},{12,8},{1,13},{5,1},{9,5},{13,9},{2,14},{6,2},{... | collective-permute-start | bytes 245768 | tf_op jit(solution)/shard_map/ppermute | solution.py:395
  (79 shorter events, 23.5 us)
Async XLA Ops:
  2.0 10.4 %collective-permute-start = (bf16[16,2176]{1,0:T(8,128)(2,1)S(1)}, bf16[16,2176]{1,0:T(8,128)(2,1)S(1)}, u32[]{:S(2)}, u32[]{:S(2)}) collective-permute-start(bf16[16,2176]{1,0:T(8,128)(2,1)S(1)} %get-tuple-element.38), channel_id=1, source_target_pairs={{0,4},{4,8},{8,12},{12,0},{1,5},{5,9},{9,13},{13,1},{2,6},{6,10},{... | collective-permute-start | bytes 208904 | tf_op jit(solution)/shard_map/ppermute | solution.py:395
  5.0 7.4 %collective-permute-start.1 = (bf16[16,2176]{1,0:T(8,128)(2,1)S(1)}, bf16[16,2176]{1,0:T(8,128)(2,1)S(1)}, u32[]{:S(2)}, u32[]{:S(2)}) collective-permute-start(bf16[16,2176]{1,0:T(8,128)(2,1)S(1)} %get-tuple-element.39), channel_id=1, source_target_pairs={{0,8},{4,12},{8,0},{12,4},{1,9},{5,13},{9,1},{13,5},{2,10},{6,14},... | collective-permute-start | bytes 208904 | tf_op jit(solution)/shard_map/ppermute | solution.py:395
  7.6 4.9 %collective-permute-start.2 = (bf16[16,2176]{1,0:T(8,128)(2,1)S(1)}, bf16[16,2176]{1,0:T(8,128)(2,1)S(1)}, u32[]{:S(2)}, u32[]{:S(2)}) collective-permute-start(bf16[16,2176]{1,0:T(8,128)(2,1)S(1)} %get-tuple-element.40), channel_id=1, source_target_pairs={{0,12},{4,0},{8,4},{12,8},{1,13},{5,1},{9,5},{13,9},{2,14},{6,2},{... | collective-permute-start | bytes 208904 | tf_op jit(solution)/shard_map/ppermute | solution.py:395
  19.2 6.8 %collective-permute-start.3 = (bf16[16,2048]{1,0:T(8,128)(2,1)S(1)}, bf16[16,2048]{1,0:T(8,128)(2,1)S(1)}, u32[]{:S(2)}, u32[]{:S(2)}) collective-permute-start(bf16[16,2048]{1,0:T(8,128)(2,1)S(1)} %get-tuple-element.42), channel_id=1, source_target_pairs={{0,12},{4,0},{8,4},{12,8},{1,13},{5,1},{9,5},{13,9},{2,14},{6,2},{... | collective-permute-start | bytes 196616 | tf_op jit(solution)/shard_map/ppermute | solution.py:395
  22.4 8.9 %collective-permute-start.4 = (bf16[16,2048]{1,0:T(8,128)(2,1)S(1)}, bf16[16,2048]{1,0:T(8,128)(2,1)S(1)}, u32[]{:S(2)}, u32[]{:S(2)}) collective-permute-start(bf16[16,2048]{1,0:T(8,128)(2,1)S(1)} %get-tuple-element.43), channel_id=1, source_target_pairs={{0,8},{4,12},{8,0},{12,4},{1,9},{5,13},{9,1},{13,5},{2,10},{6,14},... | collective-permute-start | bytes 196616 | tf_op jit(solution)/shard_map/ppermute | solution.py:395
  25.2 6.2 %collective-permute-start.5 = (bf16[16,2048]{1,0:T(8,128)(2,1)S(1)}, bf16[16,2048]{1,0:T(8,128)(2,1)S(1)}, u32[]{:S(2)}, u32[]{:S(2)}) collective-permute-start(bf16[16,2048]{1,0:T(8,128)(2,1)S(1)} %get-tuple-element.44), channel_id=1, source_target_pairs={{0,4},{4,8},{8,12},{12,0},{1,5},{5,9},{9,13},{13,1},{2,6},{6,10},{... | collective-permute-start | bytes 196616 | tf_op jit(solution)/shard_map/ppermute | solution.py:395
  31.6 9.1 %collective-permute-start.8 = (bf16[32,2048]{1,0:T(8,128)(2,1)S(1)}, bf16[32,2048]{1,0:T(8,128)(2,1)S(1)}, u32[]{:S(2)}, u32[]{:S(2)}) collective-permute-start(bf16[32,2048]{1,0:T(8,128)(2,1)S(1)} %convolution_convert_fusion.after_ref.refs_0_), channel_id=1, source_target_pairs={{0,12},{4,0},{8,4},{12,8},{1,13},{5,1},{9,5},{13,9},{2,14},{6,2},{... | collective-permute-start | bytes 393224 | tf_op jit(solution)/shard_map/ppermute | solution.py:395
  31.8 11.5 %collective-permute-start.7 = (bf16[32,2048]{1,0:T(8,128)(2,1)S(1)}, bf16[32,2048]{1,0:T(8,128)(2,1)S(1)}, u32[]{:S(2)}, u32[]{:S(2)}) collective-permute-start(bf16[32,2048]{1,0:T(8,128)(2,1)S(1)} %convolution_convert_fusion.after_ref.refs_0_), channel_id=1, source_target_pairs={{0,8},{4,12},{8,0},{12,4},{1,9},{5,13},{9,1},{13,5},{2,10},{6,14},... | collective-permute-start | bytes 393224 | tf_op jit(solution)/shard_map/ppermute | solution.py:395
  32.3 11.1 %collective-permute-start.6 = (bf16[32,2048]{1,0:T(8,128)(2,1)S(1)}, bf16[32,2048]{1,0:T(8,128)(2,1)S(1)}, u32[]{:S(2)}, u32[]{:S(2)}) collective-permute-start(bf16[32,2048]{1,0:T(8,128)(2,1)S(1)} %convolution_convert_fusion.after_ref.refs_0_), channel_id=1, source_target_pairs={{0,4},{4,8},{8,12},{12,0},{1,5},{5,9},{9,13},{13,1},{2,6},{6,10},{... | collective-permute-start | bytes 393224 | tf_op jit(solution)/shard_map/ppermute | solution.py:395
  44.9 5.3 %collective-permute-start.10 = (bf16[32,1280]{1,0:T(8,128)(2,1)S(1)}, bf16[32,1280]{1,0:T(8,128)(2,1)S(1)}, u32[]{:S(2)}, u32[]{:S(2)}) collective-permute-start(bf16[32,1280]{1,0:T(8,128)(2,1)S(1)} %get-tuple-element.54), channel_id=1, source_target_pairs={{0,2},{1,3},{2,0},{3,1},{4,6},{5,7},{6,4},{7,5},{8,10},{9,11},{10,... | collective-permute-start | bytes 245768 | tf_op jit(solution)/shard_map/ppermute | solution.py:395
  50.3 6.9 %collective-permute-start.23 = (bf16[32,1280]{1,0:T(8,128)(2,1)S(1)}, bf16[32,1280]{1,0:T(8,128)(2,1)S(1)}, u32[]{:S(2)}, u32[]{:S(2)}) collective-permute-start(bf16[32,1280]{1,0:T(8,128)(2,1)S(1)} %add_convert_fusion.refs_0_), channel_id=1, source_target_pairs={{0,12},{4,0},{8,4},{12,8},{1,13},{5,1},{9,5},{13,9},{2,14},{6,2},{... | collective-permute-start | bytes 245768 | tf_op jit(solution)/shard_map/ppermute | solution.py:395
  50.4 8.0 %collective-permute-start.19 = (bf16[32,1280]{1,0:T(8,128)(2,1)S(1)}, bf16[32,1280]{1,0:T(8,128)(2,1)S(1)}, u32[]{:S(2)}, u32[]{:S(2)}) collective-permute-start(bf16[32,1280]{1,0:T(8,128)(2,1)S(1)} %add_convert_fusion.refs_0_), channel_id=1, source_target_pairs={{0,8},{4,12},{8,0},{12,4},{1,9},{5,13},{9,1},{13,5},{2,10},{6,14},... | collective-permute-start | bytes 245768 | tf_op jit(solution)/shard_map/ppermute | solution.py:395
  52.2 8.4 %collective-permute-start.15 = (bf16[32,1280]{1,0:T(8,128)(2,1)S(1)}, bf16[32,1280]{1,0:T(8,128)(2,1)S(1)}, u32[]{:S(2)}, u32[]{:S(2)}) collective-permute-start(bf16[32,1280]{1,0:T(8,128)(2,1)S(1)} %add_convert_fusion.refs_0_), channel_id=1, source_target_pairs={{0,4},{4,8},{8,12},{12,0},{1,5},{5,9},{9,13},{13,1},{2,6},{6,10},{... | collective-permute-start | bytes 245768 | tf_op jit(solution)/shard_map/ppermute | solution.py:395
  54.2 7.5 %collective-permute-start.13 = (bf16[32,1280]{1,0:T(8,128)(2,1)S(1)}, bf16[32,1280]{1,0:T(8,128)(2,1)S(1)}, u32[]{:S(2)}, u32[]{:S(2)}) collective-permute-start(bf16[32,1280]{1,0:T(8,128)(2,1)S(1)} %add_convert_fusion.refs_0_), channel_id=1, source_target_pairs={{0,2},{1,3},{2,0},{3,1},{4,6},{5,7},{6,4},{7,5},{8,10},{9,11},{10,... | collective-permute-start | bytes 245768 | tf_op jit(solution)/shard_map/ppermute | solution.py:399
  55.3 6.4 %collective-permute-start.12 = (bf16[32,1280]{1,0:T(8,128)(2,1)S(1)}, bf16[32,1280]{1,0:T(8,128)(2,1)S(1)}, u32[]{:S(2)}, u32[]{:S(2)}) collective-permute-start(bf16[32,1280]{1,0:T(8,128)(2,1)S(1)} %add_convert_fusion.refs_0_), channel_id=1, source_target_pairs={{0,1},{1,0},{2,3},{3,2},{4,5},{5,4},{6,7},{7,6},{8,9},{9,8},{10,11... | collective-permute-start | bytes 245768 | tf_op jit(solution)/shard_map/ppermute | solution.py:399
  57.2 5.5 %collective-permute-start.25 = (bf16[32,1280]{1,0:T(8,128)(2,1)S(1)}, bf16[32,1280]{1,0:T(8,128)(2,1)S(1)}, u32[]{:S(2)}, u32[]{:S(2)}) collective-permute-start(bf16[32,1280]{1,0:T(8,128)(2,1)S(1)} %collective-permute-done.23.refs_12_), channel_id=1, source_target_pairs={{0,2},{1,3},{2,0},{3,1},{4,6},{5,7},{6,4},{7,5},{8,10},{9,11},{10,... | collective-permute-start | bytes 245768 | tf_op jit(solution)/shard_map/ppermute | solution.py:399
  61.7 5.0 %collective-permute-start.17 = (bf16[32,1280]{1,0:T(8,128)(2,1)S(1)}, bf16[32,1280]{1,0:T(8,128)(2,1)S(1)}, u32[]{:S(2)}, u32[]{:S(2)}) collective-permute-start(bf16[32,1280]{1,0:T(8,128)(2,1)S(1)} %collective-permute-done.15.refs_4_), channel_id=1, source_target_pairs={{0,2},{1,3},{2,0},{3,1},{4,6},{5,7},{6,4},{7,5},{8,10},{9,11},{10,... | collective-permute-start | bytes 245768 | tf_op jit(solution)/shard_map/ppermute | solution.py:399
  75.2 5.3 %collective-permute-start.28 = (bf16[32,1280]{1,0:T(8,128)(2,1)S(1)}, bf16[32,1280]{1,0:T(8,128)(2,1)S(1)}, u32[]{:S(2)}, u32[]{:S(2)}) collective-permute-start(bf16[32,1280]{1,0:T(8,128)(2,1)S(1)} %slice.65), channel_id=1, source_target_pairs={{0,2},{1,3},{2,0},{3,1},{4,6},{5,7},{6,4},{7,5},{8,10},{9,11},{10,... | collective-permute-start | bytes 245768 | tf_op jit(solution)/shard_map/ppermute | solution.py:399
  76.5 5.8 %collective-permute-start.31 = (bf16[32,1280]{1,0:T(8,128)(2,1)S(1)}, bf16[32,1280]{1,0:T(8,128)(2,1)S(1)}, u32[]{:S(2)}, u32[]{:S(2)}) collective-permute-start(bf16[32,1280]{1,0:T(8,128)(2,1)S(1)} %slice.64), channel_id=1, source_target_pairs={{0,2},{1,3},{2,0},{3,1},{4,6},{5,7},{6,4},{7,5},{8,10},{9,11},{10,... | collective-permute-start | bytes 245768 | tf_op jit(solution)/shard_map/ppermute | solution.py:399
  77.5 6.6 %collective-permute-start.34 = (bf16[32,1280]{1,0:T(8,128)(2,1)S(1)}, bf16[32,1280]{1,0:T(8,128)(2,1)S(1)}, u32[]{:S(2)}, u32[]{:S(2)}) collective-permute-start(bf16[32,1280]{1,0:T(8,128)(2,1)S(1)} %slice.63), channel_id=1, source_target_pairs={{0,2},{1,3},{2,0},{3,1},{4,6},{5,7},{6,4},{7,5},{8,10},{9,11},{10,... | collective-permute-start | bytes 245768 | tf_op jit(solution)/shard_map/ppermute | solution.py:399
  78.8 7.5 %collective-permute-start.37 = (bf16[32,1280]{1,0:T(8,128)(2,1)S(1)}, bf16[32,1280]{1,0:T(8,128)(2,1)S(1)}, u32[]{:S(2)}, u32[]{:S(2)}) collective-permute-start(bf16[32,1280]{1,0:T(8,128)(2,1)S(1)} %slice.62), channel_id=1, source_target_pairs={{0,2},{1,3},{2,0},{3,1},{4,6},{5,7},{6,4},{7,5},{8,10},{9,11},{10,... | collective-permute-start | bytes 245768 | tf_op jit(solution)/shard_map/ppermute | solution.py:399
  80.6 7.0 %collective-permute-start.29 = (bf16[32,1280]{1,0:T(8,128)(2,1)S(1)}, bf16[32,1280]{1,0:T(8,128)(2,1)S(1)}, u32[]{:S(2)}, u32[]{:S(2)}) collective-permute-start(bf16[32,1280]{1,0:T(8,128)(2,1)S(1)} %fusion.11), channel_id=1, source_target_pairs={{0,8},{4,12},{8,0},{12,4},{1,9},{5,13},{9,1},{13,5},{2,10},{6,14},... | collective-permute-start | bytes 245768 | tf_op jit(solution)/shard_map/ppermute | solution.py:395
  82.4 6.5 %collective-permute-start.32 = (bf16[32,1280]{1,0:T(8,128)(2,1)S(1)}, bf16[32,1280]{1,0:T(8,128)(2,1)S(1)}, u32[]{:S(2)}, u32[]{:S(2)}) collective-permute-start(bf16[32,1280]{1,0:T(8,128)(2,1)S(1)} %fusion.10), channel_id=1, source_target_pairs={{0,4},{4,8},{8,12},{12,0},{1,5},{5,9},{9,13},{13,1},{2,6},{6,10},{... | collective-permute-start | bytes 245768 | tf_op jit(solution)/shard_map/ppermute | solution.py:395
  84.1 5.5 %collective-permute-start.35 = (bf16[32,1280]{1,0:T(8,128)(2,1)S(1)}, bf16[32,1280]{1,0:T(8,128)(2,1)S(1)}, u32[]{:S(2)}, u32[]{:S(2)}) collective-permute-start(bf16[32,1280]{1,0:T(8,128)(2,1)S(1)} %fusion.9), channel_id=1, source_target_pairs={{0,12},{4,0},{8,4},{12,8},{1,13},{5,1},{9,5},{13,9},{2,14},{6,2},{... | collective-permute-start | bytes 245768 | tf_op jit(solution)/shard_map/ppermute | solution.py:395
  (17 other events, 112.4 us)

commit v6 on v5

--- a/solution.py
+++ b/solution.py
@@ -209,22 +209,36 @@
         ]
 
         def step(blocks_in, first, carry):
-            keep = iota((tall, blocks_in * tok), 1) < spans - first * tok
-            blocks = [scalars[doc, first + j] for j in range(blocks_in)]
-            after = []
+            part = min(8, blocks_in)
+            cuts = range(0, blocks_in, part)
+            ids = [scalars[doc, first + j] for j in range(blocks_in)]
+            lane = iota((tall, part * tok), 1)
+            scores = [[] for _ in range(heads)]
+            for b in cuts:
+                keep = lane < spans - (first + b) * tok
+                for k in range(heads):
+                    keys = jnp.concatenate([kv[n, 0, k] for n in ids[b : b + part]], axis=0)
+                    scores[k].append(jnp.where(keep, mxu(qt[k], keys, (1, 1)) * factors[k], -1e30))
+            higher, shrink, sums, added = [], [], [None] * heads, [None] * heads
             for k in range(heads):
-                peak, denom, acc = carry[k]
-                keys = jnp.concatenate([kv[b, 0, k] for b in blocks], axis=0)
-                scores = mxu(qt[k], keys, (1, 1)) * factors[k]
-                scores = jnp.where(keep, scores, -1e30)
-                higher = jnp.maximum(peak, jnp.max(scores, axis=1, keepdims=True))
-                shrink = jnp.exp2(peak - higher)
-                weights = jnp.exp2(scores - higher)
-                denom = denom * shrink + jnp.sum(weights, axis=1, keepdims=True)
-                values = jnp.concatenate([kv[b, 1, k] for b in blocks], axis=0)
-                acc = acc * shrink + mxu(weights.astype(bf16), values, (1, 0))
-                after.append((higher, denom, acc))
-            return tuple(after)
+                most = functools.reduce(jnp.maximum, scores[k])
+                higher.append(jnp.maximum(carry[k][0], jnp.max(most, axis=1, keepdims=True)))
+                shrink.append(jnp.exp2(carry[k][0] - higher[k]))
+            for n, b in enumerate(cuts):
+                for k in range(heads):
+                    weights = jnp.exp2(scores[k][n] - higher[k])
+                    values = jnp.concatenate([kv[n, 1, k] for n in ids[b : b + part]], axis=0)
+                    product = mxu(weights.astype(bf16), values, (1, 0))
+                    sums[k] = weights if n == 0 else sums[k] + weights
+                    added[k] = product if n == 0 else added[k] + product
+            return tuple(
+                (
+                    higher[k],
+                    carry[k][1] * shrink[k] + jnp.sum(sums[k], axis=1, keepdims=True),
+                    carry[k][2] * shrink[k] + added[k],
+                )
+                for k in range(heads)
+            )
 
         start = tuple(
             (jnp.full((tall, 1), -1e30, f32), jnp.zeros((tall, 1), f32), jnp.zeros((tall, dim), f32))

time: 90.6 us -> 89.6 us (0.989)
  starting transfers between devices: 38.4 us -> 36.1 us
  Pallas kernels: 26.1 us -> 28.2 us
    pallas_call x1, Pallas kernels: 6.65 us -> 8.72 us  [attend(): pl.pallas_call(functools.partial(attend_kernel, count, len(later), listed...]
    ppermute x20, starting transfers between devices: 13 us -> 11.4 us  [swap(): lax.ppermute(x, axis, [(i, i ^ flip) for i in range(lax.axis_size(axis))])]
  transfers between devices with their start and end apart: 38 -> 38, of which waited for: 17 -> 18; matrix products, arithmetic and copies ran while one was open for 0% -> 0% of each run, Pallas kernels for 11% -> 12%
where the time goes in v6:
time: 89.6 us; the launch traced here: 89.4 us
  starting transfers between devices  36.1 us (40%)
  Pallas kernels  28.2 us (31%)
  waiting for transfers between devices  23.7 us (26%)
  other arithmetic  1.03 us (1%)
    ppermute x18, starting transfers between devices, shift(): return lax.ppermute(x, axis, [(i, (i + step) % n) for i in range(n)])  24.7 us
    ppermute x18, waiting for transfers between devices, shift(): return lax.ppermute(x, axis, [(i, (i + step) % n) for i in range(n)])  16.4 us
    ppermute x20, starting transfers between devices, swap(): lax.ppermute(x, axis, [(i, i ^ flip) for i in range(lax.axis_size(axis))])  11.4 us
    pallas_call x2, Pallas kernels, fetch(): pl.pallas_call(functools.partial(fetch_kernel, count), out_shape=[pltpu.V...  10.4 us
    pallas_call x1, Pallas kernels, attend(): pl.pallas_call(functools.partial(attend_kernel, count, len(later), listed...  8.72 us
    ppermute x20, waiting for transfers between devices, swap(): lax.ppermute(x, axis, [(i, i ^ flip) for i in range(lax.axis_size(axis))])  7.24 us
    pallas_call x1, Pallas kernels, swiglu(): pl.pallas_call(functools.partial(swiglu_kernel, row_devs, head_devs), out...  5.65 us
    pallas_call x1, Pallas kernels, dispatch(): pl.pallas_call(functools.partial(dispatch_kernel, blocks_dev), out_shape=...  1.89 us
  transfers between devices with their start and end apart: 38, of which 18 were waited for; matrix products, arithmetic and copies ran while one was open for 0% of the time, Pallas kernels for 12%

profile of v6, /device:TPU:0, one launch (start us, length us, event | category | flops | bytes accessed | tf_op | source)
XLA Modules:
  0.0 89.4 jit_solution(11295011888138044243)
XLA Ops:
  0.1 1.9 %dispatch.1 = (bf16[32,64]{1,0:T(8,128)(2,1)S(1)}, bf16[16,2176]{1,0:T(8,128)(2,1)S(1)}, bf16[16,2176]{1,0:T(8,128)(2,1)S(1)}, bf16[16,2176]{1,0:T(8,128)(2,1)S(1)}, bf16[16,2176]{1,0:T(8,128)(2,1)S(1)}) custom-call(s32[2]{0:T(128)S(1)} %pad_add_fusion.me_ref.at_ref, s32[32,32]{1,0:T(8,128)} %ids_hbm.1, s32[1,32]{1,0:T(1,128)} %bitcast.6, bf16[32,2048]{1,0:T(8,128)(2,1)} %q_hbm.1), custom_call_target="tpu_custom_call" | custom-call | tf_op jit(solution)/shard_map/dispatch/pallas_call | solution.py:108
  2.0 3.1 %collective-permute-start = (bf16[16,2176]{1,0:T(8,128)(2,1)S(1)}, bf16[16,2176]{1,0:T(8,128)(2,1)S(1)}, u32[]{:S(2)}, u32[]{:S(2)}) collective-permute-start(bf16[16,2176]{1,0:T(8,128)(2,1)S(1)} %get-tuple-element.38), channel_id=1, source_target_pairs={{0,4},{4,8},{8,12},{12,0},{1,5},{5,9},{9,13},{13,1},{2,6},{6,10},{... | collective-permute-start | bytes 208904 | tf_op jit(solution)/shard_map/ppermute | solution.py:409
  5.0 2.6 %collective-permute-start.1 = (bf16[16,2176]{1,0:T(8,128)(2,1)S(1)}, bf16[16,2176]{1,0:T(8,128)(2,1)S(1)}, u32[]{:S(2)}, u32[]{:S(2)}) collective-permute-start(bf16[16,2176]{1,0:T(8,128)(2,1)S(1)} %get-tuple-element.39), channel_id=1, source_target_pairs={{0,8},{4,12},{8,0},{12,4},{1,9},{5,13},{9,1},{13,5},{2,10},{6,14},... | collective-permute-start | bytes 208904 | tf_op jit(solution)/shard_map/ppermute | solution.py:409
  9.0 3.4 %fetch.2.kv = bf16[64,2,2,128,128]{4,3,2,1,0:T(8,128)(2,1)S(1)} custom-call(bf16[32,64]{1,0:T(8,128)(2,1)S(1)} %get-tuple-element.36.after_ref, bf16[64,2,2,128,128]{4,3,2,1,0:T(8,128)(2,1)} %refs_0_.2), custom_call_target="tpu_custom_call" | custom-call | bytes 8388608 | tf_op jit(solution)/shard_map/fetch/pallas_call | solution.py:46
  12.5 8.7 %attend.1 = (bf16[16,2048]{1,0:T(8,128)(2,1)S(1)}, bf16[16,2048]{1,0:T(8,128)(2,1)S(1)}, bf16[16,2048]{1,0:T(8,128)(2,1)S(1)}, bf16[16,2048]{1,0:T(8,128)(2,1)S(...) custom-call(f32[2,2]{1,0:T(2,128)S(1)} %copy-done.1, bf16[64,2,2,128,128]{4,3,2,1,0:T(8,128)(2,1)S(1)} %fetch.2.kv, ...), custom_call_target="tpu_custom_call" | custom-call | tf_op jit(solution)/shard_map/attend/pallas_call | solution.py:277
  21.3 3.2 %collective-permute-start.3 = (bf16[16,2048]{1,0:T(8,128)(2,1)S(1)}, bf16[16,2048]{1,0:T(8,128)(2,1)S(1)}, u32[]{:S(2)}, u32[]{:S(2)}) collective-permute-start(bf16[16,2048]{1,0:T(8,128)(2,1)S(1)} %get-tuple-element.42), channel_id=1, source_target_pairs={{0,12},{4,0},{8,4},{12,8},{1,13},{5,1},{9,5},{13,9},{2,14},{6,2},{... | collective-permute-start | bytes 196616 | tf_op jit(solution)/shard_map/ppermute | solution.py:409
  26.4 3.3 %collective-permute-done.4 = bf16[16,2048]{1,0:T(8,128)(2,1)S(1)} collective-permute-done((bf16[16,2048]{1,0:T(8,128)(2,1)S(1)}, bf16[16,2048]{1,0:T(8,128)(2,1)S(1)}, u32[]{:S(2)}, u32[]{:S(2)}) %collective-permute-start.4) | collective-permute-done | bytes 65568 | tf_op jit(solution)/shard_map/ppermute | solution.py:409
  32.0 1.9 %collective-permute-start.6 = (bf16[32,2048]{1,0:T(8,128)(2,1)S(1)}, bf16[32,2048]{1,0:T(8,128)(2,1)S(1)}, u32[]{:S(2)}, u32[]{:S(2)}) collective-permute-start(bf16[32,2048]{1,0:T(8,128)(2,1)S(1)} %convolution_convert_fusion.after_ref.refs_0_), channel_id=1, source_target_pairs={{0,4},{4,8},{8,12},{12,0},{1,5},{5,9},{9,13},{13,1},{2,6},{6,10},{... | collective-permute-start | bytes 393224 | tf_op jit(solution)/shard_map/ppermute | solution.py:409
  34.0 7.0 %fetch.3 = (bf16[5120,1024]{1,0:T(8,128)(2,1)S(1)}, bf16[1024,5120]{1,0:T(8,128)(2,1)S(1)}) custom-call(bf16[32,2048]{1,0:T(8,128)(2,1)S(1)} %convolution_convert_fusion.after_ref.refs_0_, bf16[5120,1024]{1,0:T(8,128)(2,1)} %refs_0_.3, bf16[1024,5120]{1,0:T(8,128)(2,1)} %refs_1_.1), custom_call_target="tpu_custom_call" | custom-call | bytes 20971520 | tf_op jit(solution)/shard_map/fetch/pallas_call | solution.py:46
  41.8 1.5 %project.1 = (f32[32,1280]{1,0:T(8,128)S(1)}, bf16[32,1280]{1,0:T(8,128)(2,1)S(1)}, bf16[32,1280]{1,0:T(8,128)(2,1)S(1)}, bf16[32,1280]{1,0:T(8,128)(2,1)S(1)}) custom-call(s32[2]{0:T(128)S(1)} %pad_add_fusion.me_ref.at_ref, bf16[32,2048]{1,0:T(8,128)(2,1)S(1)} %convolution_convert_fusion.after_ref.refs_0_, ...), custom_call_target="tpu_custom_call" | custom-call | tf_op jit(solution)/shard_map/project/pallas_call | solution.py:329
  43.4 1.4 %collective-permute-start.10 = (bf16[32,1280]{1,0:T(8,128)(2,1)S(1)}, bf16[32,1280]{1,0:T(8,128)(2,1)S(1)}, u32[]{:S(2)}, u32[]{:S(2)}) collective-permute-start(bf16[32,1280]{1,0:T(8,128)(2,1)S(1)} %get-tuple-element.54), channel_id=1, source_target_pairs={{0,2},{1,3},{2,0},{3,1},{4,6},{5,7},{6,4},{7,5},{8,10},{9,11},{10,... | collective-permute-start | bytes 245768 | tf_op jit(solution)/shard_map/ppermute | solution.py:409
  44.8 1.4 %collective-permute-start.11 = (bf16[32,1280]{1,0:T(8,128)(2,1)S(1)}, bf16[32,1280]{1,0:T(8,128)(2,1)S(1)}, u32[]{:S(2)}, u32[]{:S(2)}) collective-permute-start(bf16[32,1280]{1,0:T(8,128)(2,1)S(1)} %get-tuple-element.55), channel_id=1, source_target_pairs={{0,3},{1,0},{2,1},{3,2},{4,7},{5,4},{6,5},{7,6},{8,11},{9,8},{10,9... | collective-permute-start | bytes 245768 | tf_op jit(solution)/shard_map/ppermute | solution.py:409
  50.9 1.7 %collective-permute-start.15 = (bf16[32,1280]{1,0:T(8,128)(2,1)S(1)}, bf16[32,1280]{1,0:T(8,128)(2,1)S(1)}, u32[]{:S(2)}, u32[]{:S(2)}) collective-permute-start(bf16[32,1280]{1,0:T(8,128)(2,1)S(1)} %add_convert_fusion.refs_0_), channel_id=1, source_target_pairs={{0,4},{4,8},{8,12},{12,0},{1,5},{5,9},{9,13},{13,1},{2,6},{6,10},{... | collective-permute-start | bytes 245768 | tf_op jit(solution)/shard_map/ppermute | solution.py:409
  54.2 1.4 %collective-permute-start.25 = (bf16[32,1280]{1,0:T(8,128)(2,1)S(1)}, bf16[32,1280]{1,0:T(8,128)(2,1)S(1)}, u32[]{:S(2)}, u32[]{:S(2)}) collective-permute-start(bf16[32,1280]{1,0:T(8,128)(2,1)S(1)} %collective-permute-done.23.refs_12_), channel_id=1, source_target_pairs={{0,2},{1,3},{2,0},{3,1},{4,6},{5,7},{6,4},{7,5},{8,10},{9,11},{10,... | collective-permute-start | bytes 245768 | tf_op jit(solution)/shard_map/ppermute | solution.py:413
  55.5 3.9 %collective-permute-done.19.refs_8_ = bf16[32,1280]{1,0:T(8,128)(2,1)S(1)} collective-permute-done((bf16[32,1280]{1,0:T(8,128)(2,1)S(1)}, bf16[32,1280]{1,0:T(8,128)(2,1)S(1)}, u32[]{:S(2)}, u32[]{:S(2)}) %collective-permute-start.19) | collective-permute-done | bytes 81952 | tf_op jit(solution)/shard_map/ppermute | solution.py:409
  59.4 1.4 %collective-permute-start.21 = (bf16[32,1280]{1,0:T(8,128)(2,1)S(1)}, bf16[32,1280]{1,0:T(8,128)(2,1)S(1)}, u32[]{:S(2)}, u32[]{:S(2)}) collective-permute-start(bf16[32,1280]{1,0:T(8,128)(2,1)S(1)} %collective-permute-done.19.refs_8_), channel_id=1, source_target_pairs={{0,2},{1,3},{2,0},{3,1},{4,6},{5,7},{6,4},{7,5},{8,10},{9,11},{10,... | collective-permute-start | bytes 245768 | tf_op jit(solution)/shard_map/ppermute | solution.py:413
  62.2 2.4 %collective-permute-done.21.refs_10_ = bf16[32,1280]{1,0:T(8,128)(2,1)S(1)} collective-permute-done((bf16[32,1280]{1,0:T(8,128)(2,1)S(1)}, bf16[32,1280]{1,0:T(8,128)(2,1)S(1)}, u32[]{:S(2)}, u32[]{:S(2)}) %collective-permute-start.21) | collective-permute-done | bytes 81952 | tf_op jit(solution)/shard_map/ppermute | solution.py:413
  67.3 5.7 %swiglu.1 = (f32[64,1280]{1,0:T(8,128)S(1)}, f32[64,1280]{1,0:T(8,128)S(1)}, f32[64,1280]{1,0:T(8,128)S(1)}, f32[64,1280]{1,0:T(8,128)S(1)}, bf16[64,1280]{1,0:T...) custom-call(s32[2]{0:T(128)S(1)} %pad_add_fusion.me_ref.at_ref, ...), custom_call_target="tpu_custom_call" | custom-call | tf_op jit(solution)/shard_map/swiglu/pallas_call | solution.py:391
  74.5 1.5 %collective-permute-start.28 = (bf16[32,1280]{1,0:T(8,128)(2,1)S(1)}, bf16[32,1280]{1,0:T(8,128)(2,1)S(1)}, u32[]{:S(2)}, u32[]{:S(2)}) collective-permute-start(bf16[32,1280]{1,0:T(8,128)(2,1)S(1)} %slice.65), channel_id=1, source_target_pairs={{0,2},{1,3},{2,0},{3,1},{4,6},{5,7},{6,4},{7,5},{8,10},{9,11},{10,... | collective-permute-start | bytes 245768 | tf_op jit(solution)/shard_map/ppermute | solution.py:413
  76.8 1.5 %collective-permute-start.34 = (bf16[32,1280]{1,0:T(8,128)(2,1)S(1)}, bf16[32,1280]{1,0:T(8,128)(2,1)S(1)}, u32[]{:S(2)}, u32[]{:S(2)}) collective-permute-start(bf16[32,1280]{1,0:T(8,128)(2,1)S(1)} %slice.63), channel_id=1, source_target_pairs={{0,2},{1,3},{2,0},{3,1},{4,6},{5,7},{6,4},{7,5},{8,10},{9,11},{10,... | collective-permute-start | bytes 245768 | tf_op jit(solution)/shard_map/ppermute | solution.py:413
  79.6 1.8 %collective-permute-start.29 = (bf16[32,1280]{1,0:T(8,128)(2,1)S(1)}, bf16[32,1280]{1,0:T(8,128)(2,1)S(1)}, u32[]{:S(2)}, u32[]{:S(2)}) collective-permute-start(bf16[32,1280]{1,0:T(8,128)(2,1)S(1)} %fusion.11), channel_id=1, source_target_pairs={{0,8},{4,12},{8,0},{12,4},{1,9},{5,13},{9,1},{13,5},{2,10},{6,14},... | collective-permute-start | bytes 245768 | tf_op jit(solution)/shard_map/ppermute | solution.py:409
  81.6 1.6 %collective-permute-done.34 = bf16[32,1280]{1,0:T(8,128)(2,1)S(1)} collective-permute-done((bf16[32,1280]{1,0:T(8,128)(2,1)S(1)}, bf16[32,1280]{1,0:T(8,128)(2,1)S(1)}, u32[]{:S(2)}, u32[]{:S(2)}) %collective-permute-start.34) | collective-permute-done | bytes 81952 | tf_op jit(solution)/shard_map/ppermute | solution.py:413
  83.2 2.2 %collective-permute-start.35 = (bf16[32,1280]{1,0:T(8,128)(2,1)S(1)}, bf16[32,1280]{1,0:T(8,128)(2,1)S(1)}, u32[]{:S(2)}, u32[]{:S(2)}) collective-permute-start(bf16[32,1280]{1,0:T(8,128)(2,1)S(1)} %fusion.9), channel_id=1, source_target_pairs={{0,12},{4,0},{8,4},{12,8},{1,13},{5,1},{9,5},{13,9},{2,14},{6,2},{... | collective-permute-start | bytes 245768 | tf_op jit(solution)/shard_map/ppermute | solution.py:409
  86.6 1.4 %collective-permute-done.32 = bf16[32,1280]{1,0:T(8,128)(2,1)S(1)} collective-permute-done((bf16[32,1280]{1,0:T(8,128)(2,1)S(1)}, bf16[32,1280]{1,0:T(8,128)(2,1)S(1)}, u32[]{:S(2)}, u32[]{:S(2)}) %collective-permute-start.32) | collective-permute-done | bytes 81952 | tf_op jit(solution)/shard_map/ppermute | solution.py:409
  (79 shorter events, 23.2 us)
Async XLA Ops:
  2.0 10.4 %collective-permute-start = (bf16[16,2176]{1,0:T(8,128)(2,1)S(1)}, bf16[16,2176]{1,0:T(8,128)(2,1)S(1)}, u32[]{:S(2)}, u32[]{:S(2)}) collective-permute-start(bf16[16,2176]{1,0:T(8,128)(2,1)S(1)} %get-tuple-element.38), channel_id=1, source_target_pairs={{0,4},{4,8},{8,12},{12,0},{1,5},{5,9},{9,13},{13,1},{2,6},{6,10},{... | collective-permute-start | bytes 208904 | tf_op jit(solution)/shard_map/ppermute | solution.py:409
  5.0 7.4 %collective-permute-start.1 = (bf16[16,2176]{1,0:T(8,128)(2,1)S(1)}, bf16[16,2176]{1,0:T(8,128)(2,1)S(1)}, u32[]{:S(2)}, u32[]{:S(2)}) collective-permute-start(bf16[16,2176]{1,0:T(8,128)(2,1)S(1)} %get-tuple-element.39), channel_id=1, source_target_pairs={{0,8},{4,12},{8,0},{12,4},{1,9},{5,13},{9,1},{13,5},{2,10},{6,14},... | collective-permute-start | bytes 208904 | tf_op jit(solution)/shard_map/ppermute | solution.py:409
  21.3 5.1 %collective-permute-start.3 = (bf16[16,2048]{1,0:T(8,128)(2,1)S(1)}, bf16[16,2048]{1,0:T(8,128)(2,1)S(1)}, u32[]{:S(2)}, u32[]{:S(2)}) collective-permute-start(bf16[16,2048]{1,0:T(8,128)(2,1)S(1)} %get-tuple-element.42), channel_id=1, source_target_pairs={{0,12},{4,0},{8,4},{12,8},{1,13},{5,1},{9,5},{13,9},{2,14},{6,2},{... | collective-permute-start | bytes 196616 | tf_op jit(solution)/shard_map/ppermute | solution.py:409
  24.5 5.2 %collective-permute-start.4 = (bf16[16,2048]{1,0:T(8,128)(2,1)S(1)}, bf16[16,2048]{1,0:T(8,128)(2,1)S(1)}, u32[]{:S(2)}, u32[]{:S(2)}) collective-permute-start(bf16[16,2048]{1,0:T(8,128)(2,1)S(1)} %get-tuple-element.43), channel_id=1, source_target_pairs={{0,8},{4,12},{8,0},{12,4},{1,9},{5,13},{9,1},{13,5},{2,10},{6,14},... | collective-permute-start | bytes 196616 | tf_op jit(solution)/shard_map/ppermute | solution.py:409
  24.5 6.2 %collective-permute-start.5 = (bf16[16,2048]{1,0:T(8,128)(2,1)S(1)}, bf16[16,2048]{1,0:T(8,128)(2,1)S(1)}, u32[]{:S(2)}, u32[]{:S(2)}) collective-permute-start(bf16[16,2048]{1,0:T(8,128)(2,1)S(1)} %get-tuple-element.44), channel_id=1, source_target_pairs={{0,4},{4,8},{8,12},{12,0},{1,5},{5,9},{9,13},{13,1},{2,6},{6,10},{... | collective-permute-start | bytes 196616 | tf_op jit(solution)/shard_map/ppermute | solution.py:409
  30.9 10.1 %collective-permute-start.8 = (bf16[32,2048]{1,0:T(8,128)(2,1)S(1)}, bf16[32,2048]{1,0:T(8,128)(2,1)S(1)}, u32[]{:S(2)}, u32[]{:S(2)}) collective-permute-start(bf16[32,2048]{1,0:T(8,128)(2,1)S(1)} %convolution_convert_fusion.after_ref.refs_0_), channel_id=1, source_target_pairs={{0,12},{4,0},{8,4},{12,8},{1,13},{5,1},{9,5},{13,9},{2,14},{6,2},{... | collective-permute-start | bytes 393224 | tf_op jit(solution)/shard_map/ppermute | solution.py:409
  31.7 10.1 %collective-permute-start.7 = (bf16[32,2048]{1,0:T(8,128)(2,1)S(1)}, bf16[32,2048]{1,0:T(8,128)(2,1)S(1)}, u32[]{:S(2)}, u32[]{:S(2)}) collective-permute-start(bf16[32,2048]{1,0:T(8,128)(2,1)S(1)} %convolution_convert_fusion.after_ref.refs_0_), channel_id=1, source_target_pairs={{0,8},{4,12},{8,0},{12,4},{1,9},{5,13},{9,1},{13,5},{2,10},{6,14},... | collective-permute-start | bytes 393224 | tf_op jit(solution)/shard_map/ppermute | solution.py:409
  32.0 9.8 %collective-permute-start.6 = (bf16[32,2048]{1,0:T(8,128)(2,1)S(1)}, bf16[32,2048]{1,0:T(8,128)(2,1)S(1)}, u32[]{:S(2)}, u32[]{:S(2)}) collective-permute-start(bf16[32,2048]{1,0:T(8,128)(2,1)S(1)} %convolution_convert_fusion.after_ref.refs_0_), channel_id=1, source_target_pairs={{0,4},{4,8},{8,12},{12,0},{1,5},{5,9},{9,13},{13,1},{2,6},{6,10},{... | collective-permute-start | bytes 393224 | tf_op jit(solution)/shard_map/ppermute | solution.py:409
  43.4 5.3 %collective-permute-start.10 = (bf16[32,1280]{1,0:T(8,128)(2,1)S(1)}, bf16[32,1280]{1,0:T(8,128)(2,1)S(1)}, u32[]{:S(2)}, u32[]{:S(2)}) collective-permute-start(bf16[32,1280]{1,0:T(8,128)(2,1)S(1)} %get-tuple-element.54), channel_id=1, source_target_pairs={{0,2},{1,3},{2,0},{3,1},{4,6},{5,7},{6,4},{7,5},{8,10},{9,11},{10,... | collective-permute-start | bytes 245768 | tf_op jit(solution)/shard_map/ppermute | solution.py:409
  48.8 5.3 %collective-permute-start.23 = (bf16[32,1280]{1,0:T(8,128)(2,1)S(1)}, bf16[32,1280]{1,0:T(8,128)(2,1)S(1)}, u32[]{:S(2)}, u32[]{:S(2)}) collective-permute-start(bf16[32,1280]{1,0:T(8,128)(2,1)S(1)} %add_convert_fusion.refs_0_), channel_id=1, source_target_pairs={{0,12},{4,0},{8,4},{12,8},{1,13},{5,1},{9,5},{13,9},{2,14},{6,2},{... | collective-permute-start | bytes 245768 | tf_op jit(solution)/shard_map/ppermute | solution.py:409
  50.1 9.4 %collective-permute-start.19 = (bf16[32,1280]{1,0:T(8,128)(2,1)S(1)}, bf16[32,1280]{1,0:T(8,128)(2,1)S(1)}, u32[]{:S(2)}, u32[]{:S(2)}) collective-permute-start(bf16[32,1280]{1,0:T(8,128)(2,1)S(1)} %add_convert_fusion.refs_0_), channel_id=1, source_target_pairs={{0,8},{4,12},{8,0},{12,4},{1,9},{5,13},{9,1},{13,5},{2,10},{6,14},... | collective-permute-start | bytes 245768 | tf_op jit(solution)/shard_map/ppermute | solution.py:409
  50.9 8.6 %collective-permute-start.15 = (bf16[32,1280]{1,0:T(8,128)(2,1)S(1)}, bf16[32,1280]{1,0:T(8,128)(2,1)S(1)}, u32[]{:S(2)}, u32[]{:S(2)}) collective-permute-start(bf16[32,1280]{1,0:T(8,128)(2,1)S(1)} %add_convert_fusion.refs_0_), channel_id=1, source_target_pairs={{0,4},{4,8},{8,12},{12,0},{1,5},{5,9},{9,13},{13,1},{2,6},{6,10},{... | collective-permute-start | bytes 245768 | tf_op jit(solution)/shard_map/ppermute | solution.py:409
  52.6 8.3 %collective-permute-start.13 = (bf16[32,1280]{1,0:T(8,128)(2,1)S(1)}, bf16[32,1280]{1,0:T(8,128)(2,1)S(1)}, u32[]{:S(2)}, u32[]{:S(2)}) collective-permute-start(bf16[32,1280]{1,0:T(8,128)(2,1)S(1)} %add_convert_fusion.refs_0_), channel_id=1, source_target_pairs={{0,2},{1,3},{2,0},{3,1},{4,6},{5,7},{6,4},{7,5},{8,10},{9,11},{10,... | collective-permute-start | bytes 245768 | tf_op jit(solution)/shard_map/ppermute | solution.py:413
  53.9 7.2 %collective-permute-start.12 = (bf16[32,1280]{1,0:T(8,128)(2,1)S(1)}, bf16[32,1280]{1,0:T(8,128)(2,1)S(1)}, u32[]{:S(2)}, u32[]{:S(2)}) collective-permute-start(bf16[32,1280]{1,0:T(8,128)(2,1)S(1)} %add_convert_fusion.refs_0_), channel_id=1, source_target_pairs={{0,1},{1,0},{2,3},{3,2},{4,5},{5,4},{6,7},{7,6},{8,9},{9,8},{10,11... | collective-permute-start | bytes 245768 | tf_op jit(solution)/shard_map/ppermute | solution.py:413
  54.2 7.5 %collective-permute-start.25 = (bf16[32,1280]{1,0:T(8,128)(2,1)S(1)}, bf16[32,1280]{1,0:T(8,128)(2,1)S(1)}, u32[]{:S(2)}, u32[]{:S(2)}) collective-permute-start(bf16[32,1280]{1,0:T(8,128)(2,1)S(1)} %collective-permute-done.23.refs_12_), channel_id=1, source_target_pairs={{0,2},{1,3},{2,0},{3,1},{4,6},{5,7},{6,4},{7,5},{8,10},{9,11},{10,... | collective-permute-start | bytes 245768 | tf_op jit(solution)/shard_map/ppermute | solution.py:413
  59.4 5.2 %collective-permute-start.21 = (bf16[32,1280]{1,0:T(8,128)(2,1)S(1)}, bf16[32,1280]{1,0:T(8,128)(2,1)S(1)}, u32[]{:S(2)}, u32[]{:S(2)}) collective-permute-start(bf16[32,1280]{1,0:T(8,128)(2,1)S(1)} %collective-permute-done.19.refs_8_), channel_id=1, source_target_pairs={{0,2},{1,3},{2,0},{3,1},{4,6},{5,7},{6,4},{7,5},{8,10},{9,11},{10,... | collective-permute-start | bytes 245768 | tf_op jit(solution)/shard_map/ppermute | solution.py:413
  61.1 4.9 %collective-permute-start.17 = (bf16[32,1280]{1,0:T(8,128)(2,1)S(1)}, bf16[32,1280]{1,0:T(8,128)(2,1)S(1)}, u32[]{:S(2)}, u32[]{:S(2)}) collective-permute-start(bf16[32,1280]{1,0:T(8,128)(2,1)S(1)} %collective-permute-done.15.refs_4_), channel_id=1, source_target_pairs={{0,2},{1,3},{2,0},{3,1},{4,6},{5,7},{6,4},{7,5},{8,10},{9,11},{10,... | collective-permute-start | bytes 245768 | tf_op jit(solution)/shard_map/ppermute | solution.py:413
  74.5 5.1 %collective-permute-start.28 = (bf16[32,1280]{1,0:T(8,128)(2,1)S(1)}, bf16[32,1280]{1,0:T(8,128)(2,1)S(1)}, u32[]{:S(2)}, u32[]{:S(2)}) collective-permute-start(bf16[32,1280]{1,0:T(8,128)(2,1)S(1)} %slice.65), channel_id=1, source_target_pairs={{0,2},{1,3},{2,0},{3,1},{4,6},{5,7},{6,4},{7,5},{8,10},{9,11},{10,... | collective-permute-start | bytes 245768 | tf_op jit(solution)/shard_map/ppermute | solution.py:413
  76.1 5.4 %collective-permute-start.31 = (bf16[32,1280]{1,0:T(8,128)(2,1)S(1)}, bf16[32,1280]{1,0:T(8,128)(2,1)S(1)}, u32[]{:S(2)}, u32[]{:S(2)}) collective-permute-start(bf16[32,1280]{1,0:T(8,128)(2,1)S(1)} %slice.64), channel_id=1, source_target_pairs={{0,2},{1,3},{2,0},{3,1},{4,6},{5,7},{6,4},{7,5},{8,10},{9,11},{10,... | collective-permute-start | bytes 245768 | tf_op jit(solution)/shard_map/ppermute | solution.py:413
  76.8 6.4 %collective-permute-start.34 = (bf16[32,1280]{1,0:T(8,128)(2,1)S(1)}, bf16[32,1280]{1,0:T(8,128)(2,1)S(1)}, u32[]{:S(2)}, u32[]{:S(2)}) collective-permute-start(bf16[32,1280]{1,0:T(8,128)(2,1)S(1)} %slice.63), channel_id=1, source_target_pairs={{0,2},{1,3},{2,0},{3,1},{4,6},{5,7},{6,4},{7,5},{8,10},{9,11},{10,... | collective-permute-start | bytes 245768 | tf_op jit(solution)/shard_map/ppermute | solution.py:413
  78.3 7.1 %collective-permute-start.37 = (bf16[32,1280]{1,0:T(8,128)(2,1)S(1)}, bf16[32,1280]{1,0:T(8,128)(2,1)S(1)}, u32[]{:S(2)}, u32[]{:S(2)}) collective-permute-start(bf16[32,1280]{1,0:T(8,128)(2,1)S(1)} %slice.62), channel_id=1, source_target_pairs={{0,2},{1,3},{2,0},{3,1},{4,6},{5,7},{6,4},{7,5},{8,10},{9,11},{10,... | collective-permute-start | bytes 245768 | tf_op jit(solution)/shard_map/ppermute | solution.py:413
  79.6 6.9 %collective-permute-start.29 = (bf16[32,1280]{1,0:T(8,128)(2,1)S(1)}, bf16[32,1280]{1,0:T(8,128)(2,1)S(1)}, u32[]{:S(2)}, u32[]{:S(2)}) collective-permute-start(bf16[32,1280]{1,0:T(8,128)(2,1)S(1)} %fusion.11), channel_id=1, source_target_pairs={{0,8},{4,12},{8,0},{12,4},{1,9},{5,13},{9,1},{13,5},{2,10},{6,14},... | collective-permute-start | bytes 245768 | tf_op jit(solution)/shard_map/ppermute | solution.py:409
  81.5 6.5 %collective-permute-start.32 = (bf16[32,1280]{1,0:T(8,128)(2,1)S(1)}, bf16[32,1280]{1,0:T(8,128)(2,1)S(1)}, u32[]{:S(2)}, u32[]{:S(2)}) collective-permute-start(bf16[32,1280]{1,0:T(8,128)(2,1)S(1)} %fusion.10), channel_id=1, source_target_pairs={{0,4},{4,8},{8,12},{12,0},{1,5},{5,9},{9,13},{13,1},{2,6},{6,10},{... | collective-permute-start | bytes 245768 | tf_op jit(solution)/shard_map/ppermute | solution.py:409
  83.2 5.5 %collective-permute-start.35 = (bf16[32,1280]{1,0:T(8,128)(2,1)S(1)}, bf16[32,1280]{1,0:T(8,128)(2,1)S(1)}, u32[]{:S(2)}, u32[]{:S(2)}) collective-permute-start(bf16[32,1280]{1,0:T(8,128)(2,1)S(1)} %fusion.9), channel_id=1, source_target_pairs={{0,12},{4,0},{8,4},{12,8},{1,13},{5,1},{9,5},{13,9},{2,14},{6,2},{... | collective-permute-start | bytes 245768 | tf_op jit(solution)/shard_map/ppermute | solution.py:409
  (17 other events, 110.9 us)

commit v7 on v6

--- a/solution.py
+++ b/solution.py
@@ -426,8 +426,9 @@
     total = hidden_state.astype(f32)
     order = sorted(range(row_devs), key=lambda i: (i == 0, abs(2 * i - row_devs)))
     for i in order:
-        pair = keeps[i] + swap(sends[i], "heads", 1).astype(f32)
-        part = pair[:rows] + swap(pair[rows:].astype(bf16), "heads", 2).astype(f32)
+        got = swap(sends[i], "heads", 1)
+        across = (keeps[i][rows:] + got[rows:].astype(f32)).astype(bf16)
+        part = keeps[i][:rows] + got[:rows].astype(f32) + swap(across, "heads", 2).astype(f32)
         total = total + (shift(part.astype(bf16), "rows", i).astype(f32) if i else part)
     return total.astype(bf16)
 

time: 89.6 us -> 90.2 us (level)
  starting transfers between devices: 36.1 us -> 37.7 us
  Pallas kernels: 28.2 us -> 26.9 us
    ppermute x18, starting transfers between devices: 24.7 us -> 26.2 us  [shift(): return lax.ppermute(x, axis, [(i, (i + step) % n) for i in range(n)])]
    pallas_call x1, Pallas kernels: 8.72 us -> 7.51 us  [attend(): pl.pallas_call(functools.partial(attend_kernel, count, len(later), listed...]
  transfers between devices with their start and end apart: 38 -> 38, of which waited for: 18 -> 19; matrix products, arithmetic and copies ran while one was open for 0% -> 0% of each run, Pallas kernels for 12% -> 12%
where the time goes in v7:
time: 90.2 us; the launch traced here: 89.5 us
  starting transfers between devices  37.7 us (42%)
  Pallas kernels  26.9 us (30%)
  waiting for transfers between devices  23.4 us (26%)
  other arithmetic  1.02 us (1%)
    ppermute x18, starting transfers between devices, shift(): return lax.ppermute(x, axis, [(i, (i + step) % n) for i in range(n)])  26.2 us
    ppermute x18, waiting for transfers between devices, shift(): return lax.ppermute(x, axis, [(i, (i + step) % n) for i in range(n)])  16.2 us
    ppermute x20, starting transfers between devices, swap(): lax.ppermute(x, axis, [(i, i ^ flip) for i in range(lax.axis_size(axis))])  11.5 us
    pallas_call x2, Pallas kernels, fetch(): pl.pallas_call(functools.partial(fetch_kernel, count), out_shape=[pltpu.V...  10.4 us
    pallas_call x1, Pallas kernels, attend(): pl.pallas_call(functools.partial(attend_kernel, count, len(later), listed...  7.51 us
    ppermute x20, waiting for transfers between devices, swap(): lax.ppermute(x, axis, [(i, i ^ flip) for i in range(lax.axis_size(axis))])  7.23 us
    pallas_call x1, Pallas kernels, swiglu(): pl.pallas_call(functools.partial(swiglu_kernel, row_devs, head_devs), out...  5.66 us
    pallas_call x1, Pallas kernels, dispatch(): pl.pallas_call(functools.partial(dispatch_kernel, blocks_dev), out_shape=...  1.89 us
  transfers between devices with their start and end apart: 38, of which 19 were waited for; matrix products, arithmetic and copies ran while one was open for 0% of the time, Pallas kernels for 12%

profile of v7, /device:TPU:0, one launch (start us, length us, event | category | flops | bytes accessed | tf_op | source)
XLA Modules:
  0.0 89.5 jit_solution(17278575073419376884)
XLA Ops:
  0.1 1.9 %dispatch.1 = (bf16[32,64]{1,0:T(8,128)(2,1)S(1)}, bf16[16,2176]{1,0:T(8,128)(2,1)S(1)}, bf16[16,2176]{1,0:T(8,128)(2,1)S(1)}, bf16[16,2176]{1,0:T(8,128)(2,1)S(1)}, bf16[16,2176]{1,0:T(8,128)(2,1)S(1)}) custom-call(s32[2]{0:T(128)S(1)} %pad_add_fusion.me_ref.at_ref, s32[32,32]{1,0:T(8,128)} %ids_hbm.1, s32[1,32]{1,0:T(1,128)} %bitcast.6, bf16[32,2048]{1,0:T(8,128)(2,1)} %q_hbm.1), custom_call_target="tpu_custom_call" | custom-call | tf_op jit(solution)/shard_map/dispatch/pallas_call | solution.py:108
  2.0 3.1 %collective-permute-start = (bf16[16,2176]{1,0:T(8,128)(2,1)S(1)}, bf16[16,2176]{1,0:T(8,128)(2,1)S(1)}, u32[]{:S(2)}, u32[]{:S(2)}) collective-permute-start(bf16[16,2176]{1,0:T(8,128)(2,1)S(1)} %get-tuple-element.38), channel_id=1, source_target_pairs={{0,4},{4,8},{8,12},{12,0},{1,5},{5,9},{9,13},{13,1},{2,6},{6,10},{... | collective-permute-start | bytes 208904 | tf_op jit(solution)/shard_map/ppermute | solution.py:409
  5.0 2.6 %collective-permute-start.1 = (bf16[16,2176]{1,0:T(8,128)(2,1)S(1)}, bf16[16,2176]{1,0:T(8,128)(2,1)S(1)}, u32[]{:S(2)}, u32[]{:S(2)}) collective-permute-start(bf16[16,2176]{1,0:T(8,128)(2,1)S(1)} %get-tuple-element.39), channel_id=1, source_target_pairs={{0,8},{4,12},{8,0},{12,4},{1,9},{5,13},{9,1},{13,5},{2,10},{6,14},... | collective-permute-start | bytes 208904 | tf_op jit(solution)/shard_map/ppermute | solution.py:409
  7.6 1.3 %collective-permute-start.2 = (bf16[16,2176]{1,0:T(8,128)(2,1)S(1)}, bf16[16,2176]{1,0:T(8,128)(2,1)S(1)}, u32[]{:S(2)}, u32[]{:S(2)}) collective-permute-start(bf16[16,2176]{1,0:T(8,128)(2,1)S(1)} %get-tuple-element.40), channel_id=1, source_target_pairs={{0,12},{4,0},{8,4},{12,8},{1,13},{5,1},{9,5},{13,9},{2,14},{6,2},{... | collective-permute-start | bytes 208904 | tf_op jit(solution)/shard_map/ppermute | solution.py:409
  9.0 3.4 %fetch.2.kv = bf16[64,2,2,128,128]{4,3,2,1,0:T(8,128)(2,1)S(1)} custom-call(bf16[32,64]{1,0:T(8,128)(2,1)S(1)} %get-tuple-element.36.after_ref, bf16[64,2,2,128,128]{4,3,2,1,0:T(8,128)(2,1)} %refs_0_.2), custom_call_target="tpu_custom_call" | custom-call | bytes 8388608 | tf_op jit(solution)/shard_map/fetch/pallas_call | solution.py:46
  12.5 7.5 %attend.1 = (bf16[16,2048]{1,0:T(8,128)(2,1)S(1)}, bf16[16,2048]{1,0:T(8,128)(2,1)S(1)}, bf16[16,2048]{1,0:T(8,128)(2,1)S(1)}, bf16[16,2048]{1,0:T(8,128)(2,1)S(...) custom-call(f32[2,2]{1,0:T(2,128)S(1)} %copy-done.1, bf16[64,2,2,128,128]{4,3,2,1,0:T(8,128)(2,1)S(1)} %fetch.2.kv, ...), custom_call_target="tpu_custom_call" | custom-call | tf_op jit(solution)/shard_map/attend/pallas_call | solution.py:277
  20.1 4.4 %collective-permute-start.3 = (bf16[16,2048]{1,0:T(8,128)(2,1)S(1)}, bf16[16,2048]{1,0:T(8,128)(2,1)S(1)}, u32[]{:S(2)}, u32[]{:S(2)}) collective-permute-start(bf16[16,2048]{1,0:T(8,128)(2,1)S(1)} %get-tuple-element.42), channel_id=1, source_target_pairs={{0,12},{4,0},{8,4},{12,8},{1,13},{5,1},{9,5},{13,9},{2,14},{6,2},{... | collective-permute-start | bytes 196616 | tf_op jit(solution)/shard_map/ppermute | solution.py:409
  26.4 3.3 %collective-permute-done.4 = bf16[16,2048]{1,0:T(8,128)(2,1)S(1)} collective-permute-done((bf16[16,2048]{1,0:T(8,128)(2,1)S(1)}, bf16[16,2048]{1,0:T(8,128)(2,1)S(1)}, u32[]{:S(2)}, u32[]{:S(2)}) %collective-permute-start.4) | collective-permute-done | bytes 65568 | tf_op jit(solution)/shard_map/ppermute | solution.py:409
  32.0 1.9 %collective-permute-start.6 = (bf16[32,2048]{1,0:T(8,128)(2,1)S(1)}, bf16[32,2048]{1,0:T(8,128)(2,1)S(1)}, u32[]{:S(2)}, u32[]{:S(2)}) collective-permute-start(bf16[32,2048]{1,0:T(8,128)(2,1)S(1)} %convolution_convert_fusion.after_ref.refs_0_), channel_id=1, source_target_pairs={{0,4},{4,8},{8,12},{12,0},{1,5},{5,9},{9,13},{13,1},{2,6},{6,10},{... | collective-permute-start | bytes 393224 | tf_op jit(solution)/shard_map/ppermute | solution.py:409
  34.0 7.0 %fetch.3 = (bf16[5120,1024]{1,0:T(8,128)(2,1)S(1)}, bf16[1024,5120]{1,0:T(8,128)(2,1)S(1)}) custom-call(bf16[32,2048]{1,0:T(8,128)(2,1)S(1)} %convolution_convert_fusion.after_ref.refs_0_, bf16[5120,1024]{1,0:T(8,128)(2,1)} %refs_0_.3, bf16[1024,5120]{1,0:T(8,128)(2,1)} %refs_1_.1), custom_call_target="tpu_custom_call" | custom-call | bytes 20971520 | tf_op jit(solution)/shard_map/fetch/pallas_call | solution.py:46
  41.8 1.5 %project.1 = (f32[32,1280]{1,0:T(8,128)S(1)}, bf16[32,1280]{1,0:T(8,128)(2,1)S(1)}, bf16[32,1280]{1,0:T(8,128)(2,1)S(1)}, bf16[32,1280]{1,0:T(8,128)(2,1)S(1)}) custom-call(s32[2]{0:T(128)S(1)} %pad_add_fusion.me_ref.at_ref, bf16[32,2048]{1,0:T(8,128)(2,1)S(1)} %convolution_convert_fusion.after_ref.refs_0_, ...), custom_call_target="tpu_custom_call" | custom-call | tf_op jit(solution)/shard_map/project/pallas_call | solution.py:329
  43.4 1.6 %collective-permute-start.10 = (bf16[32,1280]{1,0:T(8,128)(2,1)S(1)}, bf16[32,1280]{1,0:T(8,128)(2,1)S(1)}, u32[]{:S(2)}, u32[]{:S(2)}) collective-permute-start(bf16[32,1280]{1,0:T(8,128)(2,1)S(1)} %get-tuple-element.54), channel_id=1, source_target_pairs={{0,2},{1,3},{2,0},{3,1},{4,6},{5,7},{6,4},{7,5},{8,10},{9,11},{10,... | collective-permute-start | bytes 245768 | tf_op jit(solution)/shard_map/ppermute | solution.py:409
  44.9 1.4 %collective-permute-start.11 = (bf16[32,1280]{1,0:T(8,128)(2,1)S(1)}, bf16[32,1280]{1,0:T(8,128)(2,1)S(1)}, u32[]{:S(2)}, u32[]{:S(2)}) collective-permute-start(bf16[32,1280]{1,0:T(8,128)(2,1)S(1)} %get-tuple-element.55), channel_id=1, source_target_pairs={{0,3},{1,0},{2,1},{3,2},{4,7},{5,4},{6,5},{7,6},{8,11},{9,8},{10,9... | collective-permute-start | bytes 245768 | tf_op jit(solution)/shard_map/ppermute | solution.py:409
  50.9 1.8 %collective-permute-start.15 = (bf16[32,1280]{1,0:T(8,128)(2,1)S(1)}, bf16[32,1280]{1,0:T(8,128)(2,1)S(1)}, u32[]{:S(2)}, u32[]{:S(2)}) collective-permute-start(bf16[32,1280]{1,0:T(8,128)(2,1)S(1)} %add_convert_fusion.8.refs_0_), channel_id=1, source_target_pairs={{0,4},{4,8},{8,12},{12,0},{1,5},{5,9},{9,13},{13,1},{2,6},{6,10},{... | collective-permute-start | bytes 245768 | tf_op jit(solution)/shard_map/ppermute | solution.py:409
  54.2 1.5 %collective-permute-start.25 = (bf16[32,1280]{1,0:T(8,128)(2,1)S(1)}, bf16[32,1280]{1,0:T(8,128)(2,1)S(1)}, u32[]{:S(2)}, u32[]{:S(2)}) collective-permute-start(bf16[32,1280]{1,0:T(8,128)(2,1)S(1)} %collective-permute-done.23.refs_12_), channel_id=1, source_target_pairs={{0,2},{1,3},{2,0},{3,1},{4,6},{5,7},{6,4},{7,5},{8,10},{9,11},{10,... | collective-permute-start | bytes 245768 | tf_op jit(solution)/shard_map/ppermute | solution.py:413
  55.7 3.7 %collective-permute-done.19.refs_8_ = bf16[32,1280]{1,0:T(8,128)(2,1)S(1)} collective-permute-done((bf16[32,1280]{1,0:T(8,128)(2,1)S(1)}, bf16[32,1280]{1,0:T(8,128)(2,1)S(1)}, u32[]{:S(2)}, u32[]{:S(2)}) %collective-permute-start.19) | collective-permute-done | bytes 81952 | tf_op jit(solution)/shard_map/ppermute | solution.py:409
  59.4 1.5 %collective-permute-start.21 = (bf16[32,1280]{1,0:T(8,128)(2,1)S(1)}, bf16[32,1280]{1,0:T(8,128)(2,1)S(1)}, u32[]{:S(2)}, u32[]{:S(2)}) collective-permute-start(bf16[32,1280]{1,0:T(8,128)(2,1)S(1)} %collective-permute-done.19.refs_8_), channel_id=1, source_target_pairs={{0,2},{1,3},{2,0},{3,1},{4,6},{5,7},{6,4},{7,5},{8,10},{9,11},{10,... | collective-permute-start | bytes 245768 | tf_op jit(solution)/shard_map/ppermute | solution.py:413
  62.2 2.3 %collective-permute-done.21.refs_10_ = bf16[32,1280]{1,0:T(8,128)(2,1)S(1)} collective-permute-done((bf16[32,1280]{1,0:T(8,128)(2,1)S(1)}, bf16[32,1280]{1,0:T(8,128)(2,1)S(1)}, u32[]{:S(2)}, u32[]{:S(2)}) %collective-permute-start.21) | collective-permute-done | bytes 81952 | tf_op jit(solution)/shard_map/ppermute | solution.py:413
  67.3 5.7 %swiglu.1 = (f32[64,1280]{1,0:T(8,128)S(1)}, f32[64,1280]{1,0:T(8,128)S(1)}, f32[64,1280]{1,0:T(8,128)S(1)}, f32[64,1280]{1,0:T(8,128)S(1)}, bf16[64,1280]{1,0:T...) custom-call(s32[2]{0:T(128)S(1)} %pad_add_fusion.me_ref.at_ref, ...), custom_call_target="tpu_custom_call" | custom-call | tf_op jit(solution)/shard_map/swiglu/pallas_call | solution.py:391
  74.5 1.6 %collective-permute-start.28 = (bf16[32,1280]{1,0:T(8,128)(2,1)S(1)}, bf16[32,1280]{1,0:T(8,128)(2,1)S(1)}, u32[]{:S(2)}, u32[]{:S(2)}) collective-permute-start(bf16[32,1280]{1,0:T(8,128)(2,1)S(1)} %add_convert_fusion.7), channel_id=1, source_target_pairs={{0,2},{1,3},{2,0},{3,1},{4,6},{5,7},{6,4},{7,5},{8,10},{9,11},{10,... | collective-permute-start | bytes 245768 | tf_op jit(solution)/shard_map/ppermute | solution.py:413
  76.7 1.6 %collective-permute-start.34 = (bf16[32,1280]{1,0:T(8,128)(2,1)S(1)}, bf16[32,1280]{1,0:T(8,128)(2,1)S(1)}, u32[]{:S(2)}, u32[]{:S(2)}) collective-permute-start(bf16[32,1280]{1,0:T(8,128)(2,1)S(1)} %add_convert_fusion.3), channel_id=1, source_target_pairs={{0,2},{1,3},{2,0},{3,1},{4,6},{5,7},{6,4},{7,5},{8,10},{9,11},{10,... | collective-permute-start | bytes 245768 | tf_op jit(solution)/shard_map/ppermute | solution.py:413
  79.6 1.9 %collective-permute-start.29 = (bf16[32,1280]{1,0:T(8,128)(2,1)S(1)}, bf16[32,1280]{1,0:T(8,128)(2,1)S(1)}, u32[]{:S(2)}, u32[]{:S(2)}) collective-permute-start(bf16[32,1280]{1,0:T(8,128)(2,1)S(1)} %add_convert_fusion.6), channel_id=1, source_target_pairs={{0,8},{4,12},{8,0},{12,4},{1,9},{5,13},{9,1},{13,5},{2,10},{6,14},... | collective-permute-start | bytes 245768 | tf_op jit(solution)/shard_map/ppermute | solution.py:409
  81.6 1.6 %collective-permute-done.34 = bf16[32,1280]{1,0:T(8,128)(2,1)S(1)} collective-permute-done((bf16[32,1280]{1,0:T(8,128)(2,1)S(1)}, bf16[32,1280]{1,0:T(8,128)(2,1)S(1)}, u32[]{:S(2)}, u32[]{:S(2)}) %collective-permute-start.34) | collective-permute-done | bytes 81952 | tf_op jit(solution)/shard_map/ppermute | solution.py:413
  83.2 2.3 %collective-permute-start.35 = (bf16[32,1280]{1,0:T(8,128)(2,1)S(1)}, bf16[32,1280]{1,0:T(8,128)(2,1)S(1)}, u32[]{:S(2)}, u32[]{:S(2)}) collective-permute-start(bf16[32,1280]{1,0:T(8,128)(2,1)S(1)} %add_convert_fusion.2), channel_id=1, source_target_pairs={{0,12},{4,0},{8,4},{12,8},{1,13},{5,1},{9,5},{13,9},{2,14},{6,2},{... | collective-permute-start | bytes 245768 | tf_op jit(solution)/shard_map/ppermute | solution.py:409
  (75 shorter events, 23.1 us)
Async XLA Ops:
  2.0 10.4 %collective-permute-start = (bf16[16,2176]{1,0:T(8,128)(2,1)S(1)}, bf16[16,2176]{1,0:T(8,128)(2,1)S(1)}, u32[]{:S(2)}, u32[]{:S(2)}) collective-permute-start(bf16[16,2176]{1,0:T(8,128)(2,1)S(1)} %get-tuple-element.38), channel_id=1, source_target_pairs={{0,4},{4,8},{8,12},{12,0},{1,5},{5,9},{9,13},{13,1},{2,6},{6,10},{... | collective-permute-start | bytes 208904 | tf_op jit(solution)/shard_map/ppermute | solution.py:409
  5.0 7.4 %collective-permute-start.1 = (bf16[16,2176]{1,0:T(8,128)(2,1)S(1)}, bf16[16,2176]{1,0:T(8,128)(2,1)S(1)}, u32[]{:S(2)}, u32[]{:S(2)}) collective-permute-start(bf16[16,2176]{1,0:T(8,128)(2,1)S(1)} %get-tuple-element.39), channel_id=1, source_target_pairs={{0,8},{4,12},{8,0},{12,4},{1,9},{5,13},{9,1},{13,5},{2,10},{6,14},... | collective-permute-start | bytes 208904 | tf_op jit(solution)/shard_map/ppermute | solution.py:409
  7.6 4.9 %collective-permute-start.2 = (bf16[16,2176]{1,0:T(8,128)(2,1)S(1)}, bf16[16,2176]{1,0:T(8,128)(2,1)S(1)}, u32[]{:S(2)}, u32[]{:S(2)}) collective-permute-start(bf16[16,2176]{1,0:T(8,128)(2,1)S(1)} %get-tuple-element.40), channel_id=1, source_target_pairs={{0,12},{4,0},{8,4},{12,8},{1,13},{5,1},{9,5},{13,9},{2,14},{6,2},{... | collective-permute-start | bytes 208904 | tf_op jit(solution)/shard_map/ppermute | solution.py:409
  20.1 6.3 %collective-permute-start.3 = (bf16[16,2048]{1,0:T(8,128)(2,1)S(1)}, bf16[16,2048]{1,0:T(8,128)(2,1)S(1)}, u32[]{:S(2)}, u32[]{:S(2)}) collective-permute-start(bf16[16,2048]{1,0:T(8,128)(2,1)S(1)} %get-tuple-element.42), channel_id=1, source_target_pairs={{0,12},{4,0},{8,4},{12,8},{1,13},{5,1},{9,5},{13,9},{2,14},{6,2},{... | collective-permute-start | bytes 196616 | tf_op jit(solution)/shard_map/ppermute | solution.py:409
  24.5 5.2 %collective-permute-start.4 = (bf16[16,2048]{1,0:T(8,128)(2,1)S(1)}, bf16[16,2048]{1,0:T(8,128)(2,1)S(1)}, u32[]{:S(2)}, u32[]{:S(2)}) collective-permute-start(bf16[16,2048]{1,0:T(8,128)(2,1)S(1)} %get-tuple-element.43), channel_id=1, source_target_pairs={{0,8},{4,12},{8,0},{12,4},{1,9},{5,13},{9,1},{13,5},{2,10},{6,14},... | collective-permute-start | bytes 196616 | tf_op jit(solution)/shard_map/ppermute | solution.py:409
  24.5 6.1 %collective-permute-start.5 = (bf16[16,2048]{1,0:T(8,128)(2,1)S(1)}, bf16[16,2048]{1,0:T(8,128)(2,1)S(1)}, u32[]{:S(2)}, u32[]{:S(2)}) collective-permute-start(bf16[16,2048]{1,0:T(8,128)(2,1)S(1)} %get-tuple-element.44), channel_id=1, source_target_pairs={{0,4},{4,8},{8,12},{12,0},{1,5},{5,9},{9,13},{13,1},{2,6},{6,10},{... | collective-permute-start | bytes 196616 | tf_op jit(solution)/shard_map/ppermute | solution.py:409
  30.8 10.1 %collective-permute-start.8 = (bf16[32,2048]{1,0:T(8,128)(2,1)S(1)}, bf16[32,2048]{1,0:T(8,128)(2,1)S(1)}, u32[]{:S(2)}, u32[]{:S(2)}) collective-permute-start(bf16[32,2048]{1,0:T(8,128)(2,1)S(1)} %convolution_convert_fusion.after_ref.refs_0_), channel_id=1, source_target_pairs={{0,12},{4,0},{8,4},{12,8},{1,13},{5,1},{9,5},{13,9},{2,14},{6,2},{... | collective-permute-start | bytes 393224 | tf_op jit(solution)/shard_map/ppermute | solution.py:409
  31.7 10.1 %collective-permute-start.7 = (bf16[32,2048]{1,0:T(8,128)(2,1)S(1)}, bf16[32,2048]{1,0:T(8,128)(2,1)S(1)}, u32[]{:S(2)}, u32[]{:S(2)}) collective-permute-start(bf16[32,2048]{1,0:T(8,128)(2,1)S(1)} %convolution_convert_fusion.after_ref.refs_0_), channel_id=1, source_target_pairs={{0,8},{4,12},{8,0},{12,4},{1,9},{5,13},{9,1},{13,5},{2,10},{6,14},... | collective-permute-start | bytes 393224 | tf_op jit(solution)/shard_map/ppermute | solution.py:409
  32.0 9.8 %collective-permute-start.6 = (bf16[32,2048]{1,0:T(8,128)(2,1)S(1)}, bf16[32,2048]{1,0:T(8,128)(2,1)S(1)}, u32[]{:S(2)}, u32[]{:S(2)}) collective-permute-start(bf16[32,2048]{1,0:T(8,128)(2,1)S(1)} %convolution_convert_fusion.after_ref.refs_0_), channel_id=1, source_target_pairs={{0,4},{4,8},{8,12},{12,0},{1,5},{5,9},{9,13},{13,1},{2,6},{6,10},{... | collective-permute-start | bytes 393224 | tf_op jit(solution)/shard_map/ppermute | solution.py:409
  43.4 5.3 %collective-permute-start.10 = (bf16[32,1280]{1,0:T(8,128)(2,1)S(1)}, bf16[32,1280]{1,0:T(8,128)(2,1)S(1)}, u32[]{:S(2)}, u32[]{:S(2)}) collective-permute-start(bf16[32,1280]{1,0:T(8,128)(2,1)S(1)} %get-tuple-element.54), channel_id=1, source_target_pairs={{0,2},{1,3},{2,0},{3,1},{4,6},{5,7},{6,4},{7,5},{8,10},{9,11},{10,... | collective-permute-start | bytes 245768 | tf_op jit(solution)/shard_map/ppermute | solution.py:409
  48.9 5.2 %collective-permute-start.23 = (bf16[32,1280]{1,0:T(8,128)(2,1)S(1)}, bf16[32,1280]{1,0:T(8,128)(2,1)S(1)}, u32[]{:S(2)}, u32[]{:S(2)}) collective-permute-start(bf16[32,1280]{1,0:T(8,128)(2,1)S(1)} %add_convert_fusion.8.refs_0_), channel_id=1, source_target_pairs={{0,12},{4,0},{8,4},{12,8},{1,13},{5,1},{9,5},{13,9},{2,14},{6,2},{... | collective-permute-start | bytes 245768 | tf_op jit(solution)/shard_map/ppermute | solution.py:409
  50.1 9.3 %collective-permute-start.19 = (bf16[32,1280]{1,0:T(8,128)(2,1)S(1)}, bf16[32,1280]{1,0:T(8,128)(2,1)S(1)}, u32[]{:S(2)}, u32[]{:S(2)}) collective-permute-start(bf16[32,1280]{1,0:T(8,128)(2,1)S(1)} %add_convert_fusion.8.refs_0_), channel_id=1, source_target_pairs={{0,8},{4,12},{8,0},{12,4},{1,9},{5,13},{9,1},{13,5},{2,10},{6,14},... | collective-permute-start | bytes 245768 | tf_op jit(solution)/shard_map/ppermute | solution.py:409
  50.9 8.5 %collective-permute-start.15 = (bf16[32,1280]{1,0:T(8,128)(2,1)S(1)}, bf16[32,1280]{1,0:T(8,128)(2,1)S(1)}, u32[]{:S(2)}, u32[]{:S(2)}) collective-permute-start(bf16[32,1280]{1,0:T(8,128)(2,1)S(1)} %add_convert_fusion.8.refs_0_), channel_id=1, source_target_pairs={{0,4},{4,8},{8,12},{12,0},{1,5},{5,9},{9,13},{13,1},{2,6},{6,10},{... | collective-permute-start | bytes 245768 | tf_op jit(solution)/shard_map/ppermute | solution.py:409
  52.6 8.3 %collective-permute-start.13 = (bf16[32,1280]{1,0:T(8,128)(2,1)S(1)}, bf16[32,1280]{1,0:T(8,128)(2,1)S(1)}, u32[]{:S(2)}, u32[]{:S(2)}) collective-permute-start(bf16[32,1280]{1,0:T(8,128)(2,1)S(1)} %add_convert_fusion.8.refs_0_), channel_id=1, source_target_pairs={{0,2},{1,3},{2,0},{3,1},{4,6},{5,7},{6,4},{7,5},{8,10},{9,11},{10,... | collective-permute-start | bytes 245768 | tf_op jit(solution)/shard_map/ppermute | solution.py:413
  54.0 7.2 %collective-permute-start.12 = (bf16[32,1280]{1,0:T(8,128)(2,1)S(1)}, bf16[32,1280]{1,0:T(8,128)(2,1)S(1)}, u32[]{:S(2)}, u32[]{:S(2)}) collective-permute-start(bf16[32,1280]{1,0:T(8,128)(2,1)S(1)} %add_convert_fusion.8.refs_0_), channel_id=1, source_target_pairs={{0,1},{1,0},{2,3},{3,2},{4,5},{5,4},{6,7},{7,6},{8,9},{9,8},{10,11... | collective-permute-start | bytes 245768 | tf_op jit(solution)/shard_map/ppermute | solution.py:413
  54.2 7.5 %collective-permute-start.25 = (bf16[32,1280]{1,0:T(8,128)(2,1)S(1)}, bf16[32,1280]{1,0:T(8,128)(2,1)S(1)}, u32[]{:S(2)}, u32[]{:S(2)}) collective-permute-start(bf16[32,1280]{1,0:T(8,128)(2,1)S(1)} %collective-permute-done.23.refs_12_), channel_id=1, source_target_pairs={{0,2},{1,3},{2,0},{3,1},{4,6},{5,7},{6,4},{7,5},{8,10},{9,11},{10,... | collective-permute-start | bytes 245768 | tf_op jit(solution)/shard_map/ppermute | solution.py:413
  59.4 5.1 %collective-permute-start.21 = (bf16[32,1280]{1,0:T(8,128)(2,1)S(1)}, bf16[32,1280]{1,0:T(8,128)(2,1)S(1)}, u32[]{:S(2)}, u32[]{:S(2)}) collective-permute-start(bf16[32,1280]{1,0:T(8,128)(2,1)S(1)} %collective-permute-done.19.refs_8_), channel_id=1, source_target_pairs={{0,2},{1,3},{2,0},{3,1},{4,6},{5,7},{6,4},{7,5},{8,10},{9,11},{10,... | collective-permute-start | bytes 245768 | tf_op jit(solution)/shard_map/ppermute | solution.py:413
  74.5 5.1 %collective-permute-start.28 = (bf16[32,1280]{1,0:T(8,128)(2,1)S(1)}, bf16[32,1280]{1,0:T(8,128)(2,1)S(1)}, u32[]{:S(2)}, u32[]{:S(2)}) collective-permute-start(bf16[32,1280]{1,0:T(8,128)(2,1)S(1)} %add_convert_fusion.7), channel_id=1, source_target_pairs={{0,2},{1,3},{2,0},{3,1},{4,6},{5,7},{6,4},{7,5},{8,10},{9,11},{10,... | collective-permute-start | bytes 245768 | tf_op jit(solution)/shard_map/ppermute | solution.py:413
  76.0 5.5 %collective-permute-start.31 = (bf16[32,1280]{1,0:T(8,128)(2,1)S(1)}, bf16[32,1280]{1,0:T(8,128)(2,1)S(1)}, u32[]{:S(2)}, u32[]{:S(2)}) collective-permute-start(bf16[32,1280]{1,0:T(8,128)(2,1)S(1)} %add_convert_fusion.5), channel_id=1, source_target_pairs={{0,2},{1,3},{2,0},{3,1},{4,6},{5,7},{6,4},{7,5},{8,10},{9,11},{10,... | collective-permute-start | bytes 245768 | tf_op jit(solution)/shard_map/ppermute | solution.py:413
  76.7 6.5 %collective-permute-start.34 = (bf16[32,1280]{1,0:T(8,128)(2,1)S(1)}, bf16[32,1280]{1,0:T(8,128)(2,1)S(1)}, u32[]{:S(2)}, u32[]{:S(2)}) collective-permute-start(bf16[32,1280]{1,0:T(8,128)(2,1)S(1)} %add_convert_fusion.3), channel_id=1, source_target_pairs={{0,2},{1,3},{2,0},{3,1},{4,6},{5,7},{6,4},{7,5},{8,10},{9,11},{10,... | collective-permute-start | bytes 245768 | tf_op jit(solution)/shard_map/ppermute | solution.py:413
  78.2 7.3 %collective-permute-start.37 = (bf16[32,1280]{1,0:T(8,128)(2,1)S(1)}, bf16[32,1280]{1,0:T(8,128)(2,1)S(1)}, u32[]{:S(2)}, u32[]{:S(2)}) collective-permute-start(bf16[32,1280]{1,0:T(8,128)(2,1)S(1)} %add_convert_fusion.1), channel_id=1, source_target_pairs={{0,2},{1,3},{2,0},{3,1},{4,6},{5,7},{6,4},{7,5},{8,10},{9,11},{10,... | collective-permute-start | bytes 245768 | tf_op jit(solution)/shard_map/ppermute | solution.py:413
  79.6 7.1 %collective-permute-start.29 = (bf16[32,1280]{1,0:T(8,128)(2,1)S(1)}, bf16[32,1280]{1,0:T(8,128)(2,1)S(1)}, u32[]{:S(2)}, u32[]{:S(2)}) collective-permute-start(bf16[32,1280]{1,0:T(8,128)(2,1)S(1)} %add_convert_fusion.6), channel_id=1, source_target_pairs={{0,8},{4,12},{8,0},{12,4},{1,9},{5,13},{9,1},{13,5},{2,10},{6,14},... | collective-permute-start | bytes 245768 | tf_op jit(solution)/shard_map/ppermute | solution.py:409
  81.6 6.5 %collective-permute-start.32 = (bf16[32,1280]{1,0:T(8,128)(2,1)S(1)}, bf16[32,1280]{1,0:T(8,128)(2,1)S(1)}, u32[]{:S(2)}, u32[]{:S(2)}) collective-permute-start(bf16[32,1280]{1,0:T(8,128)(2,1)S(1)} %add_convert_fusion.4), channel_id=1, source_target_pairs={{0,4},{4,8},{8,12},{12,0},{1,5},{5,9},{9,13},{13,1},{2,6},{6,10},{... | collective-permute-start | bytes 245768 | tf_op jit(solution)/shard_map/ppermute | solution.py:409
  83.2 5.6 %collective-permute-start.35 = (bf16[32,1280]{1,0:T(8,128)(2,1)S(1)}, bf16[32,1280]{1,0:T(8,128)(2,1)S(1)}, u32[]{:S(2)}, u32[]{:S(2)}) collective-permute-start(bf16[32,1280]{1,0:T(8,128)(2,1)S(1)} %add_convert_fusion.2), channel_id=1, source_target_pairs={{0,12},{4,0},{8,4},{12,8},{1,13},{5,1},{9,5},{13,9},{2,14},{6,2},{... | collective-permute-start | bytes 245768 | tf_op jit(solution)/shard_map/ppermute | solution.py:409
  (17 other events, 110.9 us)
